TPU v7x, 512 devices: a whole 4x4x16 slice. The times are simulated.
512 devices in a mesh: patch: 128 (over x, z, core), chan: 4 (over y).
Axes of the slice: x: 4, y: 4, z: 16, core: 2. Of those that a mesh axis runs over, the one named last changes fastest.
Arguments:
- grid_in: bfloat16 [524288, 227], P(('patch', 'chan')), may hold values from -6 to 6
- mesh_embed: bfloat16 [262144, 512], P(('patch', 'chan')), may hold values from -6 to 6
- w_embed: bfloat16 [227, 512], P(None, 'chan'), may hold values from -0.375 to 0.375
- w_edge: bfloat16 [512, 512], P(None, 'chan'), may hold values from -0.25 to 0.25
- w_proc: bfloat16 [512, 512], P(None, 'chan'), may hold values from -0.25 to 0.25
- w_dec: bfloat16 [512, 512], P(None, 'chan'), may hold values from -0.25 to 0.25
- pack_rows: int32 [128, 4, 7, 384], P('patch', 'chan'), may hold values from 0 to 1023
- recv_node: int32 [128, 4, 7, 384], P('patch', 'chan'), may hold values from 0 to 512, as said below
- far_send: int32 [128, 4, 128, 8], P('patch', 'chan'), may hold values from 0 to 511
- far_recv: int32 [128, 4, 128, 8], P('patch', 'chan'), may hold values from 0 to 512, as said below
- loc_nbr: int32 [262144, 6], P(('patch', 'chan')), may hold values from 0 to 511
- dec_edge: int32 [524288, 3], P(('patch', 'chan')), may hold values from 0 to 3583
Outputs:
- grid_out: bfloat16 [524288, 512], P(('patch', 'chan'))
Inputs may be any that keep to these rules, and one draw needn't show every extreme that they name: `recv_node`: within each [p, c, o] the live entries (under 512) come first and number at most 384; in every draw and for every c some patch p has 384 live entries at every o. `far_recv`: live entries (under 512) stand only where (p - q) or (q - p) modulo 128 is a positive power of two, and come first within each [p, c, q]; each such pair has 1 to 8 live entries, exactly 8 where (p - q) modulo 128 is 1.
All inputs are finite; a program needn't handle non-finite values.
Results may differ from a plain program's by a relative error of at most 0.0075.
Values may be sent and summed in bfloat16 or wider, within the bound.
No kernel may reach another device: no remote copies, remote signals or barrier semaphores. Data moves between devices by JAX's collectives and lax.ppermute only.
A program may use at most 64 MiB of HBM per device.

v0:
```python
import math

import jax
import jax.numpy as jnp
from jax import lax
from jax.sharding import PartitionSpec as P


def from_behind(value, axis, steps):
    count = lax.axis_size(axis)
    pairs = [(source, (source + steps) % count) for source in range(count)]
    return lax.ppermute(value, axis, pairs)


def accumulate(slot_node, values, row_count):
    slots = slot_node.shape[0]
    channels = values.shape[-1]
    block_size = math.gcd(slots, 512)
    blocks = slots // block_size
    node_blocks = slot_node.reshape(blocks, block_size)
    value_blocks = values.reshape(blocks, block_size, channels)
    targets = lax.broadcasted_iota(jnp.int32, (row_count, block_size), 0)

    def add_block(running, pieces):
        node_ids, rows_here = pieces
        one_hot = (targets == node_ids[None, :]).astype(jnp.bfloat16)
        return (running + jnp.dot(one_hot, rows_here, preferred_element_type=jnp.float32), None)

    running, _unused = lax.scan(
        add_block, jnp.zeros((row_count, channels), jnp.float32), (node_blocks, value_blocks)
    )
    return running


def shards(
    grid_in,
    mesh_embed,
    w_embed,
    w_edge,
    w_proc,
    w_dec,
    pack_rows,
    recv_node,
    far_send,
    far_recv,
    loc_nbr,
    dec_edge,
):
    full_embed, full_edge, full_proc, full_dec = (
        lax.all_gather(w_embed, "chan", axis=1, tiled=True),
        lax.all_gather(w_edge, "chan", axis=1, tiled=True),
        lax.all_gather(w_proc, "chan", axis=1, tiled=True),
        lax.all_gather(w_dec, "chan", axis=1, tiled=True),
    )
    patches = lax.axis_size("patch")
    mesh_count = mesh_embed.shape[0]
    channels = full_edge.shape[1]
    offsets = pack_rows.shape[2]
    reach = (offsets - 1) // 2
    slot_count = pack_rows.shape[-1]
    far_count = far_send.shape[-1]
    pack = pack_rows.reshape(offsets, slot_count)
    receive = recv_node.reshape(offsets, slot_count)
    far_out = far_send.reshape(patches, far_count)
    far_in = far_recv.reshape(patches, far_count)
    grid_latent = jax.nn.silu(
        jnp.dot(grid_in, full_embed, preferred_element_type=jnp.float32)
    ).astype(jnp.bfloat16)
    arrived_list = []
    for offset in range(offsets):
        outgoing = jnp.take(grid_latent, pack[offset], axis=0)
        if offset == reach:
            arrived_list.append(outgoing)
        else:
            arrived_list.append(from_behind(outgoing, "patch", offset - reach))
    arrived = jnp.stack(arrived_list)
    edge_msg = jax.nn.silu(
        jnp.einsum("okd,de->oke", arrived, full_edge, preferred_element_type=jnp.float32)
    ).astype(jnp.bfloat16)
    summed = accumulate(receive.reshape(-1), edge_msg.reshape(-1, channels), mesh_count)
    mesh_latent = (mesh_embed.astype(jnp.float32) + summed).astype(jnp.bfloat16)
    node_msg = jax.nn.silu(
        jnp.dot(mesh_latent, full_proc, preferred_element_type=jnp.float32)
    ).astype(jnp.bfloat16)
    local_sum = (
        jnp.take(node_msg, loc_nbr.reshape(-1), axis=0)
        .astype(jnp.float32)
        .reshape(mesh_count, -1, channels)
        .sum(1)
    )
    far_outgoing = jnp.take(node_msg, far_out.reshape(-1), axis=0).reshape(
        patches, far_count, channels
    )
    far_arrived = lax.all_to_all(far_outgoing, "patch", split_axis=0, concat_axis=0, tiled=True)
    far_sum = accumulate(far_in.reshape(-1), far_arrived.reshape(-1, channels), mesh_count)
    mesh_next = (mesh_latent.astype(jnp.float32) + local_sum + far_sum).astype(jnp.bfloat16)
    decoded = jax.nn.silu(jnp.dot(mesh_next, full_dec, preferred_element_type=jnp.float32)).astype(
        jnp.bfloat16
    )
    window_list = []
    for offset in range(offsets):
        if offset == reach:
            window_list.append(decoded)
        else:
            window_list.append(from_behind(decoded, "patch", reach - offset))
    window = jnp.concatenate(window_list, axis=0)
    edges_per_row = dec_edge.shape[1]
    grid_sum = (
        jnp.take(window, dec_edge.reshape(-1), axis=0)
        .astype(jnp.float32)
        .reshape(-1, edges_per_row, channels)
        .sum(1)
    )
    return (grid_latent.astype(jnp.float32) + grid_sum).astype(jnp.bfloat16)


def solution(mesh):
    in_specs = (
        P(("patch", "chan"), None),
        P(("patch", "chan"), None),
        P(None, "chan"),
        P(None, "chan"),
        P(None, "chan"),
        P(None, "chan"),
        P("patch", "chan", None, None),
        P("patch", "chan", None, None),
        P("patch", "chan", None, None),
        P("patch", "chan", None, None),
        P(("patch", "chan"), None),
        P(("patch", "chan"), None),
    )
    out_specs = P(("patch", "chan"), None)
    return jax.shard_map(shards, mesh=mesh, in_specs=in_specs, out_specs=out_specs, check_vma=False)
```

profile of v0, /device:TPU:8, one launch (start us, length us, event | category | flops | bytes accessed | tf_op | source)
XLA Modules:
  0.0 322.2 jit_solution(6928698933918578960)
XLA Ops:
  0.9 15.2 %all_gather.12 = bf16[227,512]{1,0:T(8,128)(2,1)S(1)} all-gather(bf16[227,128]{1,0:T(8,128)(2,1)} %param.20), channel_id=1, replica_groups=mesh['patch'=128,'chan'=4] {'chan'}, dimensions={1}, use_global_device_ids=true | all-gather | bytes 290560 | tf_op jit(solution)/shard_map/all_gather | solution.py:50
  16.9 2.1 gather_fusion.3
  19.9 8.0 %collective-permute-start = (bf16[384,512]{1,0:T(8,128)(2,1)}, bf16[384,512]{1,0:T(8,128)(2,1)}, u32[]{:S(2)}, u32[]{:S(2)}) collective-permute-start(bf16[384,512]{1,0:T(8,128)(2,1)} %broadcast_select_fusion.5), channel_id=1, source_target_pairs={{0,500},{4,504},{8,508},{12,0},{16,4},{20,8},{24,12},{28,16},{32,2... | collective-permute-start | bytes 1179656 | tf_op jit(solution)/shard_map/ppermute | solution.py:12
  27.9 2.1 gather_fusion.4
  30.8 4.8 %collective-permute-start.1 = (bf16[384,512]{1,0:T(8,128)(2,1)}, bf16[384,512]{1,0:T(8,128)(2,1)}, u32[]{:S(2)}, u32[]{:S(2)}) collective-permute-start(bf16[384,512]{1,0:T(8,128)(2,1)} %broadcast_select_fusion.4), channel_id=1, source_target_pairs={{0,504},{4,508},{8,0},{12,4},{16,8},{20,12},{24,16},{28,20},{32,24... | collective-permute-start | bytes 1179656 | tf_op jit(solution)/shard_map/ppermute | solution.py:12
  35.7 2.1 gather_fusion.5
  38.7 3.3 %collective-permute-start.2 = (bf16[384,512]{1,0:T(8,128)(2,1)}, bf16[384,512]{1,0:T(8,128)(2,1)}, u32[]{:S(2)}, u32[]{:S(2)}) collective-permute-start(bf16[384,512]{1,0:T(8,128)(2,1)} %broadcast_select_fusion.3), channel_id=1, source_target_pairs={{0,508},{4,0},{8,4},{12,8},{16,12},{20,16},{24,20},{28,24},{32,28}... | collective-permute-start | bytes 1179656 | tf_op jit(solution)/shard_map/ppermute | solution.py:12
  42.1 2.1 gather_fusion.7
  45.0 1.9 collective-permute-start.3
  47.6 2.1 gather_fusion.8
  50.5 2.9 collective-permute-start.4
  55.2 2.1 gather_fusion.6
  57.3 2.2 gather_fusion.9
  59.5 1.3 reduce
  60.9 1.3 reshape_reshape_reshape.6
  63.5 1.4 copy.21
  65.7 13.7 %all_gather.13 = bf16[512,512]{1,0:T(8,128)(2,1)S(1)} all-gather(bf16[512,128]{1,0:T(8,128)(2,1)S(1)} %copy-done.2), channel_id=1, replica_groups=mesh['patch'=128,'chan'=4] {'chan'}, dimensions={1}, use_global_device_ids=true | all-gather | bytes 655360 | tf_op jit(solution)/shard_map/all_gather | solution.py:51
  79.4 14.3 %all_gather.14 = bf16[512,512]{1,0:T(8,128)(2,1)} all-gather(bf16[512,128]{1,0:T(8,128)(2,1)} %param.22), channel_id=1, replica_groups=mesh['patch'=128,'chan'=4] {'chan'}, dimensions={1}, use_global_device_ids=true | all-gather | bytes 655360 | tf_op jit(solution)/shard_map/all_gather | solution.py:52
  93.7 2.1 collective-permute-start.5
  101.1 11.5 %collective-permute-done.5 = bf16[384,512]{1,0:T(8,128)(2,1)S(1)} collective-permute-done((bf16[384,512]{1,0:T(8,128)(2,1)S(1)}, bf16[384,512]{1,0:T(8,128)(2,1)S(1)}, u32[]{:S(2)}, u32[]{:S(2)}) %collective-permute-start.5) | collective-permute-done | bytes 393248 | tf_op jit(solution)/shard_map/ppermute | solution.py:12
  112.6 3.9 %multiply_convert_fusion = bf16[7,384,512]{2,1,0:T(8,128)(2,1)} fusion(bf16[7,384,512]{2,1,0:T(8,128)(2,1)S(1)} %bitcast_dynamic-update-slice_fusion, bf16[512,512]{1,0:T(8,128)(2,1)S(1)} %all_gather.13), kind=kOutput, calls=%fused_computation.28 | convolution fusion | flops 1416167424 | bytes 6029312 | tf_op jit(solution)/shard_map/okd,de->oke/dot_general | solution.py:78
  116.6 41.7 %while.22 = (s32[]{:T(128)}, f32[512,512]{1,0:T(8,128)S(1)}, s32[21,128]{1,0:T(8,128)}, bf16[21,128,512]{2,1,0:T(8,128)(2,1)}, s32[]{:T(128)}, /*index=5*/s32[]{:T(128)}) while((s32[]{:T(128)}, f32[512,512]{1,0:T(8,128)S(1)}, s32[21,128]{1,0:T(8,128)}, bf16[21,128,512]{2,1,0:T(8,128)(2,1)}, s32[]{:T(128)}, ...), condition=%wide.region_1.3_spmd.clone, body=%wide.region_0.2_spmd.clone.sunk | while | flops 67698688 | bytes 2230355 | solution.py:29
  121.2 1.3 convolution_add_fusion.4
  123.2 1.3 convolution_add_fusion.4
  125.2 1.3 convolution_add_fusion.4
  127.2 1.3 convolution_add_fusion.4
  129.2 1.3 convolution_add_fusion.4
  131.2 1.3 convolution_add_fusion.4
  133.1 1.3 convolution_add_fusion.4
  139.1 1.3 convolution_add_fusion.4
  145.1 1.3 convolution_add_fusion.4
  147.1 1.3 convolution_add_fusion.4
  149.0 1.3 convolution_add_fusion.4
  151.0 1.3 convolution_add_fusion.4
  158.3 1.8 multiply_convert_fusion.3
  160.1 5.1 %gather_fusion.1 = bf16[1024,512]{1,0:T(8,128)(2,1)} fusion(bf16[512,512]{1,0:T(8,128)(2,1)S(1)} %multiply_convert_fusion.3, s32[1024]{0:T(1024)S(1)} %broadcast_clamp_fusion.2), kind=kCustom, calls=%fused_computation.8 | custom fusion | bytes 2101248 | tf_op jit(solution)/shard_map/jit(_take)/gather | solution.py:91
  165.2 2.5 bitcast_select_fusion
  167.8 7.3 %all-to-all-start = ((bf16[128,8,512]{2,1,0:T(8,128)(2,1)}), bf16[128,8,512]{2,1,0:T(8,128)(2,1)}, u32[]{:S(2)}, u32[]{:S(2)}) async-start(bf16[128,8,512]{2,1,0:T(8,128)(2,1)} %bitcast_select_fusion), calls=%async_computation | async-start | bytes 2097152 | tf_op jit(solution)/shard_map/all_to_all | solution.py:94
  176.9 1.4 reshape.148
  178.3 14.4 %all_gather.15 = bf16[512,512]{1,0:T(8,128)(2,1)} all-gather(bf16[512,128]{1,0:T(8,128)(2,1)S(1)} %copy-done.3), channel_id=1, replica_groups=mesh['patch'=128,'chan'=4] {'chan'}, dimensions={1}, use_global_device_ids=true | all-gather | bytes 655360 | tf_op jit(solution)/shard_map/all_gather | solution.py:53
  192.7 13.3 %gather_fusion = bf16[3072,512]{1,0:T(8,128)(2,1)} fusion(bf16[512,512]{1,0:T(8,128)(2,1)S(1)} %multiply_convert_fusion.3, s32[3072]{0:T(1024)S(1)} %broadcast_clamp_fusion.1), kind=kCustom, calls=%fused_computation.7 | custom fusion | bytes 6303744 | tf_op jit(solution)/shard_map/jit(_take)/gather | solution.py:86
  206.0 6.3 %gather.22 = bf16[512,6,512]{2,1,0:T(8,128)(2,1)} reshape(bf16[3072,512]{1,0:T(8,128)(2,1)} %gather_fusion) | data formatting | bytes 6291456 | tf_op jit(solution)/shard_map/jit(_take)/gather | solution.py:86
  212.3 5.7 %convert_reduce_fusion.1 = f32[512,512]{1,0:T(8,128)} fusion(bf16[512,6,512]{2,1,0:T(8,128)(2,1)} %gather.22, pred[512,6]{1,0:T(8,128)(4,1)S(1)} %copy.18), kind=kLoop, calls=%fused_computation.27 | loop fusion | flops 4456448 | bytes 4197376 | tf_op jit(solution)/shard_map/reduce_sum | solution.py:89
  218.1 12.2 %all-to-all-done = bf16[128,8,512]{2,1,0:T(8,128)(2,1)} async-done(((bf16[128,8,512]{2,1,0:T(8,128)(2,1)}), bf16[128,8,512]{2,1,0:T(8,128)(2,1)}, u32[]{:S(2)}, u32[]{:S(2)}) %all-to-all-start) | async-done | bytes 1048608 | tf_op jit(solution)/shard_map/all_to_all | solution.py:94
  230.3 5.4 %while.23 = (s32[]{:T(128)}, f32[512,512]{1,0:T(8,128)}, s32[2,512]{1,0:T(2,128)S(1)}, bf16[2,512,512]{2,1,0:T(8,128)(2,1)}, s32[]{:T(128)}, /*index=5*/s32[]{:T(128)}) while((s32[]{:T(128)}, f32[512,512]{1,0:T(8,128)}, s32[2,512]{1,0:T(2,128)S(1)}, bf16[2,512,512]{2,1,0:T(8,128)(2,1)}, s32[]{:T(128)}, /*index=5*/s32[]{:T(128)}) %tuple.52), condition=%wide.region_4.6_spmd.clone, body=%wide.region_3.5_spmd.clone.sunk | while | flops 269221888 | bytes 2628179 | solution.py:29
  230.3 2.5 convolution_add_fusion.5
  232.9 2.8 convolution_add_fusion.5
  235.7 3.1 multiply_convert_fusion.2
  238.8 1.9 collective-permute-start.6
  240.7 2.7 collective-permute-start.7
  243.4 3.4 %collective-permute-start.8 = (bf16[512,512]{1,0:T(8,128)(2,1)}, bf16[512,512]{1,0:T(8,128)(2,1)S(1)}, u32[]{:S(2)}, u32[]{:S(2)}) collective-permute-start(bf16[512,512]{1,0:T(8,128)(2,1)} %multiply_convert_fusion.2), channel_id=1, source_target_pairs={{0,4},{4,8},{8,12},{12,16},{16,20},{20,24},{24,28},{28,32},{32,36}... | collective-permute-start | bytes 1572872 | tf_op jit(solution)/shard_map/ppermute | solution.py:12
  246.8 5.5 %collective-permute-start.9 = (bf16[512,512]{1,0:T(8,128)(2,1)}, bf16[512,512]{1,0:T(8,128)(2,1)S(1)}, u32[]{:S(2)}, u32[]{:S(2)}) collective-permute-start(bf16[512,512]{1,0:T(8,128)(2,1)} %multiply_convert_fusion.2), channel_id=1, source_target_pairs={{0,508},{4,0},{8,4},{12,8},{16,12},{20,16},{24,20},{28,24},{32,28}... | collective-permute-start | bytes 1572872 | tf_op jit(solution)/shard_map/ppermute | solution.py:12
  252.6 3.1 collective-permute-start.10
  255.8 6.1 %collective-permute-done.6 = bf16[512,512]{1,0:T(8,128)(2,1)S(1)} collective-permute-done((bf16[512,512]{1,0:T(8,128)(2,1)}, bf16[512,512]{1,0:T(8,128)(2,1)S(1)}, u32[]{:S(2)}, u32[]{:S(2)}) %collective-permute-start.6) | collective-permute-done | bytes 524320 | tf_op jit(solution)/shard_map/ppermute | solution.py:12
  261.8 2.1 collective-permute-start.11
  264.8 7.2 %collective-permute-done.7 = bf16[512,512]{1,0:T(8,128)(2,1)} collective-permute-done((bf16[512,512]{1,0:T(8,128)(2,1)}, bf16[512,512]{1,0:T(8,128)(2,1)}, u32[]{:S(2)}, u32[]{:S(2)}) %collective-permute-start.7) | collective-permute-done | bytes 524320 | tf_op jit(solution)/shard_map/ppermute | solution.py:12
  272.0 1.9 constant_dynamic-update-slice_fusion.5
  273.9 5.4 %collective-permute-done.8 = bf16[512,512]{1,0:T(8,128)(2,1)S(1)} collective-permute-done((bf16[512,512]{1,0:T(8,128)(2,1)}, bf16[512,512]{1,0:T(8,128)(2,1)S(1)}, u32[]{:S(2)}, u32[]{:S(2)}) %collective-permute-start.8) | collective-permute-done | bytes 524320 | tf_op jit(solution)/shard_map/ppermute | solution.py:12
  280.2 1.9 constant_dynamic-update-slice_fusion.3
  283.8 3.6 %collective-permute-done.11 = bf16[512,512]{1,0:T(8,128)(2,1)S(1)} collective-permute-done((bf16[512,512]{1,0:T(8,128)(2,1)}, bf16[512,512]{1,0:T(8,128)(2,1)S(1)}, u32[]{:S(2)}, u32[]{:S(2)}) %collective-permute-start.11) | collective-permute-done | bytes 524320 | tf_op jit(solution)/shard_map/ppermute | solution.py:12
  288.2 15.9 %gather_fusion.2 = bf16[3072,512]{1,0:T(8,128)(2,1)} fusion(bf16[3584,512]{1,0:T(8,128)(2,1)} %constant_dynamic-update-slice_fusion, s32[3072]{0:T(1024)S(1)} %broadcast_clamp_fusion), kind=kCustom, calls=%fused_computation.9 | custom fusion | bytes 6303744 | tf_op jit(solution)/shard_map/jit(_take)/gather | solution.py:109
  304.1 9.1 %gather.26 = bf16[1024,3,512]{2,1,0:T(4,128)(2,1)} reshape(bf16[3072,512]{1,0:T(8,128)(2,1)} %gather_fusion.2) | data formatting | bytes 6291456 | tf_op jit(solution)/shard_map/jit(_take)/gather | solution.py:109
  313.2 7.6 %convert_reduce_fusion = f32[1024,512]{1,0:T(8,128)S(1)} fusion(bf16[1024,3,512]{2,1,0:T(4,128)(2,1)} %gather.26, pred[1024,3]{1,0:T(8,128)(4,1)S(1)} %copy.17), kind=kLoop, calls=%fused_computation.26 | loop fusion | flops 4194304 | bytes 5245952 | tf_op jit(solution)/shard_map/reduce_sum | solution.py:112
  320.8 1.4 add_convert_fusion
  (117 shorter events, 48.2 us)
Async XLA Ops:
  0.0 16.1 %copy-start = (bf16[1024,227]{0,1:T(8,128)(2,1)S(1)}, bf16[1024,227]{0,1:T(8,128)(2,1)}, u32[]{:S(2)}) copy-start(bf16[1024,227]{0,1:T(8,128)(2,1)} %param.18) | copy-start | bytes 1394692
  19.9 73.8 %collective-permute-start = (bf16[384,512]{1,0:T(8,128)(2,1)}, bf16[384,512]{1,0:T(8,128)(2,1)}, u32[]{:S(2)}, u32[]{:S(2)}) collective-permute-start(bf16[384,512]{1,0:T(8,128)(2,1)} %broadcast_select_fusion.5), channel_id=1, source_target_pairs={{0,500},{4,504},{8,508},{12,0},{16,4},{20,8},{24,12},{28,16},{32,2... | collective-permute-start | bytes 1179656 | tf_op jit(solution)/shard_map/ppermute | solution.py:12
  30.8 66.0 %collective-permute-start.1 = (bf16[384,512]{1,0:T(8,128)(2,1)}, bf16[384,512]{1,0:T(8,128)(2,1)}, u32[]{:S(2)}, u32[]{:S(2)}) collective-permute-start(bf16[384,512]{1,0:T(8,128)(2,1)} %broadcast_select_fusion.4), channel_id=1, source_target_pairs={{0,504},{4,508},{8,0},{12,4},{16,8},{20,12},{24,16},{28,20},{32,24... | collective-permute-start | bytes 1179656 | tf_op jit(solution)/shard_map/ppermute | solution.py:12
  38.7 59.1 %collective-permute-start.2 = (bf16[384,512]{1,0:T(8,128)(2,1)}, bf16[384,512]{1,0:T(8,128)(2,1)}, u32[]{:S(2)}, u32[]{:S(2)}) collective-permute-start(bf16[384,512]{1,0:T(8,128)(2,1)} %broadcast_select_fusion.3), channel_id=1, source_target_pairs={{0,508},{4,0},{8,4},{12,8},{16,12},{20,16},{24,20},{28,24},{32,28}... | collective-permute-start | bytes 1179656 | tf_op jit(solution)/shard_map/ppermute | solution.py:12
  44.1 10.4 %copy-start.7 = (s32[1,1,128,8]{2,3,1,0:T(8,128)S(1)}, s32[1,1,128,8]{2,3,1,0:T(8,128)}, u32[]{:S(2)}) copy-start(s32[1,1,128,8]{2,3,1,0:T(8,128)} %param.26) | copy-start | bytes 12292
  45.0 54.0 %collective-permute-start.3 = (bf16[384,512]{1,0:T(8,128)(2,1)}, bf16[384,512]{1,0:T(8,128)(2,1)}, u32[]{:S(2)}, u32[]{:S(2)}) collective-permute-start(bf16[384,512]{1,0:T(8,128)(2,1)} %broadcast_select_fusion.2), channel_id=1, source_target_pairs={{0,4},{4,8},{8,12},{12,16},{16,20},{20,24},{24,28},{28,32},{32,36}... | collective-permute-start | bytes 1179656 | tf_op jit(solution)/shard_map/ppermute | solution.py:12
  50.5 49.6 %collective-permute-start.4 = (bf16[384,512]{1,0:T(8,128)(2,1)}, bf16[384,512]{1,0:T(8,128)(2,1)}, u32[]{:S(2)}, u32[]{:S(2)}) collective-permute-start(bf16[384,512]{1,0:T(8,128)(2,1)} %broadcast_select_fusion.1), channel_id=1, source_target_pairs={{0,8},{4,12},{8,16},{12,20},{16,24},{20,28},{24,32},{28,36},{32,40... | collective-permute-start | bytes 1179656 | tf_op jit(solution)/shard_map/ppermute | solution.py:12
  55.2 10.4 %copy-start.2 = (bf16[512,128]{1,0:T(8,128)(2,1)S(1)}, bf16[512,128]{1,0:T(8,128)(2,1)}, u32[]{:S(2)}) copy-start(bf16[512,128]{1,0:T(8,128)(2,1)} %param.21) | copy-start | bytes 393220
  62.8 36.1 %copy-start.9 = (pred[384]{0:T(512)(128)(4,1)S(1)}, pred[384]{0:T(512)(128)(4,1)}, u32[]{:S(2)}) copy-start(pred[384]{0:T(512)(128)(4,1)} %compare_and_fusion.6) | copy-start | bytes 1156
  93.7 18.9 %collective-permute-start.5 = (bf16[384,512]{1,0:T(8,128)(2,1)S(1)}, bf16[384,512]{1,0:T(8,128)(2,1)S(1)}, u32[]{:S(2)}, u32[]{:S(2)}) collective-permute-start(bf16[384,512]{1,0:T(8,128)(2,1)S(1)} %broadcast_select_fusion), channel_id=1, source_target_pairs={{0,12},{4,16},{8,20},{12,24},{16,28},{20,32},{24,36},{28,40},{32,4... | collective-permute-start | bytes 1179656 | tf_op jit(solution)/shard_map/ppermute | solution.py:12
  160.1 5.1 %copy-start.4 = (pred[128,8]{1,0:T(8,128)(4,1)S(1)}, pred[128,8]{1,0:T(8,128)(4,1)}, u32[]{:S(2)}) copy-start(pred[128,8]{1,0:T(8,128)(4,1)} %copy.21) | copy-start | bytes 3076
  165.2 9.9 %copy-start.5 = (s32[512,6]{0,1:T(8,128)S(1)}, s32[512,6]{0,1:T(8,128)}, u32[]{:S(2)}) copy-start(s32[512,6]{0,1:T(8,128)} %param.28) | copy-start | bytes 36868
  165.2 10.5 %copy-start.8 = (s32[1,1,128,8]{2,3,1,0:T(8,128)S(1)}, s32[1,1,128,8]{2,3,1,0:T(8,128)}, u32[]{:S(2)}) copy-start(s32[1,1,128,8]{2,3,1,0:T(8,128)} %param.27) | copy-start | bytes 12292
  165.2 10.7 %copy-start.6 = (s32[1024,3]{0,1:T(4,128)S(1)}, s32[1024,3]{0,1:T(4,128)}, u32[]{:S(2)}) copy-start(s32[1024,3]{0,1:T(4,128)} %param.29) | copy-start | bytes 36868
  165.2 13.1 %copy-start.3 = (bf16[512,128]{1,0:T(8,128)(2,1)S(1)}, bf16[512,128]{1,0:T(8,128)(2,1)}, u32[]{:S(2)}) copy-start(bf16[512,128]{1,0:T(8,128)(2,1)} %param.23) | copy-start | bytes 393220
  167.8 62.5 %all-to-all-start = ((bf16[128,8,512]{2,1,0:T(8,128)(2,1)}), bf16[128,8,512]{2,1,0:T(8,128)(2,1)}, u32[]{:S(2)}, u32[]{:S(2)}) async-start(bf16[128,8,512]{2,1,0:T(8,128)(2,1)} %bitcast_select_fusion), calls=%async_computation | async-start | bytes 2097152 | tf_op jit(solution)/shard_map/all_to_all | solution.py:94
  230.3 5.4 %copy-start.1 = (bf16[512,512]{1,0:T(8,128)(2,1)S(1)}, bf16[512,512]{1,0:T(8,128)(2,1)}, u32[]{:S(2)}) copy-start(bf16[512,512]{1,0:T(8,128)(2,1)} %all_gather.15) | copy-start | bytes 1572868
  238.8 23.1 %collective-permute-start.6 = (bf16[512,512]{1,0:T(8,128)(2,1)}, bf16[512,512]{1,0:T(8,128)(2,1)S(1)}, u32[]{:S(2)}, u32[]{:S(2)}) collective-permute-start(bf16[512,512]{1,0:T(8,128)(2,1)} %multiply_convert_fusion.2), channel_id=1, source_target_pairs={{0,12},{4,16},{8,20},{12,24},{16,28},{20,32},{24,36},{28,40},{32,4... | collective-permute-start | bytes 1572872 | tf_op jit(solution)/shard_map/ppermute | solution.py:12
  240.7 31.3 %collective-permute-start.7 = (bf16[512,512]{1,0:T(8,128)(2,1)}, bf16[512,512]{1,0:T(8,128)(2,1)}, u32[]{:S(2)}, u32[]{:S(2)}) collective-permute-start(bf16[512,512]{1,0:T(8,128)(2,1)} %multiply_convert_fusion.2), channel_id=1, source_target_pairs={{0,8},{4,12},{8,16},{12,20},{16,24},{20,28},{24,32},{28,36},{32,40... | collective-permute-start | bytes 1572872 | tf_op jit(solution)/shard_map/ppermute | solution.py:12
  243.4 35.9 %collective-permute-start.8 = (bf16[512,512]{1,0:T(8,128)(2,1)}, bf16[512,512]{1,0:T(8,128)(2,1)S(1)}, u32[]{:S(2)}, u32[]{:S(2)}) collective-permute-start(bf16[512,512]{1,0:T(8,128)(2,1)} %multiply_convert_fusion.2), channel_id=1, source_target_pairs={{0,4},{4,8},{8,12},{12,16},{16,20},{20,24},{24,28},{28,32},{32,36}... | collective-permute-start | bytes 1572872 | tf_op jit(solution)/shard_map/ppermute | solution.py:12
  246.8 35.3 %collective-permute-start.9 = (bf16[512,512]{1,0:T(8,128)(2,1)}, bf16[512,512]{1,0:T(8,128)(2,1)S(1)}, u32[]{:S(2)}, u32[]{:S(2)}) collective-permute-start(bf16[512,512]{1,0:T(8,128)(2,1)} %multiply_convert_fusion.2), channel_id=1, source_target_pairs={{0,508},{4,0},{8,4},{12,8},{16,12},{20,16},{24,20},{28,24},{32,28}... | collective-permute-start | bytes 1572872 | tf_op jit(solution)/shard_map/ppermute | solution.py:12
  252.6 30.3 %collective-permute-start.10 = (bf16[512,512]{1,0:T(8,128)(2,1)}, bf16[512,512]{1,0:T(8,128)(2,1)S(1)}, u32[]{:S(2)}, u32[]{:S(2)}) collective-permute-start(bf16[512,512]{1,0:T(8,128)(2,1)} %multiply_convert_fusion.2), channel_id=1, source_target_pairs={{0,504},{4,508},{8,0},{12,4},{16,8},{20,12},{24,16},{28,20},{32,24... | collective-permute-start | bytes 1572872 | tf_op jit(solution)/shard_map/ppermute | solution.py:12
  261.8 25.6 %collective-permute-start.11 = (bf16[512,512]{1,0:T(8,128)(2,1)}, bf16[512,512]{1,0:T(8,128)(2,1)S(1)}, u32[]{:S(2)}, u32[]{:S(2)}) collective-permute-start(bf16[512,512]{1,0:T(8,128)(2,1)} %multiply_convert_fusion.2), channel_id=1, source_target_pairs={{0,500},{4,504},{8,508},{12,0},{16,4},{20,8},{24,12},{28,16},{32,2... | collective-permute-start | bytes 1572872 | tf_op jit(solution)/shard_map/ppermute | solution.py:12
where the time goes:
time: 325 us; the launch traced here: 322 us
  local copies, waits for them, and re-layouts  99.6 us (31%)
  blocking collectives  57.6 us (18%)
  starting transfers between devices  49.2 us (15%)
  waiting for transfers between devices  46.1 us (14%)
  matrix products  41.7 us (13%)
  other arithmetic  27 us (8%)
    ppermute x12, starting transfers between devices, from_behind(): return lax.ppermute(value, axis, pairs)  41.9 us
    ppermute x12, waiting for transfers between devices, from_behind(): return lax.ppermute(value, axis, pairs)  33.9 us
    dot_general x23, matrix products, add_block(): jnp.dot(one_hot, rows_here, preferred_element_type=jnp.float32)  32.1 us
    gather x2, local copies, waits for them, and re-layouts, shards(): jnp.take(window, dec_edge.reshape(-1), axis=0).astype(jnp.float32)  25 us
    gather x2, local copies, waits for them, and re-layouts, shards(): jnp.take(node_msg, loc_nbr.reshape(-1), axis=0).astype(jnp.float32)  19.6 us
    all_gather x1, blocking collectives, shards(): lax.all_gather(w_embed, 'chan', axis=1, tiled=True)  15.2 us
    gather x7, local copies, waits for them, and re-layouts, shards(): outgoing = jnp.take(grid_latent, pack[offset], axis=0)  14.6 us
    eq x21, local copies, waits for them, and re-layouts, add_block(): one_hot = (targets == node_ids[None, :]).astype(jnp.bfloat16)  14.5 us
  transfers between devices with their start and end apart: 13, of which 6 were waited for; matrix products, arithmetic and copies ran while one was open for 20% of the time, Pallas kernels for 0%

commit v1 on v0

v1 whole, which is shorter than its diff:
```python
import functools

import jax
import jax.numpy as jnp
from jax import lax
from jax.experimental import pallas as pl
from jax.experimental.pallas import tpu as pltpu
from jax.sharding import PartitionSpec as P

BF16 = jnp.bfloat16
F32 = jnp.float32
SENT = 240
WIDE = 256
FAR = (64, 32, -32, 16, -16, 8, -8, 4, -4, 2, -2, 1, -1)
VMEM = pltpu.CompilerParams(vmem_limit_bytes=56 * 1024 * 1024)


def silu(v):
    h = 0.5 * v
    return h + h * jnp.tanh(h)


def mul(a, b):
    return jnp.dot(a, b, preferred_element_type=F32)


def mul_nt(a, b):
    return lax.dot_general(a, b, (((1,), (1,)), ((), ())), preferred_element_type=F32)


def mul_tn(a, b):
    return lax.dot_general(a, b, (((0,), (0,)), ((), ())), preferred_element_type=F32)


def shifted(value, steps):
    count = lax.axis_size("patch")
    return lax.ppermute(value, "patch", [(i, (i + steps) % count) for i in range(count)])


def by_core(value, even_steps, odd_steps):
    count = lax.axis_size("patch")
    pairs = [(i, (i + (even_steps if i % 2 == 0 else odd_steps)) % count) for i in range(count)]
    return lax.ppermute(value, "patch", pairs)


def pack_body(core, x, pack, up, down, three, own, local, padded):
    here = core[0]
    channels, rows = x.shape
    slots = pack.shape[-1]
    padded[...] = jnp.zeros_like(padded)
    padded[0:channels, :] = x[...]
    row_of = lax.broadcasted_iota(jnp.int32, (rows, slots), 0)

    def chosen(offset):
        hot = jnp.where(row_of == pack[offset], 1.0, 0.0).astype(BF16)
        return mul(padded[...], hot).astype(BF16)

    up[0] = chosen(5)
    up[1] = chosen(jnp.where(here == 0, 6, 4))
    down[0] = chosen(1)
    down[1] = chosen(jnp.where(here == 0, 2, 0))
    three[...] = chosen(jnp.where(here == 0, 0, 6))
    own[...] = chosen(jnp.where(here == 0, 4, 2))
    local[...] = chosen(3)


def weights_body(embed, edge, proc, dec, out, padded):
    rows = embed.shape[0]
    padded[...] = jnp.zeros_like(padded)
    padded[0:rows, :] = embed[...]
    width = out.shape[0]
    eye = (
        lax.broadcasted_iota(jnp.int32, (width, width), 0)
        == lax.broadcasted_iota(jnp.int32, (width, width), 1)
    ).astype(F32).astype(BF16)
    at = 0
    for piece in (padded, edge, proc, dec):
        k = piece.shape[0]
        out[:, at : at + k] = mul_nt(eye, piece[...]).astype(BF16)
        at += k


def prepare_body(x, weights, edges, latent, table, padded):
    channels, rows = x.shape
    padded[...] = jnp.zeros_like(padded)
    padded[0:channels, :] = x[...]
    latent[...] = silu(
        lax.dot_general(
            padded[...], weights[:, 0:WIDE], (((0,), (1,)), ((), ())), preferred_element_type=F32
        )
    ).astype(BF16)
    count = edges.shape[0]
    columns = table.shape[1]
    spare = jnp.zeros((8 - count, rows), jnp.int32)
    ids = jnp.concatenate([edges[...], spare], axis=0).T
    step = 128
    for first in range(0, rows, step):
        for block in range(0, columns, 512):
            where = lax.broadcasted_iota(jnp.int32, (step, 512), 1) + block
            total = jnp.zeros((step, 512), F32)
            for k in range(count):
                total += jnp.where(where == ids[first : first + step, k : k + 1], 1.0, 0.0)
            table[first : first + step, block : block + 512] = total.astype(BF16)


def encode_body(
    core, here, local, up, down, three, sib, weights, recv, embed, far_ids, latent, message, far
):
    is_even = core[0] == 0
    nodes = embed.shape[0]
    slots = recv.shape[-1]
    w_embed = weights[:, 0:SENT]
    channels = weights.shape[0]
    w_edge = weights[:, WIDE : WIDE + channels]
    w_proc = weights[:, WIDE + channels : WIDE + 2 * channels]
    node_of = lax.broadcasted_iota(jnp.int32, (nodes, slots), 0)

    def summed(block, offset):
        rows = silu(mul(w_embed, block)).astype(BF16)
        sent = silu(mul(w_edge, rows)).astype(BF16)
        hot = jnp.where(node_of == recv[offset], 1.0, 0.0).astype(BF16)
        return mul_nt(hot, sent)

    total = embed[...].astype(F32)
    total += summed(local[...], 3)
    total += summed(up[0], 5)
    total += summed(down[0], 1)
    total += summed(three[...], jnp.where(is_even, 6, 0))
    total += summed(sib[0], jnp.where(is_even, 2, 4))
    total += summed(sib[1], jnp.where(is_even, 4, 6))
    total += summed(sib[2], jnp.where(is_even, 0, 2))
    rounded = total.astype(BF16)
    latent[...] = rounded
    sent = silu(mul_nt(rounded, w_proc)).astype(BF16)
    message[...] = sent
    hot = far_table(far_ids, here[0], 1, nodes)
    far[...] = mul(hot, sent).astype(BF16)


def far_table(ids, here, sign, nodes):
    count = ids.shape[1]
    column = lax.broadcasted_iota(jnp.int32, ids.shape, 1)
    node = lax.broadcasted_iota(jnp.int32, (ids.shape[0], nodes), 1)
    pieces = []
    for offset in FAR:
        partner = lax.rem(here + sign * offset + count, count)
        chosen = jnp.sum(jnp.where(column == partner, ids[...], 0), axis=1, keepdims=True)
        pieces.append(jnp.where(node == chosen, 1.0, 0.0))
    pieces.append(jnp.zeros_like(pieces[0]))
    return jnp.concatenate(pieces, axis=0).astype(BF16)


def local_body(latent, message, neighbours, out):
    nodes = latent.shape[0]
    count = neighbours.shape[0]
    spare = jnp.zeros((8 - count, nodes), jnp.int32)
    ids = jnp.concatenate([neighbours[...], spare], axis=0).T
    node = lax.broadcasted_iota(jnp.int32, (nodes, nodes), 1)
    table = jnp.zeros((nodes, nodes), F32)
    for k in range(count):
        table += jnp.where(node == ids[:, k : k + 1], 1.0, 0.0)
    out[...] = latent[...].astype(F32) + mul(table.astype(BF16), message[...])


def decode_body(here, base, far_ids, *rest):
    arrived, (weights, out) = rest[:-2], rest[-2:]
    nodes, channels = base.shape
    w_dec = weights[:, WIDE + 2 * channels :]
    hot = far_table(far_ids, here[0], -1, nodes)
    rows = [piece[...].astype(F32) for piece in arrived]
    rows.append(jnp.zeros_like(rows[0]))
    values = jnp.concatenate(rows, axis=0).astype(BF16)
    after = (base[...] + mul_tn(hot, values)).astype(BF16)
    out[...] = silu(mul_nt(after, w_dec)).astype(BF16)


def gather_body(core, latent, table, local, up, down, three, sib, out):
    is_even = core[0] == 0
    nodes = local.shape[0]

    def part(block, offset):
        at = pl.multiple_of(offset * nodes, nodes)
        return mul(table[:, pl.ds(at, nodes)], block)

    total = latent[...].astype(F32)
    total += part(local[...], 3)
    total += part(up[...], 1)
    total += part(down[...], 5)
    total += part(three[...], jnp.where(is_even, 0, 6))
    total += part(sib[0], jnp.where(is_even, 4, 2))
    total += part(sib[1], jnp.where(is_even, 2, 0))
    total += part(sib[2], jnp.where(is_even, 6, 4))
    out[...] = total.astype(BF16)


def call(body, out_shape, args, scratch=(), name=None):
    smem = pl.BlockSpec(memory_space=pltpu.SMEM)
    vmem = pl.BlockSpec(memory_space=pltpu.VMEM)
    specs = [smem if a.ndim == 1 else vmem for a in args]
    many = isinstance(out_shape, (list, tuple))
    return pl.pallas_call(
        body,
        out_shape=out_shape,
        in_specs=specs,
        out_specs=[vmem for _ in out_shape] if many else vmem,
        scratch_shapes=scratch,
        compiler_params=VMEM,
        name=name,
    )(*args)


def shape(*dims, kind=BF16):
    return jax.ShapeDtypeStruct(dims, kind)


def gather_weights(shard):
    patches, chans = lax.axis_size("patch"), lax.axis_size("chan")
    rows = shard.shape[0]
    half = rows // 2
    even = lax.axis_index("patch") % 2 == 0
    me = lax.axis_index("chan")

    def moved(value, even_steps, odd_steps):
        pairs = []
        for p in range(patches):
            steps = even_steps if p % 2 == 0 else odd_steps
            for c in range(chans):
                pairs.append((p * chans + c, p * chans + (c + steps) % chans))
        return lax.ppermute(value, ("patch", "chan"), pairs)

    near = moved(shard, 1, -1)
    part = moved(jnp.where(even, shard[:half], shard[half:]), 2, 2)
    both = by_core(jnp.concatenate([near, part], axis=0), 1, -1)
    near2, part2 = both[:rows], both[rows:]
    before = jnp.where(even, near, near2)
    after = jnp.where(even, near2, near)
    first = jnp.where(even, part, part2)
    second = jnp.where(even, part2, part)
    across = jnp.concatenate([first, second], axis=0)
    ring = jnp.stack([shard, after, across, before])
    order = (jnp.arange(chans) - me) % chans
    return jnp.take(ring, order, axis=0).reshape(chans * rows, -1)


def shards(
    grid_in,
    mesh_embed,
    w_embed,
    w_edge,
    w_proc,
    w_dec,
    pack_rows,
    recv_node,
    far_send,
    far_recv,
    loc_nbr,
    dec_edge,
):
    patch = lax.axis_index("patch").astype(jnp.int32)
    here = patch.reshape(1)
    core = (patch % 2).reshape(1)
    channels = mesh_embed.shape[1]
    nodes = mesh_embed.shape[0]
    rows = grid_in.shape[0]
    offsets, slots = pack_rows.shape[2:]
    x = grid_in.T
    pack = pack_rows.reshape(offsets, 1, slots)
    recv = recv_node.reshape(offsets, 1, slots)
    far_out_ids = far_send.reshape(far_send.shape[2:]).T
    far_in_ids = far_recv.reshape(far_recv.shape[2:]).T
    block = shape(SENT, slots)
    pair = shape(2, SENT, slots)

    shard = call(
        weights_body,
        shape(w_edge.shape[1], WIDE + 3 * channels),
        (w_embed, w_edge, w_proc, w_dec),
        [pltpu.VMEM((WIDE, w_edge.shape[1]), BF16)],
        name="weights",
    )
    up, down, three, own, local = call(
        pack_body,
        [pair, pair, block, block, block],
        (core, x, pack),
        [pltpu.VMEM((SENT, rows), BF16)],
        name="pack",
    )
    weights = lax.all_gather(shard, "chan", axis=0, tiled=True)
    up = shifted(up, 2)
    down = shifted(down, -2)
    three = by_core(three, -3, 3)
    sib = by_core(jnp.stack([own, up[1], down[1]]), 1, -1)
    latent, table = call(
        prepare_body,
        [shape(rows, channels), shape(rows, offsets * nodes)],
        (x, weights, dec_edge.T),
        [pltpu.VMEM((WIDE, rows), BF16)],
        name="prepare",
    )
    mesh_latent, node_msg, far_sent = call(
        encode_body,
        [shape(nodes, channels), shape(nodes, channels), shape(8 * len(FAR) + 8, channels)],
        (core, here, local, up, down, three, sib, weights, recv, mesh_embed, far_out_ids),
        name="encode",
    )
    arrived = [
        shifted(far_sent[8 * i : 8 * i + 8], offset) for i, offset in enumerate(FAR)
    ]
    base = call(
        local_body,
        shape(nodes, channels, kind=F32),
        (mesh_latent, node_msg, loc_nbr.T),
        name="short",
    )
    dec_msg = call(
        decode_body,
        shape(nodes, channels),
        (here, base, far_in_ids, *arrived, weights),
        name="decode",
    )
    up = shifted(dec_msg, 2)
    down = shifted(dec_msg, -2)
    three = by_core(dec_msg, -3, 3)
    sib = by_core(jnp.stack([dec_msg, up, down]), 1, -1)
    return call(
        gather_body,
        shape(rows, channels),
        (core, latent, table, dec_msg, up, down, three, sib),
        name="collect",
    )


def solution(mesh):
    both = P(("patch", "chan"), None)
    column = P(None, "chan")
    lists = P("patch", "chan", None, None)
    in_specs = (both, both, column, column, column, column, lists, lists, lists, lists, both, both)
    return jax.shard_map(shards, mesh=mesh, in_specs=in_specs, out_specs=both, check_vma=False)
```

time: 325 us -> 201 us (0.62)
  the two profiles are of different devices: /device:TPU:8 before, /device:TPU:56 now
where the time goes in v1:
time: 201 us; the launch traced here: 200 us
  starting transfers between devices  106 us (53%)
  Pallas kernels  41.1 us (20%)
  waiting for transfers between devices  33 us (16%)
  between operations  13.9 us (7%)
  local copies, waits for them, and re-layouts  3.66 us (2%)
  other arithmetic  2.55 us (1%)
    ppermute x17, starting transfers between devices, shifted(): lax.ppermute(value, 'patch', [(i, (i + steps) % count) for i in range(cou...  80.3 us
    pallas_call x7, Pallas kernels, call(): pl.pallas_call(body, out_shape=out_shape, in_specs=specs, out_specs=[vmem...  41.1 us
    ppermute x17, waiting for transfers between devices, shifted(): lax.ppermute(value, 'patch', [(i, (i + steps) % count) for i in range(cou...  25.4 us
    ppermute x4, starting transfers between devices, by_core(): return lax.ppermute(value, 'patch', pairs)  25.2 us
    ppermute x4, waiting for transfers between devices, by_core(): return lax.ppermute(value, 'patch', pairs)  7.63 us
  transfers between devices with their start and end apart: 22, of which 6 were waited for; matrix products, arithmetic and copies ran while one was open for 1% of the time, Pallas kernels for 8%

profile of v1, /device:TPU:56, one launch (start us, length us, event | category | flops | bytes accessed | tf_op | source)
XLA Modules:
  0.0 199.8 jit_solution(943535128789565319)
XLA Ops:
  6.5 0.0 all-gather.2.cloned.1.call-start
  6.5 2.1 %weights.1 = bf16[128,1792]{1,0:T(8,128)(2,1)} custom-call(bf16[227,128]{1,0:T(8,128)(2,1)} %embed.2, bf16[512,128]{1,0:T(8,128)(2,1)} %edge.1, bf16[512,128]{1,0:T(8,128)(2,1)} %proc.1, bf16[512,128]{1,0:T(8,128)(2,1)} %dec.1), custom_call_target="tpu_custom_call" | custom-call | tf_op jit(solution)/shard_map/weights/pallas_call | solution.py:201
  8.7 0.0 all-gather.2.cloned.1.call-update
  8.7 3.7 %pack.1 = (bf16[2,240,384]{2,1,0:T(8,128)(2,1)}, bf16[2,240,384]{2,1,0:T(8,128)(2,1)}, bf16[240,384]{1,0:T(8,128)(2,1)}, bf16[240,384]{1,0:T(8,128)(2,1)}, bf16[240,384]{1,0:T(8,128)(2,1)}) custom-call(s32[1]{0:T(128)} %bitcast.core, bf16[227,1024]{1,0:T(8,128)(2,1)} %bitcast.20, s32[7,1,384]{2,1,0:T(1,128)} %bitcast.26), custom_call_target="tpu_custom_call" | custom-call | tf_op jit(solution)/shard_map/pack/pallas_call | solution.py:201
  12.4 2.1 %collective-permute-start.1 = (bf16[2,240,384]{2,1,0:T(8,128)(2,1)}, bf16[2,240,384]{2,1,0:T(8,128)(2,1)S(1)}, u32[]{:S(2)}, u32[]{:S(2)}) collective-permute-start(bf16[2,240,384]{2,1,0:T(8,128)(2,1)} %get-tuple-element.19), channel_id=1, source_target_pairs={{0,504},{4,508},{8,0},{12,4},{16,8},{20,12},{24,16},{28,20},{32,24... | collective-permute-start | bytes 1105928 | tf_op jit(solution)/shard_map/ppermute | solution.py:37
  14.6 3.8 %collective-permute-start = (bf16[2,240,384]{2,1,0:T(8,128)(2,1)}, bf16[2,240,384]{2,1,0:T(8,128)(2,1)S(1)}, u32[]{:S(2)}, u32[]{:S(2)}) collective-permute-start(bf16[2,240,384]{2,1,0:T(8,128)(2,1)} %get-tuple-element.18), channel_id=1, source_target_pairs={{0,8},{4,12},{8,16},{12,20},{16,24},{20,28},{24,32},{28,36},{32,40... | collective-permute-start | bytes 1105928 | tf_op jit(solution)/shard_map/ppermute | solution.py:37
  18.4 6.8 %collective-permute-done.1.down = bf16[2,240,384]{2,1,0:T(8,128)(2,1)S(1)} collective-permute-done((bf16[2,240,384]{2,1,0:T(8,128)(2,1)}, bf16[2,240,384]{2,1,0:T(8,128)(2,1)S(1)}, u32[]{:S(2)}, u32[]{:S(2)}) %collective-permute-start.1) | collective-permute-done | bytes 368672 | tf_op jit(solution)/shard_map/ppermute | solution.py:37
  25.2 11.5 %collective-permute-done.up = bf16[2,240,384]{2,1,0:T(8,128)(2,1)S(1)} collective-permute-done((bf16[2,240,384]{2,1,0:T(8,128)(2,1)}, bf16[2,240,384]{2,1,0:T(8,128)(2,1)S(1)}, u32[]{:S(2)}, u32[]{:S(2)}) %collective-permute-start) | collective-permute-done | bytes 368672 | tf_op jit(solution)/shard_map/ppermute | solution.py:37
  36.7 1.1 pad_maximum_fusion.1
  37.8 1.9 collective-permute-start.3
  39.8 6.2 %collective-permute-start.2 = (bf16[240,384]{1,0:T(8,128)(2,1)S(1)}, bf16[240,384]{1,0:T(8,128)(2,1)S(1)}, u32[]{:S(2)}, u32[]{:S(2)}) collective-permute-start(bf16[240,384]{1,0:T(8,128)(2,1)S(1)} %copy-done.22), channel_id=1, source_target_pairs={{0,500},{4,16},{8,508},{12,24},{16,4},{20,32},{24,12},{28,40},{32,... | collective-permute-start | bytes 552968 | tf_op jit(solution)/shard_map/ppermute | solution.py:43
  45.9 5.0 %collective-permute-done.2.three = bf16[240,384]{1,0:T(8,128)(2,1)S(1)} collective-permute-done((bf16[240,384]{1,0:T(8,128)(2,1)S(1)}, bf16[240,384]{1,0:T(8,128)(2,1)S(1)}, u32[]{:S(2)}, u32[]{:S(2)}) %collective-permute-start.2) | collective-permute-done | bytes 184352 | tf_op jit(solution)/shard_map/ppermute | solution.py:43
  50.9 0.0 collective-permute-done.3.sib
  50.9 0.0 all-gather.2.cloned.1.call-done.weights.rest_13_
  51.0 0.6 copy-done.8
  51.6 0.2 copy-done.6
  51.8 9.5 %encode.1 = (bf16[512,512]{1,0:T(8,128)(2,1)}, bf16[512,512]{1,0:T(8,128)(2,1)}, bf16[112,512]{1,0:T(8,128)(2,1)}) custom-call(s32[1]{0:T(128)} %bitcast.core, s32[1]{0:T(128)} %bitcast.3.here, bf16[240,384]{1,0:T(8,128)(2,1)} %get-tuple-element.17.local, bf16[2,240,384]{2,1,0:T(8,128)(2,1)} %copy-done.5, bf16[2,240,384]{2,1,0:T(8,128)(2,1)} %copy-done.4, ...), custom_call_target="tpu_custom_call" | custom-call | tf_op jit(solution)/shard_map/encode/pallas_call | solution.py:201
  61.2 0.9 fusion
  62.1 1.9 collective-permute-start.4
  64.0 2.4 %collective-permute-start.5 = (bf16[8,512]{1,0:T(8,128)(2,1)S(1)}, bf16[8,512]{1,0:T(8,128)(2,1)S(1)}, u32[]{:S(2)}, u32[]{:S(2)}) collective-permute-start(bf16[8,512]{1,0:T(8,128)(2,1)S(1)} %get-tuple-element.36), channel_id=1, source_target_pairs={{0,128},{4,132},{8,136},{12,140},{16,144},{20,148},{24,152},{28,15... | collective-permute-start | bytes 24584 | tf_op jit(solution)/shard_map/ppermute | solution.py:37
  66.4 4.7 %collective-permute-start.6 = (bf16[8,512]{1,0:T(8,128)(2,1)S(1)}, bf16[8,512]{1,0:T(8,128)(2,1)S(1)}, u32[]{:S(2)}, u32[]{:S(2)}) collective-permute-start(bf16[8,512]{1,0:T(8,128)(2,1)S(1)} %get-tuple-element.35), channel_id=1, source_target_pairs={{0,384},{4,388},{8,392},{12,396},{16,400},{20,404},{24,408},{28,41... | collective-permute-start | bytes 24584 | tf_op jit(solution)/shard_map/ppermute | solution.py:37
  71.1 11.1 %collective-permute-start.7 = (bf16[8,512]{1,0:T(8,128)(2,1)S(1)}, bf16[8,512]{1,0:T(8,128)(2,1)S(1)}, u32[]{:S(2)}, u32[]{:S(2)}) collective-permute-start(bf16[8,512]{1,0:T(8,128)(2,1)S(1)} %get-tuple-element.34), channel_id=1, source_target_pairs={{0,64},{4,68},{8,72},{12,76},{16,80},{20,84},{24,88},{28,92},{32,9... | collective-permute-start | bytes 24584 | tf_op jit(solution)/shard_map/ppermute | solution.py:37
  82.2 5.6 %collective-permute-start.8 = (bf16[8,512]{1,0:T(8,128)(2,1)S(1)}, bf16[8,512]{1,0:T(8,128)(2,1)S(1)}, u32[]{:S(2)}, u32[]{:S(2)}) collective-permute-start(bf16[8,512]{1,0:T(8,128)(2,1)S(1)} %get-tuple-element.33), channel_id=1, source_target_pairs={{0,448},{4,452},{8,456},{12,460},{16,464},{20,468},{24,472},{28,47... | collective-permute-start | bytes 24584 | tf_op jit(solution)/shard_map/ppermute | solution.py:37
  87.8 0.0 collective-permute-done.4.rest_0_
  87.8 6.8 %collective-permute-start.9 = (bf16[8,512]{1,0:T(8,128)(2,1)S(1)}, bf16[8,512]{1,0:T(8,128)(2,1)S(1)}, u32[]{:S(2)}, u32[]{:S(2)}) collective-permute-start(bf16[8,512]{1,0:T(8,128)(2,1)S(1)} %get-tuple-element.32), channel_id=1, source_target_pairs={{0,32},{4,36},{8,40},{12,44},{16,48},{20,52},{24,56},{28,60},{32,6... | collective-permute-start | bytes 24584 | tf_op jit(solution)/shard_map/ppermute | solution.py:37
  94.6 0.0 collective-permute-done.5.rest_1_
  94.7 5.0 %collective-permute-start.10 = (bf16[8,512]{1,0:T(8,128)(2,1)S(1)}, bf16[8,512]{1,0:T(8,128)(2,1)S(1)}, u32[]{:S(2)}, u32[]{:S(2)}) collective-permute-start(bf16[8,512]{1,0:T(8,128)(2,1)S(1)} %get-tuple-element.31), channel_id=1, source_target_pairs={{0,480},{4,484},{8,488},{12,492},{16,496},{20,500},{24,504},{28,50... | collective-permute-start | bytes 24584 | tf_op jit(solution)/shard_map/ppermute | solution.py:37
  99.7 0.0 collective-permute-done.6.rest_2_
  99.7 3.6 %collective-permute-start.11 = (bf16[8,512]{1,0:T(8,128)(2,1)S(1)}, bf16[8,512]{1,0:T(8,128)(2,1)S(1)}, u32[]{:S(2)}, u32[]{:S(2)}) collective-permute-start(bf16[8,512]{1,0:T(8,128)(2,1)S(1)} %get-tuple-element.30), channel_id=1, source_target_pairs={{0,16},{4,20},{8,24},{12,28},{16,32},{20,36},{24,40},{28,44},{32,4... | collective-permute-start | bytes 24584 | tf_op jit(solution)/shard_map/ppermute | solution.py:37
  103.4 0.0 collective-permute-done.7.rest_3_
  103.4 6.4 %collective-permute-start.12 = (bf16[8,512]{1,0:T(8,128)(2,1)S(1)}, bf16[8,512]{1,0:T(8,128)(2,1)S(1)}, u32[]{:S(2)}, u32[]{:S(2)}) collective-permute-start(bf16[8,512]{1,0:T(8,128)(2,1)S(1)} %get-tuple-element.29), channel_id=1, source_target_pairs={{0,496},{4,500},{8,504},{12,508},{16,0},{20,4},{24,8},{28,12},{32,... | collective-permute-start | bytes 24584 | tf_op jit(solution)/shard_map/ppermute | solution.py:37
  109.8 0.0 collective-permute-done.8.rest_4_
  109.8 2.1 %collective-permute-start.13 = (bf16[8,512]{1,0:T(8,128)(2,1)S(1)}, bf16[8,512]{1,0:T(8,128)(2,1)S(1)}, u32[]{:S(2)}, u32[]{:S(2)}) collective-permute-start(bf16[8,512]{1,0:T(8,128)(2,1)S(1)} %get-tuple-element.28), channel_id=1, source_target_pairs={{0,8},{4,12},{8,16},{12,20},{16,24},{20,28},{24,32},{28,36},{32,40... | collective-permute-start | bytes 24584 | tf_op jit(solution)/shard_map/ppermute | solution.py:37
  111.9 0.0 collective-permute-done.9.rest_5_
  112.0 6.7 %collective-permute-start.14 = (bf16[8,512]{1,0:T(8,128)(2,1)S(1)}, bf16[8,512]{1,0:T(8,128)(2,1)S(1)}, u32[]{:S(2)}, u32[]{:S(2)}) collective-permute-start(bf16[8,512]{1,0:T(8,128)(2,1)S(1)} %get-tuple-element.27), channel_id=1, source_target_pairs={{0,504},{4,508},{8,0},{12,4},{16,8},{20,12},{24,16},{28,20},{32,24... | collective-permute-start | bytes 24584 | tf_op jit(solution)/shard_map/ppermute | solution.py:37
  118.7 0.0 collective-permute-done.10.rest_6_
  118.7 1.9 collective-permute-start.15
  120.6 0.0 collective-permute-done.11.rest_7_
  120.6 3.6 %collective-permute-start.16 = (bf16[8,512]{1,0:T(8,128)(2,1)S(1)}, bf16[8,512]{1,0:T(8,128)(2,1)S(1)}, u32[]{:S(2)}, u32[]{:S(2)}) collective-permute-start(bf16[8,512]{1,0:T(8,128)(2,1)S(1)} %get-tuple-element.25), channel_id=1, source_target_pairs={{0,508},{4,0},{8,4},{12,8},{16,12},{20,16},{24,20},{28,24},{32,28}... | collective-permute-start | bytes 24584 | tf_op jit(solution)/shard_map/ppermute | solution.py:37
  124.3 3.4 %short.1.base = f32[512,512]{1,0:T(8,128)} custom-call(bf16[512,512]{1,0:T(8,128)(2,1)} %get-tuple-element.22.latent, bf16[512,512]{1,0:T(8,128)(2,1)} %get-tuple-element.23.message, s32[6,512]{1,0:T(8,128)} %bitcast.23), custom_call_target="tpu_custom_call" | custom-call | tf_op jit(solution)/shard_map/short/pallas_call | solution.py:201
  127.6 0.0 collective-permute-done.12.rest_8_
  127.7 0.0 collective-permute-done.13.rest_9_
  127.7 0.0 collective-permute-done.14.rest_10_
  127.7 0.0 collective-permute-done.15.rest_11_
  127.7 0.0 collective-permute-done.16.rest_12_
  127.8 0.4 copy-done.17
  128.3 0.0 copy-done.18
  128.3 0.0 copy-done.19
  128.3 0.0 copy-done.20
  128.3 0.0 copy-done.21
  128.3 3.5 %decode.1.local = bf16[512,512]{1,0:T(8,128)(2,1)} custom-call(s32[1]{0:T(128)} %bitcast.3.here, f32[512,512]{1,0:T(8,128)} %short.1.base, s32[8,128]{1,0:T(8,128)} %bitcast.27, bf16[8,512]{1,0:T(8,128)(2,1)} %copy-done.9, bf16[8,512]{1,0:T(8,128)(2,1)} %copy-done.10, bf16[8,512]{1,0:T(8,128)(2,1)} %copy-done.11, bf16[8,512]{1,0:T(8,128)(2,1)} %copy-done.12, ...), custom_call_target="tpu_custom_call" | custom-call | tf_op jit(solution)/shard_map/decode/pallas_call | solution.py:201
  131.8 1.9 collective-permute-start.17
  133.7 10.6 %collective-permute-start.18 = (bf16[512,512]{1,0:T(8,128)(2,1)}, bf16[512,512]{1,0:T(8,128)(2,1)S(1)}, u32[]{:S(2)}, u32[]{:S(2)}) collective-permute-start(bf16[512,512]{1,0:T(8,128)(2,1)} %decode.1.local), channel_id=1, source_target_pairs={{0,504},{4,508},{8,0},{12,4},{16,8},{20,12},{24,16},{28,20},{32,24... | collective-permute-start | bytes 1572872 | tf_op jit(solution)/shard_map/ppermute | solution.py:37
  144.3 5.8 %collective-permute-done.17.up = bf16[512,512]{1,0:T(8,128)(2,1)S(1)} collective-permute-done((bf16[512,512]{1,0:T(8,128)(2,1)}, bf16[512,512]{1,0:T(8,128)(2,1)S(1)}, u32[]{:S(2)}, u32[]{:S(2)}) %collective-permute-start.17) | collective-permute-done | bytes 524320 | tf_op jit(solution)/shard_map/ppermute | solution.py:37
  150.1 1.3 collective-permute-done.18.down
  151.4 1.4 pad_maximum_fusion
  152.9 1.9 collective-permute-start.20
  154.8 15.2 %collective-permute-start.19 = (bf16[512,512]{1,0:T(8,128)(2,1)S(1)}, bf16[512,512]{1,0:T(8,128)(2,1)S(1)}, u32[]{:S(2)}, u32[]{:S(2)}) collective-permute-start(bf16[512,512]{1,0:T(8,128)(2,1)S(1)} %copy-done), channel_id=1, source_target_pairs={{0,500},{4,16},{8,508},{12,24},{16,4},{20,32},{24,12},{28,40},{32,... | collective-permute-start | bytes 1572872 | tf_op jit(solution)/shard_map/ppermute | solution.py:43
  170.0 9.7 %prepare.1 = (bf16[1024,512]{1,0:T(8,128)(2,1)}, bf16[1024,3584]{1,0:T(8,128)(2,1)}) custom-call(bf16[227,1024]{1,0:T(8,128)(2,1)} %bitcast.21, bf16[512,1792]{1,0:T(8,128)(2,1)} %all-gather.2.cloned.1.call-done.weights.rest_13_, s32[3,1024]{1,0:T(4,128)} %bitcast.24), custom_call_target="tpu_custom_call" | custom-call | tf_op jit(solution)/shard_map/prepare/pallas_call | solution.py:201
  179.7 2.6 %collective-permute-done.19.three = bf16[512,512]{1,0:T(8,128)(2,1)S(1)} collective-permute-done((bf16[512,512]{1,0:T(8,128)(2,1)S(1)}, bf16[512,512]{1,0:T(8,128)(2,1)S(1)}, u32[]{:S(2)}, u32[]{:S(2)}) %collective-permute-start.19) | collective-permute-done | bytes 524320 | tf_op jit(solution)/shard_map/ppermute | solution.py:43
  182.3 0.0 collective-permute-done.20.sib
  182.3 0.8 copy-done.7
  183.1 0.6 copy-done.3
  183.7 9.3 %collect.1 = bf16[1024,512]{1,0:T(8,128)(2,1)} custom-call(s32[1]{0:T(128)} %bitcast.core, bf16[1024,512]{1,0:T(8,128)(2,1)} %get-tuple-element.15.latent, bf16[1024,3584]{1,0:T(8,128)(2,1)} %get-tuple-element.16.table, bf16[512,512]{1,0:T(8,128)(2,1)} %decode.1.local, bf16[512,512]{1,0:T(8,128)(2,1)} %copy-done.1, bf16[512,512]{1,0:T(8,128)(2,1)} %copy-done.2, ...), custom_call_target="tpu_custom_call" | custom-call | tf_op jit(solution)/shard_map/collect/pallas_call | solution.py:201
  (39 shorter events, 0.1 us)
Async XLA Ops:
  6.5 44.4 %all-gather.2.cloned.1.call-start = ((), (), s32[]{:S(2)}) async-start(), calls=%async_computation | async-start | bytes 2293760 | tf_op jit(solution)/shard_map/all_gather | solution.py:288
  12.4 27.3 %copy-start.22 = (bf16[240,384]{1,0:T(8,128)(2,1)S(1)}, bf16[240,384]{1,0:T(8,128)(2,1)}, u32[]{:S(2)}) copy-start(bf16[240,384]{1,0:T(8,128)(2,1)} %get-tuple-element.20) | copy-start | bytes 552964
  12.4 12.7 %collective-permute-start.1 = (bf16[2,240,384]{2,1,0:T(8,128)(2,1)}, bf16[2,240,384]{2,1,0:T(8,128)(2,1)S(1)}, u32[]{:S(2)}, u32[]{:S(2)}) collective-permute-start(bf16[2,240,384]{2,1,0:T(8,128)(2,1)} %get-tuple-element.19), channel_id=1, source_target_pairs={{0,504},{4,508},{8,0},{12,4},{16,8},{20,12},{24,16},{28,20},{32,24... | collective-permute-start | bytes 1105928 | tf_op jit(solution)/shard_map/ppermute | solution.py:37
  14.6 22.1 %collective-permute-start = (bf16[2,240,384]{2,1,0:T(8,128)(2,1)}, bf16[2,240,384]{2,1,0:T(8,128)(2,1)S(1)}, u32[]{:S(2)}, u32[]{:S(2)}) collective-permute-start(bf16[2,240,384]{2,1,0:T(8,128)(2,1)} %get-tuple-element.18), channel_id=1, source_target_pairs={{0,8},{4,12},{8,16},{12,20},{16,24},{20,28},{24,32},{28,36},{32,40... | collective-permute-start | bytes 1105928 | tf_op jit(solution)/shard_map/ppermute | solution.py:37
  25.1 25.8 %copy-start.4 = (bf16[2,240,384]{2,1,0:T(8,128)(2,1)}, bf16[2,240,384]{2,1,0:T(8,128)(2,1)S(1)}, u32[]{:S(2)}) copy-start(bf16[2,240,384]{2,1,0:T(8,128)(2,1)S(1)} %collective-permute-done.1.down) | copy-start | bytes 1105924
  36.7 14.3 %copy-start.5 = (bf16[2,240,384]{2,1,0:T(8,128)(2,1)}, bf16[2,240,384]{2,1,0:T(8,128)(2,1)S(1)}, u32[]{:S(2)}) copy-start(bf16[2,240,384]{2,1,0:T(8,128)(2,1)S(1)} %collective-permute-done.up) | copy-start | bytes 1105924
  37.8 13.1 %collective-permute-start.3 = (bf16[3,240,384]{2,1,0:T(8,128)(2,1)S(1)}, bf16[3,240,384]{2,1,0:T(8,128)(2,1)S(1)}, u32[]{:S(2)}, u32[]{:S(2)}) collective-permute-start(bf16[3,240,384]{2,1,0:T(8,128)(2,1)S(1)} %pad_maximum_fusion.1), channel_id=1, source_target_pairs={{0,4},{4,0},{8,12},{12,8},{16,20},{20,16},{24,28},{28,24},{32,36},... | collective-permute-start | bytes 1658888 | tf_op jit(solution)/shard_map/ppermute | solution.py:43
  39.8 11.2 %collective-permute-start.2 = (bf16[240,384]{1,0:T(8,128)(2,1)S(1)}, bf16[240,384]{1,0:T(8,128)(2,1)S(1)}, u32[]{:S(2)}, u32[]{:S(2)}) collective-permute-start(bf16[240,384]{1,0:T(8,128)(2,1)S(1)} %copy-done.22), channel_id=1, source_target_pairs={{0,500},{4,16},{8,508},{12,24},{16,4},{20,32},{24,12},{28,40},{32,... | collective-permute-start | bytes 552968 | tf_op jit(solution)/shard_map/ppermute | solution.py:43
  50.9 0.7 copy-start.8
  50.9 0.9 copy-start.6
  62.1 25.7 %collective-permute-start.4 = (bf16[8,512]{1,0:T(8,128)(2,1)S(1)}, bf16[8,512]{1,0:T(8,128)(2,1)S(1)}, u32[]{:S(2)}, u32[]{:S(2)}) collective-permute-start(bf16[8,512]{1,0:T(8,128)(2,1)S(1)} %get-tuple-element.37), channel_id=1, source_target_pairs={{0,256},{4,260},{8,264},{12,268},{16,272},{20,276},{24,280},{28,28... | collective-permute-start | bytes 24584 | tf_op jit(solution)/shard_map/ppermute | solution.py:37
  64.0 30.6 %collective-permute-start.5 = (bf16[8,512]{1,0:T(8,128)(2,1)S(1)}, bf16[8,512]{1,0:T(8,128)(2,1)S(1)}, u32[]{:S(2)}, u32[]{:S(2)}) collective-permute-start(bf16[8,512]{1,0:T(8,128)(2,1)S(1)} %get-tuple-element.36), channel_id=1, source_target_pairs={{0,128},{4,132},{8,136},{12,140},{16,144},{20,148},{24,152},{28,15... | collective-permute-start | bytes 24584 | tf_op jit(solution)/shard_map/ppermute | solution.py:37
  66.4 33.3 %collective-permute-start.6 = (bf16[8,512]{1,0:T(8,128)(2,1)S(1)}, bf16[8,512]{1,0:T(8,128)(2,1)S(1)}, u32[]{:S(2)}, u32[]{:S(2)}) collective-permute-start(bf16[8,512]{1,0:T(8,128)(2,1)S(1)} %get-tuple-element.35), channel_id=1, source_target_pairs={{0,384},{4,388},{8,392},{12,396},{16,400},{20,404},{24,408},{28,41... | collective-permute-start | bytes 24584 | tf_op jit(solution)/shard_map/ppermute | solution.py:37
  71.1 32.3 %collective-permute-start.7 = (bf16[8,512]{1,0:T(8,128)(2,1)S(1)}, bf16[8,512]{1,0:T(8,128)(2,1)S(1)}, u32[]{:S(2)}, u32[]{:S(2)}) collective-permute-start(bf16[8,512]{1,0:T(8,128)(2,1)S(1)} %get-tuple-element.34), channel_id=1, source_target_pairs={{0,64},{4,68},{8,72},{12,76},{16,80},{20,84},{24,88},{28,92},{32,9... | collective-permute-start | bytes 24584 | tf_op jit(solution)/shard_map/ppermute | solution.py:37
  82.2 27.6 %collective-permute-start.8 = (bf16[8,512]{1,0:T(8,128)(2,1)S(1)}, bf16[8,512]{1,0:T(8,128)(2,1)S(1)}, u32[]{:S(2)}, u32[]{:S(2)}) collective-permute-start(bf16[8,512]{1,0:T(8,128)(2,1)S(1)} %get-tuple-element.33), channel_id=1, source_target_pairs={{0,448},{4,452},{8,456},{12,460},{16,464},{20,468},{24,472},{28,47... | collective-permute-start | bytes 24584 | tf_op jit(solution)/shard_map/ppermute | solution.py:37
  87.8 39.9 %copy-start.9 = (bf16[8,512]{1,0:T(8,128)(2,1)}, bf16[8,512]{1,0:T(8,128)(2,1)S(1)}, u32[]{:S(2)}) copy-start(bf16[8,512]{1,0:T(8,128)(2,1)S(1)} %collective-permute-done.4.rest_0_) | copy-start | bytes 24580
  87.8 24.1 %collective-permute-start.9 = (bf16[8,512]{1,0:T(8,128)(2,1)S(1)}, bf16[8,512]{1,0:T(8,128)(2,1)S(1)}, u32[]{:S(2)}, u32[]{:S(2)}) collective-permute-start(bf16[8,512]{1,0:T(8,128)(2,1)S(1)} %get-tuple-element.32), channel_id=1, source_target_pairs={{0,32},{4,36},{8,40},{12,44},{16,48},{20,52},{24,56},{28,60},{32,6... | collective-permute-start | bytes 24584 | tf_op jit(solution)/shard_map/ppermute | solution.py:37
  94.6 33.1 %copy-start.10 = (bf16[8,512]{1,0:T(8,128)(2,1)}, bf16[8,512]{1,0:T(8,128)(2,1)S(1)}, u32[]{:S(2)}) copy-start(bf16[8,512]{1,0:T(8,128)(2,1)S(1)} %collective-permute-done.5.rest_1_) | copy-start | bytes 24580
  94.7 24.0 %collective-permute-start.10 = (bf16[8,512]{1,0:T(8,128)(2,1)S(1)}, bf16[8,512]{1,0:T(8,128)(2,1)S(1)}, u32[]{:S(2)}, u32[]{:S(2)}) collective-permute-start(bf16[8,512]{1,0:T(8,128)(2,1)S(1)} %get-tuple-element.31), channel_id=1, source_target_pairs={{0,480},{4,484},{8,488},{12,492},{16,496},{20,500},{24,504},{28,50... | collective-permute-start | bytes 24584 | tf_op jit(solution)/shard_map/ppermute | solution.py:37
  99.7 28.0 %copy-start.11 = (bf16[8,512]{1,0:T(8,128)(2,1)}, bf16[8,512]{1,0:T(8,128)(2,1)S(1)}, u32[]{:S(2)}) copy-start(bf16[8,512]{1,0:T(8,128)(2,1)S(1)} %collective-permute-done.6.rest_2_) | copy-start | bytes 24580
  99.7 20.9 %collective-permute-start.11 = (bf16[8,512]{1,0:T(8,128)(2,1)S(1)}, bf16[8,512]{1,0:T(8,128)(2,1)S(1)}, u32[]{:S(2)}, u32[]{:S(2)}) collective-permute-start(bf16[8,512]{1,0:T(8,128)(2,1)S(1)} %get-tuple-element.30), channel_id=1, source_target_pairs={{0,16},{4,20},{8,24},{12,28},{16,32},{20,36},{24,40},{28,44},{32,4... | collective-permute-start | bytes 24584 | tf_op jit(solution)/shard_map/ppermute | solution.py:37
  103.4 24.4 %copy-start.12 = (bf16[8,512]{1,0:T(8,128)(2,1)}, bf16[8,512]{1,0:T(8,128)(2,1)S(1)}, u32[]{:S(2)}) copy-start(bf16[8,512]{1,0:T(8,128)(2,1)S(1)} %collective-permute-done.7.rest_3_) | copy-start | bytes 24580
  103.4 24.3 %collective-permute-start.12 = (bf16[8,512]{1,0:T(8,128)(2,1)S(1)}, bf16[8,512]{1,0:T(8,128)(2,1)S(1)}, u32[]{:S(2)}, u32[]{:S(2)}) collective-permute-start(bf16[8,512]{1,0:T(8,128)(2,1)S(1)} %get-tuple-element.29), channel_id=1, source_target_pairs={{0,496},{4,500},{8,504},{12,508},{16,0},{20,4},{24,8},{28,12},{32,... | collective-permute-start | bytes 24584 | tf_op jit(solution)/shard_map/ppermute | solution.py:37
  109.8 17.9 %copy-start.13 = (bf16[8,512]{1,0:T(8,128)(2,1)}, bf16[8,512]{1,0:T(8,128)(2,1)S(1)}, u32[]{:S(2)}) copy-start(bf16[8,512]{1,0:T(8,128)(2,1)S(1)} %collective-permute-done.8.rest_4_) | copy-start | bytes 24580
  109.8 17.8 %collective-permute-start.13 = (bf16[8,512]{1,0:T(8,128)(2,1)S(1)}, bf16[8,512]{1,0:T(8,128)(2,1)S(1)}, u32[]{:S(2)}, u32[]{:S(2)}) collective-permute-start(bf16[8,512]{1,0:T(8,128)(2,1)S(1)} %get-tuple-element.28), channel_id=1, source_target_pairs={{0,8},{4,12},{8,16},{12,20},{16,24},{20,28},{24,32},{28,36},{32,40... | collective-permute-start | bytes 24584 | tf_op jit(solution)/shard_map/ppermute | solution.py:37
  111.9 15.8 %copy-start.14 = (bf16[8,512]{1,0:T(8,128)(2,1)}, bf16[8,512]{1,0:T(8,128)(2,1)S(1)}, u32[]{:S(2)}) copy-start(bf16[8,512]{1,0:T(8,128)(2,1)S(1)} %collective-permute-done.9.rest_5_) | copy-start | bytes 24580
  112.0 15.7 %collective-permute-start.14 = (bf16[8,512]{1,0:T(8,128)(2,1)S(1)}, bf16[8,512]{1,0:T(8,128)(2,1)S(1)}, u32[]{:S(2)}, u32[]{:S(2)}) collective-permute-start(bf16[8,512]{1,0:T(8,128)(2,1)S(1)} %get-tuple-element.27), channel_id=1, source_target_pairs={{0,504},{4,508},{8,0},{12,4},{16,8},{20,12},{24,16},{28,20},{32,24... | collective-permute-start | bytes 24584 | tf_op jit(solution)/shard_map/ppermute | solution.py:37
  118.7 9.1 %copy-start.15 = (bf16[8,512]{1,0:T(8,128)(2,1)}, bf16[8,512]{1,0:T(8,128)(2,1)S(1)}, u32[]{:S(2)}) copy-start(bf16[8,512]{1,0:T(8,128)(2,1)S(1)} %collective-permute-done.10.rest_6_) | copy-start | bytes 24580
  118.7 9.0 %collective-permute-start.15 = (bf16[8,512]{1,0:T(8,128)(2,1)S(1)}, bf16[8,512]{1,0:T(8,128)(2,1)S(1)}, u32[]{:S(2)}, u32[]{:S(2)}) collective-permute-start(bf16[8,512]{1,0:T(8,128)(2,1)S(1)} %get-tuple-element.26), channel_id=1, source_target_pairs={{0,4},{4,8},{8,12},{12,16},{16,20},{20,24},{24,28},{28,32},{32,36}... | collective-permute-start | bytes 24584 | tf_op jit(solution)/shard_map/ppermute | solution.py:37
  120.6 7.2 %copy-start.16 = (bf16[8,512]{1,0:T(8,128)(2,1)}, bf16[8,512]{1,0:T(8,128)(2,1)S(1)}, u32[]{:S(2)}) copy-start(bf16[8,512]{1,0:T(8,128)(2,1)S(1)} %collective-permute-done.11.rest_7_) | copy-start | bytes 24580
  120.6 7.1 %collective-permute-start.16 = (bf16[8,512]{1,0:T(8,128)(2,1)S(1)}, bf16[8,512]{1,0:T(8,128)(2,1)S(1)}, u32[]{:S(2)}, u32[]{:S(2)}) collective-permute-start(bf16[8,512]{1,0:T(8,128)(2,1)S(1)} %get-tuple-element.25), channel_id=1, source_target_pairs={{0,508},{4,0},{8,4},{12,8},{16,12},{20,16},{24,20},{28,24},{32,28}... | collective-permute-start | bytes 24584 | tf_op jit(solution)/shard_map/ppermute | solution.py:37
  127.6 0.6 copy-start.17
  127.7 0.6 copy-start.18
  127.7 0.6 copy-start.19
  127.7 0.6 copy-start.20
  127.7 0.6 copy-start.21
  131.8 18.3 %collective-permute-start.17 = (bf16[512,512]{1,0:T(8,128)(2,1)}, bf16[512,512]{1,0:T(8,128)(2,1)S(1)}, u32[]{:S(2)}, u32[]{:S(2)}) collective-permute-start(bf16[512,512]{1,0:T(8,128)(2,1)} %decode.1.local), channel_id=1, source_target_pairs={{0,8},{4,12},{8,16},{12,20},{16,24},{20,28},{24,32},{28,36},{32,40... | collective-permute-start | bytes 1572872 | tf_op jit(solution)/shard_map/ppermute | solution.py:37
  133.7 17.7 %collective-permute-start.18 = (bf16[512,512]{1,0:T(8,128)(2,1)}, bf16[512,512]{1,0:T(8,128)(2,1)S(1)}, u32[]{:S(2)}, u32[]{:S(2)}) collective-permute-start(bf16[512,512]{1,0:T(8,128)(2,1)} %decode.1.local), channel_id=1, source_target_pairs={{0,504},{4,508},{8,0},{12,4},{16,8},{20,12},{24,16},{28,20},{32,24... | collective-permute-start | bytes 1572872 | tf_op jit(solution)/shard_map/ppermute | solution.py:37
  150.1 2.7 %copy-start.1 = (bf16[512,512]{1,0:T(8,128)(2,1)}, bf16[512,512]{1,0:T(8,128)(2,1)S(1)}, u32[]{:S(2)}) copy-start(bf16[512,512]{1,0:T(8,128)(2,1)S(1)} %collective-permute-done.17.up) | copy-start | bytes 1572868
  151.4 1.4 copy-start.2
  151.4 3.4 %copy-start = (bf16[512,512]{1,0:T(8,128)(2,1)S(1)}, bf16[512,512]{1,0:T(8,128)(2,1)}, u32[]{:S(2)}) copy-start(bf16[512,512]{1,0:T(8,128)(2,1)} %decode.1.local) | copy-start | bytes 1572868
  152.9 29.4 %collective-permute-start.20 = (bf16[3,512,512]{2,1,0:T(8,128)(2,1)S(1)}, bf16[3,512,512]{2,1,0:T(8,128)(2,1)S(1)}, u32[]{:S(2)}, u32[]{:S(2)}) collective-permute-start(bf16[3,512,512]{2,1,0:T(8,128)(2,1)S(1)} %pad_maximum_fusion), channel_id=1, source_target_pairs={{0,4},{4,0},{8,12},{12,8},{16,20},{20,16},{24,28},{28,24},{32,36},... | collective-permute-start | bytes 4718600 | tf_op jit(solution)/shard_map/ppermute | solution.py:43
  154.8 27.5 %collective-permute-start.19 = (bf16[512,512]{1,0:T(8,128)(2,1)S(1)}, bf16[512,512]{1,0:T(8,128)(2,1)S(1)}, u32[]{:S(2)}, u32[]{:S(2)}) collective-permute-start(bf16[512,512]{1,0:T(8,128)(2,1)S(1)} %copy-done), channel_id=1, source_target_pairs={{0,500},{4,16},{8,508},{12,24},{16,4},{20,32},{24,12},{28,40},{32,... | collective-permute-start | bytes 1572872 | tf_op jit(solution)/shard_map/ppermute | solution.py:43
  182.3 0.8 copy-start.7
  182.3 1.4 copy-start.3
Sparse Core Ops, SparseCore 0:
  9.5 38.4 all-gather.1

commit v2 on v1

v2 whole, which is shorter than its diff:
```python
import functools

import jax
import jax.numpy as jnp
from jax import lax
from jax.experimental import pallas as pl
from jax.experimental.pallas import tpu as pltpu
from jax.sharding import PartitionSpec as P

BF16 = jnp.bfloat16
F32 = jnp.float32
SENT = 240
WIDE = 256
SPLIT = 128
FAR = ((16, 1, 2, None), (-16, -1, -2, None), (8, 4, 32, 64), (-8, -4, -32, None))
VMEM = pltpu.CompilerParams(vmem_limit_bytes=56 * 1024 * 1024)


def silu(v):
    h = 0.5 * v
    return h + h * jnp.tanh(h)


def mul(a, b):
    return jnp.dot(a, b, preferred_element_type=F32)


def mul_nt(a, b):
    return lax.dot_general(a, b, (((1,), (1,)), ((), ())), preferred_element_type=F32)


def mul_tn(a, b):
    return lax.dot_general(a, b, (((0,), (0,)), ((), ())), preferred_element_type=F32)


def shifted(value, steps):
    count = lax.axis_size("patch")
    return lax.ppermute(value, "patch", [(i, (i + steps) % count) for i in range(count)])


def by_core(value, even_steps, odd_steps):
    count = lax.axis_size("patch")
    pairs = [(i, (i + (even_steps if i % 2 == 0 else odd_steps)) % count) for i in range(count)]
    return lax.ppermute(value, "patch", pairs)


def silu_rows(weights, block):
    return silu(mul(weights, block)).astype(BF16)


def one_hot(where, ids):
    return jnp.where(where == ids, 1.0, 0.0).astype(BF16)


def pack_body(core, x, pack, up, down, three, own, padded):
    here = core[0]
    channels, rows = x.shape
    slots = pack.shape[-1]
    padded[...] = jnp.zeros_like(padded)
    padded[0:channels, :] = x[...]
    row_of = lax.broadcasted_iota(jnp.int32, (rows, slots), 0)

    def chosen(offset):
        return mul(padded[...], one_hot(row_of, pack[offset])).astype(BF16)

    up[0] = chosen(5)
    up[1] = chosen(jnp.where(here == 0, 6, 4))
    down[0] = chosen(1)
    down[1] = chosen(jnp.where(here == 0, 2, 0))
    three[...] = chosen(jnp.where(here == 0, 0, 6))
    own[...] = chosen(jnp.where(here == 0, 4, 2))


def weights_body(core, embed, edge, proc, dec, out, padded):
    width = out.shape[0]
    eye = one_hot(
        lax.broadcasted_iota(jnp.int32, (width, width), 0),
        lax.broadcasted_iota(jnp.int32, (width, width), 1),
    )

    def turn(piece, at):
        out[:, at : at + piece.shape[0]] = mul_nt(eye, piece).astype(BF16)

    @pl.when(core[0] == 0)
    def _():
        padded[...] = jnp.zeros_like(padded)
        padded[0 : embed.shape[0], :] = embed[...]
        turn(padded[...], 0)
        turn(edge[...], WIDE)
        turn(proc[0:SPLIT, :], WIDE + edge.shape[0])

    @pl.when(core[0] != 0)
    def _():
        turn(proc[SPLIT:, :], 0)
        turn(dec[...], proc.shape[0] - SPLIT)


def prepare_body(core, x, mine, other, edges, latent, table, padded):
    is_even = core[0] == 0
    channels, rows = x.shape
    padded[...] = jnp.zeros_like(padded)
    padded[0:channels, :] = x[...]
    w_embed = jnp.where(is_even, mine[:, 0:WIDE], other[:, 0:WIDE])
    latent[...] = silu(
        lax.dot_general(
            padded[...], w_embed, (((0,), (1,)), ((), ())), preferred_element_type=F32
        )
    ).astype(BF16)
    nodes = table.shape[1] // 3
    late = (jnp.where(is_even, 2, 0), jnp.where(is_even, 6, 4), jnp.where(is_even, 0, 6))
    for i, offset in enumerate(late):
        table[:, i * nodes : (i + 1) * nodes] = edge_table(edges, offset, nodes)


def edge_table(edges, offset, nodes):
    count, rows = edges.shape
    spare = jnp.zeros((8 - count, rows), jnp.int32)
    ids = jnp.concatenate([edges[...] - offset * nodes, spare], axis=0).T
    where = lax.broadcasted_iota(jnp.int32, (rows, nodes), 1)
    total = jnp.where(where == ids[:, 0:1], 1.0, 0.0)
    for k in range(1, count):
        total += jnp.where(where == ids[:, k : k + 1], 1.0, 0.0)
    return total.astype(BF16)


def messages(block, w_embed, w_edge):
    return silu_rows(w_edge, silu_rows(w_embed, block))


def early_body(core, x, pack, up, down, three, mine, other, recv, embed, out, padded):
    is_even = core[0] == 0
    nodes, channels = embed.shape
    slots = recv.shape[-1]
    w_embed = jnp.where(is_even, mine[:, 0:SENT], other[:, 0:SENT])
    w_edge = jnp.where(is_even, mine[:, WIDE : WIDE + channels], other[:, WIDE : WIDE + channels])
    padded[...] = jnp.zeros_like(padded)
    padded[0 : x.shape[0], :] = x[...]
    row_of = lax.broadcasted_iota(jnp.int32, (x.shape[1], slots), 0)
    local = mul(padded[...], one_hot(row_of, pack[3])).astype(BF16)
    node_of = lax.broadcasted_iota(jnp.int32, (nodes, slots), 0)
    total = embed[...].astype(F32)
    blocks = (
        (local, 3),
        (up[0], 5),
        (down[0], 1),
        (three[...], jnp.where(is_even, 6, 0)),
    )
    for block, offset in blocks:
        total += mul_nt(one_hot(node_of, recv[offset]), messages(block, w_embed, w_edge))
    out[...] = total


def encode_body(core, here, early, sib, mine, other, recv, far_ids, latent, message, far):
    is_even = core[0] == 0
    nodes, channels = early.shape
    slots = recv.shape[-1]
    w_embed = jnp.where(is_even, mine[:, 0:SENT], other[:, 0:SENT])
    w_edge = jnp.where(is_even, mine[:, WIDE : WIDE + channels], other[:, WIDE : WIDE + channels])
    first = WIDE + channels
    low = jnp.where(is_even, mine[:, first : first + SPLIT], other[:, first : first + SPLIT])
    rest = channels - SPLIT
    high = jnp.where(is_even, other[:, 0:rest], mine[:, 0:rest])
    w_proc = jnp.concatenate([low, high], axis=1)
    node_of = lax.broadcasted_iota(jnp.int32, (nodes, slots), 0)
    total = early[...]
    offsets = (jnp.where(is_even, 2, 4), jnp.where(is_even, 4, 6), jnp.where(is_even, 0, 2))
    for i, offset in enumerate(offsets):
        total += mul_nt(one_hot(node_of, recv[offset]), messages(sib[i], w_embed, w_edge))
    rounded = total.astype(BF16)
    latent[...] = rounded
    sent = silu(mul_nt(rounded, w_proc)).astype(BF16)
    message[...] = sent
    far[...] = mul(far_table(far_ids, here[0], 1, nodes), sent).astype(BF16)


def far_table(ids, here, sign, nodes):
    count = ids.shape[1]
    column = lax.broadcasted_iota(jnp.int32, ids.shape, 1)
    node = lax.broadcasted_iota(jnp.int32, (ids.shape[0], nodes), 1)
    pieces = []
    for offset in sum(FAR, ()):
        if offset is None:
            pieces.append(jnp.zeros((ids.shape[0], nodes), F32))
            continue
        partner = lax.rem(here + sign * offset + count, count)
        chosen = jnp.sum(jnp.where(column == partner, ids[...], 0), axis=1, keepdims=True)
        pieces.append(jnp.where(node == chosen, 1.0, 0.0))
    return jnp.concatenate(pieces, axis=0).astype(BF16)


def local_body(latent, message, neighbours, out):
    nodes = latent.shape[0]
    count = neighbours.shape[0]
    spare = jnp.zeros((8 - count, nodes), jnp.int32)
    ids = jnp.concatenate([neighbours[...], spare], axis=0).T
    node = lax.broadcasted_iota(jnp.int32, (nodes, nodes), 1)
    table = jnp.where(node == ids[:, 0:1], 1.0, 0.0)
    for k in range(1, count):
        table += jnp.where(node == ids[:, k : k + 1], 1.0, 0.0)
    out[...] = latent[...].astype(F32) + mul(table.astype(BF16), message[...])


def decode_body(core, here, base, far_ids, arrived, mine, other, out):
    nodes, channels = base.shape
    at = channels - SPLIT
    w_dec = jnp.where(core[0] == 0, other[:, at : at + channels], mine[:, at : at + channels])
    hot = far_table(far_ids, here[0], -1, nodes)
    after = (base[...] + mul_tn(hot, arrived[...])).astype(BF16)
    out[...] = silu(mul_nt(after, w_dec)).astype(BF16)


def near_body(core, latent, edges, local, sib, up, down, out):
    is_even = core[0] == 0
    nodes = local.shape[0]
    total = latent[...].astype(F32)
    blocks = ((local, 3), (sib, jnp.where(is_even, 4, 2)), (up, 1), (down, 5))
    for block, offset in blocks:
        total += mul(edge_table(edges, offset, nodes), block[...])
    out[...] = total


def collect_body(near, table, relay, three, out):
    nodes = three.shape[0]
    total = near[...]
    for i, block in enumerate((relay[0], relay[1], three[...])):
        total += mul(table[:, i * nodes : (i + 1) * nodes], block)
    out[...] = total.astype(BF16)


def call(body, out_shape, args, scratch=(), name=None):
    smem = pl.BlockSpec(memory_space=pltpu.SMEM)
    vmem = pl.BlockSpec(memory_space=pltpu.VMEM)
    specs = [smem if a.ndim == 1 else vmem for a in args]
    many = isinstance(out_shape, (list, tuple))
    return pl.pallas_call(
        body,
        out_shape=out_shape,
        in_specs=specs,
        out_specs=[vmem for _ in out_shape] if many else vmem,
        scratch_shapes=scratch,
        compiler_params=VMEM,
        name=name,
    )(*args)


def shape(*dims, kind=BF16):
    return jax.ShapeDtypeStruct(dims, kind)


def far_exchange(rows):
    patches, chans = lax.axis_size("patch"), lax.axis_size("chan")
    kinds = len(FAR[0])
    count, channels = rows.shape
    each = count // (chans * kinds)
    mine = lax.all_to_all(
        rows.reshape(chans, kinds * each, channels), "chan", 0, 0, tiled=True
    ).reshape(chans, kinds, each, channels)
    arrived = []
    for kind in range(kinds):
        pairs = []
        for c in range(chans):
            if FAR[c][kind] is None:
                continue
            for p in range(patches):
                pairs.append((p * chans + c, (p + FAR[c][kind]) % patches * chans + c))
        arrived.append(lax.ppermute(mine[:, kind], ("patch", "chan"), pairs))
    back = jnp.stack(arrived, axis=1).reshape(chans, kinds * each, channels)
    return lax.all_to_all(back, "chan", 0, 0, tiled=True).reshape(count, channels)


def shards(
    grid_in,
    mesh_embed,
    w_embed,
    w_edge,
    w_proc,
    w_dec,
    pack_rows,
    recv_node,
    far_send,
    far_recv,
    loc_nbr,
    dec_edge,
):
    patch = lax.axis_index("patch").astype(jnp.int32)
    here = patch.reshape(1)
    core = (patch % 2).reshape(1)
    channels = mesh_embed.shape[1]
    nodes = mesh_embed.shape[0]
    rows = grid_in.shape[0]
    offsets, slots = pack_rows.shape[2:]
    x = grid_in.T
    pack = pack_rows.reshape(offsets, 1, slots)
    recv = recv_node.reshape(offsets, 1, slots)
    far_out_ids = far_send.reshape(far_send.shape[2:]).T
    far_in_ids = far_recv.reshape(far_recv.shape[2:]).T
    block = shape(SENT, slots)
    pair = shape(2, SENT, slots)
    padded = pltpu.VMEM((SENT, rows), BF16)

    up, down, three, own = call(
        pack_body, [pair, pair, block, block], (core, x, pack), [padded], name="pack"
    )
    up, down, three, own, w_embed, w_edge, w_proc, w_dec = lax.optimization_barrier(
        (up, down, three, own, w_embed, w_edge, w_proc, w_dec)
    )
    three = by_core(three, -3, 3)
    up = shifted(up, 2)
    down = shifted(down, -2)
    shard = call(
        weights_body,
        shape(w_edge.shape[1], (WIDE + 3 * channels) // 2),
        (core, w_embed, w_edge, w_proc, w_dec),
        [pltpu.VMEM((WIDE, w_edge.shape[1]), BF16)],
        name="weights",
    )
    mine = lax.all_gather(shard, "chan", axis=0, tiled=True)
    mine, up, down, three = lax.optimization_barrier((mine, up, down, three))
    sib = by_core(jnp.stack([own, up[1], down[1]]), 1, -1)
    other = by_core(mine, 1, -1)
    early = call(
        early_body,
        shape(nodes, channels, kind=F32),
        (core, x, pack, up, down, three, mine, other, recv, mesh_embed),
        [padded],
        name="early",
    )
    mesh_latent, node_msg, far_sent = call(
        encode_body,
        [shape(nodes, channels), shape(nodes, channels), shape(8 * 16, channels)],
        (core, here, early, sib, mine, other, recv, far_out_ids),
        name="encode",
    )
    arrived = far_exchange(far_sent)
    base = call(
        local_body,
        shape(nodes, channels, kind=F32),
        (mesh_latent, node_msg, loc_nbr.T),
        name="short",
    )
    dec_msg = call(
        decode_body,
        shape(nodes, channels),
        (core, here, base, far_in_ids, arrived, mine, other),
        name="decode",
    )
    up = shifted(dec_msg, 2)
    down = shifted(dec_msg, -2)
    sib = by_core(dec_msg, 1, -1)
    latent, table = call(
        prepare_body,
        [shape(rows, channels), shape(rows, 3 * nodes)],
        (core, x, mine, other, dec_edge.T),
        [pltpu.VMEM((WIDE, rows), BF16)],
        name="prepare",
    )
    up, down, sib, latent, table = lax.optimization_barrier((up, down, sib, latent, table))
    three = by_core(jnp.where(core[0] == 0, down, up), -1, 1)
    relay = by_core(jnp.stack([up, down]), 1, -1)
    near = call(
        near_body,
        shape(rows, channels, kind=F32),
        (core, latent, dec_edge.T, dec_msg, sib, up, down),
        name="near",
    )
    return call(
        collect_body,
        shape(rows, channels),
        (near, table, relay, three),
        name="collect",
    )


def solution(mesh):
    both = P(("patch", "chan"), None)
    column = P(None, "chan")
    lists = P("patch", "chan", None, None)
    in_specs = (both, both, column, column, column, column, lists, lists, lists, lists, both, both)
    return jax.shard_map(shards, mesh=mesh, in_specs=in_specs, out_specs=both, check_vma=False)
```

time: 201 us -> 149 us (0.74)
  the two profiles are of different devices: /device:TPU:56 before, /device:TPU:8 now
where the time goes in v2:
time: 149 us; the launch traced here: 148 us
  starting transfers between devices  56.5 us (38%)
  Pallas kernels  44.8 us (30%)
  blocking collectives  23.5 us (16%)
  waiting for transfers between devices  17.1 us (11%)
  local copies, waits for them, and re-layouts  4.25 us (3%)
  other arithmetic  1.82 us (1%)
    pallas_call x9, Pallas kernels, call(): pl.pallas_call(body, out_shape=out_shape, in_specs=specs, out_specs=[vmem...  44.8 us
    ppermute x4, starting transfers between devices, shifted(): lax.ppermute(value, 'patch', [(i, (i + steps) % count) for i in range(cou...  21.5 us
    all_gather x1, blocking collectives, shards(): mine = lax.all_gather(shard, 'chan', axis=0, tiled=True)  14.5 us
    ppermute x4, starting transfers between devices, far_exchange(): arrived.append(lax.ppermute(mine[:, kind], ('patch', 'chan'), pairs))  13.5 us
    ppermute x6, starting transfers between devices, by_core(): return lax.ppermute(value, 'patch', pairs)  13.3 us
    ppermute x4, waiting for transfers between devices, shifted(): lax.ppermute(value, 'patch', [(i, (i + steps) % count) for i in range(cou...  10.5 us
    all_to_all x1, blocking collectives, far_exchange(): lax.all_to_all(rows.reshape(chans, kinds * each, channels), 'chan', 0, 0,...  9.02 us
    all_to_all x1, starting transfers between devices, far_exchange(): lax.all_to_all(back, 'chan', 0, 0, tiled=True).reshape(count, channels)  8.11 us
  transfers between devices with their start and end apart: 15, of which 6 were waited for; matrix products, arithmetic and copies ran while one was open for 1% of the time, Pallas kernels for 18%

profile of v2, /device:TPU:8, one launch (start us, length us, event | category | flops | bytes accessed | tf_op | source)
XLA Modules:
  0.0 148.2 jit_solution(5820020486385505265)
XLA Ops:
  0.0 3.4 %pack.1 = (bf16[2,240,384]{2,1,0:T(8,128)(2,1)}, bf16[2,240,384]{2,1,0:T(8,128)(2,1)}, bf16[240,384]{1,0:T(8,128)(2,1)}, bf16[240,384]{1,0:T(8,128)(2,1)}) custom-call(s32[1]{0:T(128)} %bitcast.core, bf16[227,1024]{1,0:T(8,128)(2,1)} %bitcast.43, s32[7,1,384]{2,1,0:T(1,128)} %bitcast.54), custom_call_target="tpu_custom_call" | custom-call | tf_op jit(solution)/shard_map/pack/pallas_call | solution.py:235
  3.4 3.8 %collective-permute-start = (bf16[2,240,384]{2,1,0:T(8,128)(2,1)}, bf16[2,240,384]{2,1,0:T(8,128)(2,1)S(1)}, u32[]{:S(2)}, u32[]{:S(2)}) collective-permute-start(bf16[2,240,384]{2,1,0:T(8,128)(2,1)} %get-tuple-element.39), channel_id=1, source_target_pairs={{0,8},{4,12},{8,16},{12,20},{16,24},{20,28},{24,32},{28,36},{32,40... | collective-permute-start | bytes 1105928 | tf_op jit(solution)/shard_map/ppermute | solution.py:38
  7.3 11.7 %collective-permute-start.1 = (bf16[2,240,384]{2,1,0:T(8,128)(2,1)}, bf16[2,240,384]{2,1,0:T(8,128)(2,1)S(1)}, u32[]{:S(2)}, u32[]{:S(2)}) collective-permute-start(bf16[2,240,384]{2,1,0:T(8,128)(2,1)} %get-tuple-element.40), channel_id=1, source_target_pairs={{0,504},{4,508},{8,0},{12,4},{16,8},{20,12},{24,16},{28,20},{32,24... | collective-permute-start | bytes 1105928 | tf_op jit(solution)/shard_map/ppermute | solution.py:38
  19.0 3.2 %collective-permute-start.2 = (bf16[240,384]{1,0:T(8,128)(2,1)}, bf16[240,384]{1,0:T(8,128)(2,1)S(1)}, u32[]{:S(2)}, u32[]{:S(2)}) collective-permute-start(bf16[240,384]{1,0:T(8,128)(2,1)} %get-tuple-element.41), channel_id=1, source_target_pairs={{0,500},{4,16},{8,508},{12,24},{16,4},{20,32},{24,12},{28,40},{32,... | collective-permute-start | bytes 552968 | tf_op jit(solution)/shard_map/ppermute | solution.py:44
  22.2 2.0 %weights.1 = bf16[128,896]{1,0:T(8,128)(2,1)} custom-call(s32[1]{0:T(128)} %bitcast.core, bf16[227,128]{1,0:T(8,128)(2,1)} %embed.1, bf16[512,128]{1,0:T(8,128)(2,1)} %edge, bf16[512,128]{1,0:T(8,128)(2,1)} %proc, bf16[512,128]{1,0:T(8,128)(2,1)} %dec), custom_call_target="tpu_custom_call" | custom-call | tf_op jit(solution)/shard_map/weights/pallas_call | solution.py:235
  24.2 14.5 %all_gather.3.mine = bf16[512,896]{1,0:T(8,128)(2,1)S(1)} all-gather(bf16[128,896]{1,0:T(8,128)(2,1)} %weights.1), channel_id=1, replica_groups=mesh['patch'=128,'chan'=4] {'chan'}, dimensions={0}, use_global_device_ids=true | all-gather | bytes 1146880 | tf_op jit(solution)/shard_map/all_gather | solution.py:317
  38.7 0.0 copy-start
  38.7 0.0 collective-permute-done.2.three
  38.7 0.0 copy-start.11
  38.7 0.0 collective-permute-done.up
  38.7 0.0 copy-start.5
  38.8 0.0 collective-permute-done.1.down
  38.8 0.0 copy-start.6
  38.8 1.9 %collective-permute-start.3 = (bf16[512,896]{1,0:T(8,128)(2,1)S(1)}, bf16[512,896]{1,0:T(8,128)(2,1)S(1)}, u32[]{:S(2)}, u32[]{:S(2)}) collective-permute-start(bf16[512,896]{1,0:T(8,128)(2,1)S(1)} %all_gather.3.mine), channel_id=1, source_target_pairs={{0,4},{4,0},{8,12},{12,8},{16,20},{20,16},{24,28},{28,24},{32,36},... | collective-permute-start | bytes 2752520 | tf_op jit(solution)/shard_map/ppermute | solution.py:44
  40.8 1.0 pad_maximum_fusion.1
  41.8 2.4 %collective-permute-start.4 = (bf16[3,240,384]{2,1,0:T(8,128)(2,1)S(1)}, bf16[3,240,384]{2,1,0:T(8,128)(2,1)S(1)}, u32[]{:S(2)}, u32[]{:S(2)}) collective-permute-start(bf16[3,240,384]{2,1,0:T(8,128)(2,1)S(1)} %pad_maximum_fusion.1), channel_id=1, source_target_pairs={{0,4},{4,0},{8,12},{12,8},{16,20},{20,16},{24,28},{28,24},{32,36},... | collective-permute-start | bytes 1658888 | tf_op jit(solution)/shard_map/ppermute | solution.py:44
  44.2 0.0 collective-permute-done.3.other
  44.2 0.0 copy-start.1
  44.2 0.0 copy-done
  44.2 0.0 copy-done.11
  44.2 0.0 copy-done.5
  44.2 0.0 copy-done.6
  44.2 0.9 copy-done.1
  45.1 7.1 %early.1 = f32[512,512]{1,0:T(8,128)} custom-call(s32[1]{0:T(128)} %bitcast.core, bf16[227,1024]{1,0:T(8,128)(2,1)} %bitcast.44, s32[7,1,384]{2,1,0:T(1,128)} %bitcast.55, bf16[2,240,384]{2,1,0:T(8,128)(2,1)} %copy-done.5, bf16[2,240,384]{2,1,0:T(8,128)(2,1)} %copy-done.6, bf16[240,384]{1,0:T(8,128)(2,1)} %copy-done.11, bf16[512,896]{1,0:T(8,128)(2,1)} %copy-done, ...), custom_call_target="tpu_custom_call" | custom-call | tf_op jit(solution)/shard_map/early/pallas_call | solution.py:235
  52.2 0.0 collective-permute-done.4.sib
  52.2 0.0 copy-start.7
  52.2 0.8 copy-done.7
  53.0 6.0 %encode.1 = (bf16[512,512]{1,0:T(8,128)(2,1)}, bf16[512,512]{1,0:T(8,128)(2,1)}, bf16[128,512]{1,0:T(8,128)(2,1)}) custom-call(s32[1]{0:T(128)} %bitcast.core, s32[1]{0:T(128)} %bitcast.1.here, f32[512,512]{1,0:T(8,128)} %early.1, bf16[3,240,384]{2,1,0:T(8,128)(2,1)} %copy-done.7, bf16[512,896]{1,0:T(8,128)(2,1)} %copy-done, bf16[512,896]{1,0:T(8,128)(2,1)} %copy-done.1, ...), custom_call_target="tpu_custom_call" | custom-call | tf_op jit(solution)/shard_map/encode/pallas_call | solution.py:235
  59.0 9.0 %all_to_all.10 = bf16[4,32,512]{2,1,0:T(8,128)(2,1)S(1)} all-to-all(bf16[4,32,512]{2,1,0:T(8,128)(2,1)} %bitcast.49), channel_id=1, replica_groups=mesh['patch'=128,'chan'=4] {'chan'}, dimensions={0} | all-to-all | bytes 262144 | tf_op jit(solution)/shard_map/all_to_all | solution.py:255
  68.0 8.9 %collective-permute-start.5 = (bf16[4,8,512]{2,1,0:T(8,128)(2,1)S(1)}, bf16[4,8,512]{2,1,0:T(8,128)(2,1)S(1)}, u32[]{:S(2)}, u32[]{:S(2)}) collective-permute-start(bf16[4,8,512]{2,1,0:T(8,128)(2,1)S(1)} %get-tuple-element.57), channel_id=1, source_target_pairs={{0,64},{4,68},{8,72},{12,76},{16,80},{20,84},{24,88},{28,92},{32,9... | collective-permute-start | bytes 98312 | tf_op jit(solution)/shard_map/ppermute | solution.py:266
  76.9 1.9 %collective-permute-start.7 = (bf16[4,8,512]{2,1,0:T(8,128)(2,1)S(1)}, bf16[4,8,512]{2,1,0:T(8,128)(2,1)S(1)}, u32[]{:S(2)}, u32[]{:S(2)}) collective-permute-start(bf16[4,8,512]{2,1,0:T(8,128)(2,1)S(1)} %get-tuple-element.58), channel_id=1, source_target_pairs={{0,8},{4,12},{8,16},{12,20},{16,24},{20,28},{24,32},{28,36},{32,40... | collective-permute-start | bytes 98312 | tf_op jit(solution)/shard_map/ppermute | solution.py:266
  78.9 2.1 %collective-permute-start.6 = (bf16[4,8,512]{2,1,0:T(8,128)(2,1)S(1)}, bf16[4,8,512]{2,1,0:T(8,128)(2,1)S(1)}, u32[]{:S(2)}, u32[]{:S(2)}) collective-permute-start(bf16[4,8,512]{2,1,0:T(8,128)(2,1)S(1)} %get-tuple-element.59), channel_id=1, source_target_pairs={{0,4},{4,8},{8,12},{12,16},{16,20},{20,24},{24,28},{28,32},{32,36}... | collective-permute-start | bytes 98312 | tf_op jit(solution)/shard_map/ppermute | solution.py:266
  80.9 0.7 collective-permute-start.8
  81.6 1.0 collective-permute-done.5
  82.6 0.2 collective-permute-done.7
  82.7 0.0 collective-permute-done.6
  82.8 0.0 collective-permute-done.8
  82.8 0.7 maximum_bitcast_fusion
  83.4 8.1 %all-to-all-start.1 = ((bf16[4,32,512]{2,1,0:T(8,128)(2,1)}), bf16[4,32,512]{2,1,0:T(8,128)(2,1)S(1)}, u32[]{:S(2)}, u32[]{:S(2)}) async-start(bf16[4,32,512]{2,1,0:T(8,128)(2,1)} %maximum_bitcast_fusion), calls=%async_computation.1 | async-start | bytes 262144 | tf_op jit(solution)/shard_map/all_to_all | solution.py:268
  91.5 3.4 %short.1.base = f32[512,512]{1,0:T(8,128)} custom-call(bf16[512,512]{1,0:T(8,128)(2,1)} %get-tuple-element.47.latent, bf16[512,512]{1,0:T(8,128)(2,1)} %get-tuple-element.48.message, s32[6,512]{1,0:T(8,128)} %bitcast.60), custom_call_target="tpu_custom_call" | custom-call | tf_op jit(solution)/shard_map/short/pallas_call | solution.py:235
  94.9 1.2 all-to-all-done.1
  96.1 0.7 copy-done.8
  96.7 3.4 %decode.1.local = bf16[512,512]{1,0:T(8,128)(2,1)} custom-call(s32[1]{0:T(128)} %bitcast.core, s32[1]{0:T(128)} %bitcast.1.here, f32[512,512]{1,0:T(8,128)} %short.1.base, s32[8,128]{1,0:T(8,128)} %bitcast.62, bf16[128,512]{1,0:T(8,128)(2,1)} %bitcast.46, bf16[512,896]{1,0:T(8,128)(2,1)} %copy-done, bf16[512,896]{1,0:T(8,128)(2,1)} %copy-done.1), custom_call_target="tpu_custom_call" | custom-call | tf_op jit(solution)/shard_map/decode/pallas_call | solution.py:235
  100.1 1.9 %collective-permute-start.11 = (bf16[512,512]{1,0:T(8,128)(2,1)}, bf16[512,512]{1,0:T(8,128)(2,1)S(1)}, u32[]{:S(2)}, u32[]{:S(2)}) collective-permute-start(bf16[512,512]{1,0:T(8,128)(2,1)} %decode.1.local), channel_id=1, source_target_pairs={{0,4},{4,0},{8,12},{12,8},{16,20},{20,16},{24,28},{28,24},{32,36},... | collective-permute-start | bytes 1572872 | tf_op jit(solution)/shard_map/ppermute | solution.py:44
  102.0 3.3 %collective-permute-start.10 = (bf16[512,512]{1,0:T(8,128)(2,1)}, bf16[512,512]{1,0:T(8,128)(2,1)S(1)}, u32[]{:S(2)}, u32[]{:S(2)}) collective-permute-start(bf16[512,512]{1,0:T(8,128)(2,1)} %decode.1.local), channel_id=1, source_target_pairs={{0,504},{4,508},{8,0},{12,4},{16,8},{20,12},{24,16},{28,20},{32,24... | collective-permute-start | bytes 1572872 | tf_op jit(solution)/shard_map/ppermute | solution.py:38
  105.3 2.7 %collective-permute-start.9 = (bf16[512,512]{1,0:T(8,128)(2,1)}, bf16[512,512]{1,0:T(8,128)(2,1)S(1)}, u32[]{:S(2)}, u32[]{:S(2)}) collective-permute-start(bf16[512,512]{1,0:T(8,128)(2,1)} %decode.1.local), channel_id=1, source_target_pairs={{0,8},{4,12},{8,16},{12,20},{16,24},{20,28},{24,32},{28,36},{32,40... | collective-permute-start | bytes 1572872 | tf_op jit(solution)/shard_map/ppermute | solution.py:38
  108.0 6.3 %prepare.1 = (bf16[1024,512]{1,0:T(8,128)(2,1)}, bf16[1024,1536]{1,0:T(8,128)(2,1)}) custom-call(s32[1]{0:T(128)} %bitcast.core, bf16[227,1024]{1,0:T(8,128)(2,1)} %bitcast.45, bf16[512,896]{1,0:T(8,128)(2,1)} %copy-done, bf16[512,896]{1,0:T(8,128)(2,1)} %copy-done.1, s32[3,1024]{1,0:T(4,128)} %bitcast.50), custom_call_target="tpu_custom_call" | custom-call | tf_op jit(solution)/shard_map/prepare/pallas_call | solution.py:235
  114.3 0.0 collective-permute-done.11.sib
  114.3 0.0 copy-start.9
  114.3 4.1 %collective-permute-done.10.down = bf16[512,512]{1,0:T(8,128)(2,1)S(1)} collective-permute-done((bf16[512,512]{1,0:T(8,128)(2,1)}, bf16[512,512]{1,0:T(8,128)(2,1)S(1)}, u32[]{:S(2)}, u32[]{:S(2)}) %collective-permute-start.10) | collective-permute-done | bytes 524320 | tf_op jit(solution)/shard_map/ppermute | solution.py:38
  118.4 6.4 %collective-permute-done.9.up = bf16[512,512]{1,0:T(8,128)(2,1)S(1)} collective-permute-done((bf16[512,512]{1,0:T(8,128)(2,1)}, bf16[512,512]{1,0:T(8,128)(2,1)S(1)}, u32[]{:S(2)}, u32[]{:S(2)}) %collective-permute-start.9) | collective-permute-done | bytes 524320 | tf_op jit(solution)/shard_map/ppermute | solution.py:38
  124.8 0.0 copy-done.9
  124.8 0.1 pad_maximum_fusion
  124.9 1.9 %collective-permute-start.12 = (bf16[2,512,512]{2,1,0:T(8,128)(2,1)S(1)}, bf16[2,512,512]{2,1,0:T(8,128)(2,1)S(1)}, u32[]{:S(2)}, u32[]{:S(2)}) collective-permute-start(bf16[2,512,512]{2,1,0:T(8,128)(2,1)S(1)} %pad_maximum_fusion), channel_id=1, source_target_pairs={{0,4},{4,0},{8,12},{12,8},{16,20},{20,16},{24,28},{28,24},{32,36},... | collective-permute-start | bytes 3145736 | tf_op jit(solution)/shard_map/ppermute | solution.py:44
  126.9 0.1 broadcast_select_fusion
  126.9 1.9 %collective-permute-start.13 = (bf16[512,512]{1,0:T(8,128)(2,1)S(1)}, bf16[512,512]{1,0:T(8,128)(2,1)S(1)}, u32[]{:S(2)}, u32[]{:S(2)}) collective-permute-start(bf16[512,512]{1,0:T(8,128)(2,1)S(1)} %broadcast_select_fusion), channel_id=1, source_target_pairs={{0,508},{4,8},{8,4},{12,16},{16,12},{20,24},{24,20},{28,32},{32,28... | collective-permute-start | bytes 1572872 | tf_op jit(solution)/shard_map/ppermute | solution.py:44
  128.9 0.0 copy-done.2
  128.9 0.0 copy-done.3
  128.9 7.6 %near.1 = f32[1024,512]{1,0:T(8,128)} custom-call(s32[1]{0:T(128)} %bitcast.core, bf16[1024,512]{1,0:T(8,128)(2,1)} %get-tuple-element.52.latent, s32[3,1024]{1,0:T(4,128)} %bitcast.51, bf16[512,512]{1,0:T(8,128)(2,1)} %decode.1.local, bf16[512,512]{1,0:T(8,128)(2,1)} %copy-done.9, bf16[512,512]{1,0:T(8,128)(2,1)} %copy-done.3, bf16[512,512]{1,0:T(8,128)(2,1)} %copy-done.2), custom_call_target="tpu_custom_call" | custom-call | tf_op jit(solution)/shard_map/near/pallas_call | solution.py:235
  136.4 4.3 %collective-permute-done.13.three = bf16[512,512]{1,0:T(8,128)(2,1)S(1)} collective-permute-done((bf16[512,512]{1,0:T(8,128)(2,1)S(1)}, bf16[512,512]{1,0:T(8,128)(2,1)S(1)}, u32[]{:S(2)}, u32[]{:S(2)}) %collective-permute-start.13) | collective-permute-done | bytes 524320 | tf_op jit(solution)/shard_map/ppermute | solution.py:44
  140.7 0.0 collective-permute-done.12.relay
  140.8 0.8 copy-done.10
  141.6 1.0 copy-done.4
  142.6 5.7 %collect.1 = bf16[1024,512]{1,0:T(8,128)(2,1)} custom-call(f32[1024,512]{1,0:T(8,128)} %near.1, bf16[1024,1536]{1,0:T(8,128)(2,1)} %get-tuple-element.56.table, bf16[2,512,512]{2,1,0:T(8,128)(2,1)} %copy-done.4, bf16[512,512]{1,0:T(8,128)(2,1)} %copy-done.10), custom_call_target="tpu_custom_call" | custom-call | tf_op jit(solution)/shard_map/collect/pallas_call | solution.py:235
  (8 shorter events, 0.1 us)
Async XLA Ops:
  3.4 35.3 %collective-permute-start = (bf16[2,240,384]{2,1,0:T(8,128)(2,1)}, bf16[2,240,384]{2,1,0:T(8,128)(2,1)S(1)}, u32[]{:S(2)}, u32[]{:S(2)}) collective-permute-start(bf16[2,240,384]{2,1,0:T(8,128)(2,1)} %get-tuple-element.39), channel_id=1, source_target_pairs={{0,8},{4,12},{8,16},{12,20},{16,24},{20,28},{24,32},{28,36},{32,40... | collective-permute-start | bytes 1105928 | tf_op jit(solution)/shard_map/ppermute | solution.py:38
  7.3 31.5 %collective-permute-start.1 = (bf16[2,240,384]{2,1,0:T(8,128)(2,1)}, bf16[2,240,384]{2,1,0:T(8,128)(2,1)S(1)}, u32[]{:S(2)}, u32[]{:S(2)}) collective-permute-start(bf16[2,240,384]{2,1,0:T(8,128)(2,1)} %get-tuple-element.40), channel_id=1, source_target_pairs={{0,504},{4,508},{8,0},{12,4},{16,8},{20,12},{24,16},{28,20},{32,24... | collective-permute-start | bytes 1105928 | tf_op jit(solution)/shard_map/ppermute | solution.py:38
  19.0 19.8 %collective-permute-start.2 = (bf16[240,384]{1,0:T(8,128)(2,1)}, bf16[240,384]{1,0:T(8,128)(2,1)S(1)}, u32[]{:S(2)}, u32[]{:S(2)}) collective-permute-start(bf16[240,384]{1,0:T(8,128)(2,1)} %get-tuple-element.41), channel_id=1, source_target_pairs={{0,500},{4,16},{8,508},{12,24},{16,4},{20,32},{24,12},{28,40},{32,... | collective-permute-start | bytes 552968 | tf_op jit(solution)/shard_map/ppermute | solution.py:44
  38.7 5.5 %copy-start = (bf16[512,896]{1,0:T(8,128)(2,1)}, bf16[512,896]{1,0:T(8,128)(2,1)S(1)}, u32[]{:S(2)}) copy-start(bf16[512,896]{1,0:T(8,128)(2,1)S(1)} %all_gather.3.mine) | copy-start | bytes 2752516
  38.7 5.5 %copy-start.11 = (bf16[240,384]{1,0:T(8,128)(2,1)}, bf16[240,384]{1,0:T(8,128)(2,1)S(1)}, u32[]{:S(2)}) copy-start(bf16[240,384]{1,0:T(8,128)(2,1)S(1)} %collective-permute-done.2.three) | copy-start | bytes 552964
  38.7 5.5 %copy-start.5 = (bf16[2,240,384]{2,1,0:T(8,128)(2,1)}, bf16[2,240,384]{2,1,0:T(8,128)(2,1)S(1)}, u32[]{:S(2)}) copy-start(bf16[2,240,384]{2,1,0:T(8,128)(2,1)S(1)} %collective-permute-done.up) | copy-start | bytes 1105924
  38.8 5.5 %copy-start.6 = (bf16[2,240,384]{2,1,0:T(8,128)(2,1)}, bf16[2,240,384]{2,1,0:T(8,128)(2,1)S(1)}, u32[]{:S(2)}) copy-start(bf16[2,240,384]{2,1,0:T(8,128)(2,1)S(1)} %collective-permute-done.1.down) | copy-start | bytes 1105924
  38.8 5.4 %collective-permute-start.3 = (bf16[512,896]{1,0:T(8,128)(2,1)S(1)}, bf16[512,896]{1,0:T(8,128)(2,1)S(1)}, u32[]{:S(2)}, u32[]{:S(2)}) collective-permute-start(bf16[512,896]{1,0:T(8,128)(2,1)S(1)} %all_gather.3.mine), channel_id=1, source_target_pairs={{0,4},{4,0},{8,12},{12,8},{16,20},{20,16},{24,28},{28,24},{32,36},... | collective-permute-start | bytes 2752520 | tf_op jit(solution)/shard_map/ppermute | solution.py:44
  41.8 10.5 %collective-permute-start.4 = (bf16[3,240,384]{2,1,0:T(8,128)(2,1)S(1)}, bf16[3,240,384]{2,1,0:T(8,128)(2,1)S(1)}, u32[]{:S(2)}, u32[]{:S(2)}) collective-permute-start(bf16[3,240,384]{2,1,0:T(8,128)(2,1)S(1)} %pad_maximum_fusion.1), channel_id=1, source_target_pairs={{0,4},{4,0},{8,12},{12,8},{16,20},{20,16},{24,28},{28,24},{32,36},... | collective-permute-start | bytes 1658888 | tf_op jit(solution)/shard_map/ppermute | solution.py:44
  44.2 0.9 copy-start.1
  52.2 0.8 copy-start.7
  68.0 14.5 %collective-permute-start.5 = (bf16[4,8,512]{2,1,0:T(8,128)(2,1)S(1)}, bf16[4,8,512]{2,1,0:T(8,128)(2,1)S(1)}, u32[]{:S(2)}, u32[]{:S(2)}) collective-permute-start(bf16[4,8,512]{2,1,0:T(8,128)(2,1)S(1)} %get-tuple-element.57), channel_id=1, source_target_pairs={{0,64},{4,68},{8,72},{12,76},{16,80},{20,84},{24,88},{28,92},{32,9... | collective-permute-start | bytes 98312 | tf_op jit(solution)/shard_map/ppermute | solution.py:266
  76.9 5.8 %collective-permute-start.7 = (bf16[4,8,512]{2,1,0:T(8,128)(2,1)S(1)}, bf16[4,8,512]{2,1,0:T(8,128)(2,1)S(1)}, u32[]{:S(2)}, u32[]{:S(2)}) collective-permute-start(bf16[4,8,512]{2,1,0:T(8,128)(2,1)S(1)} %get-tuple-element.58), channel_id=1, source_target_pairs={{0,8},{4,12},{8,16},{12,20},{16,24},{20,28},{24,32},{28,36},{32,40... | collective-permute-start | bytes 98312 | tf_op jit(solution)/shard_map/ppermute | solution.py:266
  78.9 3.9 %collective-permute-start.6 = (bf16[4,8,512]{2,1,0:T(8,128)(2,1)S(1)}, bf16[4,8,512]{2,1,0:T(8,128)(2,1)S(1)}, u32[]{:S(2)}, u32[]{:S(2)}) collective-permute-start(bf16[4,8,512]{2,1,0:T(8,128)(2,1)S(1)} %get-tuple-element.59), channel_id=1, source_target_pairs={{0,4},{4,8},{8,12},{12,16},{16,20},{20,24},{24,28},{28,32},{32,36}... | collective-permute-start | bytes 98312 | tf_op jit(solution)/shard_map/ppermute | solution.py:266
  80.9 1.8 %collective-permute-start.8 = (bf16[4,8,512]{2,1,0:T(8,128)(2,1)S(1)}, bf16[4,8,512]{2,1,0:T(8,128)(2,1)S(1)}, u32[]{:S(2)}, u32[]{:S(2)}) collective-permute-start(bf16[4,8,512]{2,1,0:T(8,128)(2,1)S(1)} %get-tuple-element.60), channel_id=1, source_target_pairs={{2,258},{6,262},{10,266},{14,270},{18,274},{22,278},{26,282},{30,2... | collective-permute-start | bytes 98312 | tf_op jit(solution)/shard_map/ppermute | solution.py:266
  83.4 12.6 %all-to-all-start.1 = ((bf16[4,32,512]{2,1,0:T(8,128)(2,1)}), bf16[4,32,512]{2,1,0:T(8,128)(2,1)S(1)}, u32[]{:S(2)}, u32[]{:S(2)}) async-start(bf16[4,32,512]{2,1,0:T(8,128)(2,1)} %maximum_bitcast_fusion), calls=%async_computation.1 | async-start | bytes 262144 | tf_op jit(solution)/shard_map/all_to_all | solution.py:268
  96.1 0.7 copy-start.8
  100.1 14.2 %collective-permute-start.11 = (bf16[512,512]{1,0:T(8,128)(2,1)}, bf16[512,512]{1,0:T(8,128)(2,1)S(1)}, u32[]{:S(2)}, u32[]{:S(2)}) collective-permute-start(bf16[512,512]{1,0:T(8,128)(2,1)} %decode.1.local), channel_id=1, source_target_pairs={{0,4},{4,0},{8,12},{12,8},{16,20},{20,16},{24,28},{28,24},{32,36},... | collective-permute-start | bytes 1572872 | tf_op jit(solution)/shard_map/ppermute | solution.py:44
  102.0 16.4 %collective-permute-start.10 = (bf16[512,512]{1,0:T(8,128)(2,1)}, bf16[512,512]{1,0:T(8,128)(2,1)S(1)}, u32[]{:S(2)}, u32[]{:S(2)}) collective-permute-start(bf16[512,512]{1,0:T(8,128)(2,1)} %decode.1.local), channel_id=1, source_target_pairs={{0,504},{4,508},{8,0},{12,4},{16,8},{20,12},{24,16},{28,20},{32,24... | collective-permute-start | bytes 1572872 | tf_op jit(solution)/shard_map/ppermute | solution.py:38
  105.3 19.5 %collective-permute-start.9 = (bf16[512,512]{1,0:T(8,128)(2,1)}, bf16[512,512]{1,0:T(8,128)(2,1)S(1)}, u32[]{:S(2)}, u32[]{:S(2)}) collective-permute-start(bf16[512,512]{1,0:T(8,128)(2,1)} %decode.1.local), channel_id=1, source_target_pairs={{0,8},{4,12},{8,16},{12,20},{16,24},{20,28},{24,32},{28,36},{32,40... | collective-permute-start | bytes 1572872 | tf_op jit(solution)/shard_map/ppermute | solution.py:38
  114.3 10.5 %copy-start.9 = (bf16[512,512]{1,0:T(8,128)(2,1)}, bf16[512,512]{1,0:T(8,128)(2,1)S(1)}, u32[]{:S(2)}) copy-start(bf16[512,512]{1,0:T(8,128)(2,1)S(1)} %collective-permute-done.11.sib) | copy-start | bytes 1572868
  118.4 10.4 %copy-start.2 = (bf16[512,512]{1,0:T(8,128)(2,1)}, bf16[512,512]{1,0:T(8,128)(2,1)S(1)}, u32[]{:S(2)}) copy-start(bf16[512,512]{1,0:T(8,128)(2,1)S(1)} %collective-permute-done.10.down) | copy-start | bytes 1572868
  124.8 4.0 %copy-start.3 = (bf16[512,512]{1,0:T(8,128)(2,1)}, bf16[512,512]{1,0:T(8,128)(2,1)S(1)}, u32[]{:S(2)}) copy-start(bf16[512,512]{1,0:T(8,128)(2,1)S(1)} %collective-permute-done.9.up) | copy-start | bytes 1572868
  124.9 15.8 %collective-permute-start.12 = (bf16[2,512,512]{2,1,0:T(8,128)(2,1)S(1)}, bf16[2,512,512]{2,1,0:T(8,128)(2,1)S(1)}, u32[]{:S(2)}, u32[]{:S(2)}) collective-permute-start(bf16[2,512,512]{2,1,0:T(8,128)(2,1)S(1)} %pad_maximum_fusion), channel_id=1, source_target_pairs={{0,4},{4,0},{8,12},{12,8},{16,20},{20,16},{24,28},{28,24},{32,36},... | collective-permute-start | bytes 3145736 | tf_op jit(solution)/shard_map/ppermute | solution.py:44
  126.9 13.8 %collective-permute-start.13 = (bf16[512,512]{1,0:T(8,128)(2,1)S(1)}, bf16[512,512]{1,0:T(8,128)(2,1)S(1)}, u32[]{:S(2)}, u32[]{:S(2)}) collective-permute-start(bf16[512,512]{1,0:T(8,128)(2,1)S(1)} %broadcast_select_fusion), channel_id=1, source_target_pairs={{0,508},{4,8},{8,4},{12,16},{16,12},{20,24},{24,20},{28,32},{32,28... | collective-permute-start | bytes 1572872 | tf_op jit(solution)/shard_map/ppermute | solution.py:44
  140.7 0.8 copy-start.10
  141.6 1.0 copy-start.4

commit v3 on v2

--- a/solution.py
+++ b/solution.py
@@ -13,7 +13,7 @@
 WIDE = 256
 SPLIT = 128
 FAR = ((16, 1, 2, None), (-16, -1, -2, None), (8, 4, 32, 64), (-8, -4, -32, None))
-VMEM = pltpu.CompilerParams(vmem_limit_bytes=56 * 1024 * 1024)
+VMEM = pltpu.CompilerParams(vmem_limit_bytes=20 * 1024 * 1024)
 
 
 def silu(v):
@@ -49,33 +49,38 @@
 
 
 def one_hot(where, ids):
-    return jnp.where(where == ids, 1.0, 0.0).astype(BF16)
-
-
-def pack_body(core, x, pack, up, down, three, own, padded):
+    same = where == jnp.broadcast_to(ids.astype(jnp.int16), where.shape)
+    return jnp.where(same, jnp.ones(where.shape, BF16), jnp.zeros(where.shape, BF16))
+
+
+def positions(dims, axis):
+    return lax.broadcasted_iota(jnp.int32, dims, axis).astype(jnp.int16)
+
+
+def pack_body(core, x, pack, up, down, three, own, hot):
     here = core[0]
     channels, rows = x.shape
     slots = pack.shape[-1]
-    padded[...] = jnp.zeros_like(padded)
-    padded[0:channels, :] = x[...]
-    row_of = lax.broadcasted_iota(jnp.int32, (rows, slots), 0)
-
-    def chosen(offset):
-        return mul(padded[...], one_hot(row_of, pack[offset])).astype(BF16)
-
-    up[0] = chosen(5)
-    up[1] = chosen(jnp.where(here == 0, 6, 4))
-    down[0] = chosen(1)
-    down[1] = chosen(jnp.where(here == 0, 2, 0))
-    three[...] = chosen(jnp.where(here == 0, 0, 6))
-    own[...] = chosen(jnp.where(here == 0, 4, 2))
+    row_of = positions((rows, slots), 0)
+    blank = jnp.zeros((SENT - channels, slots), BF16)
+
+    def chosen(outs, offsets):
+        for i, offset in enumerate(offsets):
+            hot[:, i * slots : (i + 1) * slots] = one_hot(row_of, pack[offset])
+        found = mul(x[...], hot[...]).astype(BF16)
+        for i, out in enumerate(outs):
+            out[0:channels, :] = found[:, i * slots : (i + 1) * slots]
+            out[channels:SENT, :] = blank
+
+    chosen((up.at[0], up.at[1]), (5, jnp.where(here == 0, 6, 4)))
+    chosen((down.at[0], down.at[1]), (1, jnp.where(here == 0, 2, 0)))
+    chosen((three, own), (jnp.where(here == 0, 0, 6), jnp.where(here == 0, 4, 2)))
 
 
 def weights_body(core, embed, edge, proc, dec, out, padded):
     width = out.shape[0]
     eye = one_hot(
-        lax.broadcasted_iota(jnp.int32, (width, width), 0),
-        lax.broadcasted_iota(jnp.int32, (width, width), 1),
+        positions((width, width), 0), lax.broadcasted_iota(jnp.int32, (width, width), 1)
     )
 
     def turn(piece, at):
@@ -95,7 +100,8 @@
         turn(dec[...], proc.shape[0] - SPLIT)
 
 
-def prepare_body(core, x, mine, other, edges, latent, table, padded):
+def prepare_body(core, mine, other, x, edges, latent, *rest):
+    *tables, padded = rest
     is_even = core[0] == 0
     channels, rows = x.shape
     padded[...] = jnp.zeros_like(padded)
@@ -106,28 +112,60 @@
             padded[...], w_embed, (((0,), (1,)), ((), ())), preferred_element_type=F32
         )
     ).astype(BF16)
-    nodes = table.shape[1] // 3
-    late = (jnp.where(is_even, 2, 0), jnp.where(is_even, 6, 4), jnp.where(is_even, 0, 6))
-    for i, offset in enumerate(late):
-        table[:, i * nodes : (i + 1) * nodes] = edge_table(edges, offset, nodes)
-
-
-def edge_table(edges, offset, nodes):
-    count, rows = edges.shape
+    order = (
+        3,
+        jnp.where(is_even, 4, 2),
+        1,
+        5,
+        jnp.where(is_even, 0, 6),
+        jnp.where(is_even, 2, 0),
+        jnp.where(is_even, 6, 4),
+    )
+    count = edges.shape[0]
     spare = jnp.zeros((8 - count, rows), jnp.int32)
-    ids = jnp.concatenate([edges[...] - offset * nodes, spare], axis=0).T
-    where = lax.broadcasted_iota(jnp.int32, (rows, nodes), 1)
-    total = jnp.where(where == ids[:, 0:1], 1.0, 0.0)
-    for k in range(1, count):
-        total += jnp.where(where == ids[:, k : k + 1], 1.0, 0.0)
-    return total.astype(BF16)
-
-
-def messages(block, w_embed, w_edge):
-    return silu_rows(w_edge, silu_rows(w_embed, block))
-
-
-def early_body(core, x, pack, up, down, three, mine, other, recv, embed, out, padded):
+    ids = jnp.concatenate([edges[...], spare], axis=0).T
+    nodes = sum(table.shape[1] for table in tables) // len(order)
+    step = 128
+    columns = positions((step, step), 1)
+    for first in range(0, rows, step):
+        wide = [
+            jnp.broadcast_to(ids[first : first + step, k : k + 1], (step, step))
+            for k in range(count)
+        ]
+        at = 0
+        for table in tables:
+            for block in range(table.shape[1] // nodes):
+                base = order[at] * nodes
+                moved = [(w - base).astype(jnp.int16) for w in wide]
+                at += 1
+                for part in range(0, nodes, step):
+                    here = columns + jnp.int16(part)
+                    total = one_hot(here, moved[0])
+                    for k in range(1, count):
+                        total += one_hot(here, moved[k])
+                    left = block * nodes + part
+                    table[first : first + step, left : left + step] = total
+
+
+def messages(blocks, w_embed, w_edge, rows, sent):
+    slots = blocks[0].shape[1]
+    for i, block in enumerate(blocks):
+        rows[:, i * slots : (i + 1) * slots] = silu_rows(w_embed, block)
+    for i in range(len(blocks)):
+        at = slice(i * slots, (i + 1) * slots)
+        sent[:, at] = silu_rows(w_edge, rows[:, at])
+
+
+def receivers(recv, offsets, hot):
+    nodes, slots = hot.shape[0], recv.shape[-1]
+    node_of = positions((nodes, slots), 0)
+    for i, offset in enumerate(offsets):
+        hot[:, i * slots : (i + 1) * slots] = one_hot(node_of, recv[offset])
+
+
+def early_body(
+    core, x, pack, up, down, three, mine, other, recv, embed, out, rows, sent, hot, padded
+):
     is_even = core[0] == 0
     nodes, channels = embed.shape
     slots = recv.shape[-1]
@@ -135,25 +173,17 @@
     w_edge = jnp.where(is_even, mine[:, WIDE : WIDE + channels], other[:, WIDE : WIDE + channels])
     padded[...] = jnp.zeros_like(padded)
     padded[0 : x.shape[0], :] = x[...]
-    row_of = lax.broadcasted_iota(jnp.int32, (x.shape[1], slots), 0)
-    local = mul(padded[...], one_hot(row_of, pack[3])).astype(BF16)
-    node_of = lax.broadcasted_iota(jnp.int32, (nodes, slots), 0)
-    total = embed[...].astype(F32)
-    blocks = (
-        (local, 3),
-        (up[0], 5),
-        (down[0], 1),
-        (three[...], jnp.where(is_even, 6, 0)),
-    )
-    for block, offset in blocks:
-        total += mul_nt(one_hot(node_of, recv[offset]), messages(block, w_embed, w_edge))
-    out[...] = total
-
-
-def encode_body(core, here, early, sib, mine, other, recv, far_ids, latent, message, far):
+    local = mul(padded[...], one_hot(positions((x.shape[1], slots), 0), pack[3])).astype(BF16)
+    messages((local, up[0], down[0], three[...]), w_embed, w_edge, rows, sent)
+    receivers(recv, (3, 5, 1, jnp.where(is_even, 6, 0)), hot)
+    out[...] = embed[...].astype(F32) + mul_nt(hot[...], sent[...])
+
+
+def encode_body(
+    core, here, early, sib, mine, other, recv, far_ids, latent, message, far, rows, sent, hot
+):
     is_even = core[0] == 0
     nodes, channels = early.shape
-    slots = recv.shape[-1]
     w_embed = jnp.where(is_even, mine[:, 0:SENT], other[:, 0:SENT])
     w_edge = jnp.where(is_even, mine[:, WIDE : WIDE + channels], other[:, WIDE : WIDE + channels])
     first = WIDE + channels
@@ -161,16 +191,14 @@
     rest = channels - SPLIT
     high = jnp.where(is_even, other[:, 0:rest], mine[:, 0:rest])
     w_proc = jnp.concatenate([low, high], axis=1)
-    node_of = lax.broadcasted_iota(jnp.int32, (nodes, slots), 0)
-    total = early[...]
+    messages((sib[0], sib[1], sib[2]), w_embed, w_edge, rows, sent)
     offsets = (jnp.where(is_even, 2, 4), jnp.where(is_even, 4, 6), jnp.where(is_even, 0, 2))
-    for i, offset in enumerate(offsets):
-        total += mul_nt(one_hot(node_of, recv[offset]), messages(sib[i], w_embed, w_edge))
-    rounded = total.astype(BF16)
+    receivers(recv, offsets, hot)
+    rounded = (early[...] + mul_nt(hot[...], sent[...])).astype(BF16)
     latent[...] = rounded
-    sent = silu(mul_nt(rounded, w_proc)).astype(BF16)
-    message[...] = sent
-    far[...] = mul(far_table(far_ids, here[0], 1, nodes), sent).astype(BF16)
+    made = silu(mul_nt(rounded, w_proc)).astype(BF16)
+    message[...] = made
+    far[...] = mul(far_table(far_ids, here[0], 1, nodes), made).astype(BF16)
 
 
 def far_table(ids, here, sign, nodes):
@@ -209,33 +237,28 @@
     out[...] = silu(mul_nt(after, w_dec)).astype(BF16)
 
 
-def near_body(core, latent, edges, local, sib, up, down, out):
-    is_even = core[0] == 0
-    nodes = local.shape[0]
-    total = latent[...].astype(F32)
-    blocks = ((local, 3), (sib, jnp.where(is_even, 4, 2)), (up, 1), (down, 5))
-    for block, offset in blocks:
-        total += mul(edge_table(edges, offset, nodes), block[...])
-    out[...] = total
-
-
-def collect_body(near, table, relay, three, out):
-    nodes = three.shape[0]
-    total = near[...]
-    for i, block in enumerate((relay[0], relay[1], three[...])):
-        total += mul(table[:, i * nodes : (i + 1) * nodes], block)
-    out[...] = total.astype(BF16)
-
-
-def call(body, out_shape, args, scratch=(), name=None):
+def add_body(before, *rest):
+    *blocks, table, out, joined = rest
+    nodes = blocks[0].shape[0]
+    for i, block in enumerate(blocks):
+        joined[i * nodes : (i + 1) * nodes, :] = block[...]
+    out[...] = (before[...].astype(F32) + mul(table[...], joined[...])).astype(out.dtype)
+
+
+def call(body, out_shape, args, scratch=(), name=None, stored=()):
+    near = len(args)
+    args = (*args, *stored)
     smem = pl.BlockSpec(memory_space=pltpu.SMEM)
     vmem = pl.BlockSpec(memory_space=pltpu.VMEM)
-    specs = [smem if a.ndim == 1 else vmem for a in args]
     many = isinstance(out_shape, (list, tuple))
+    args = [
+        a if a.ndim == 1 else pltpu.with_memory_space_constraint(a, place)
+        for a, place in zip(args, [pltpu.VMEM] * near + [pltpu.HBM] * (len(args) - near))
+    ]
     return pl.pallas_call(
         body,
         out_shape=out_shape,
-        in_specs=specs,
+        in_specs=[smem if a.ndim == 1 else vmem for a in args],
         out_specs=[vmem for _ in out_shape] if many else vmem,
         scratch_shapes=scratch,
         compiler_params=VMEM,
@@ -244,7 +267,7 @@
 
 
 def shape(*dims, kind=BF16):
-    return jax.ShapeDtypeStruct(dims, kind)
+    return pltpu.VMEM(dims, kind)
 
 
 def far_exchange(rows):
@@ -294,12 +317,24 @@
     recv = recv_node.reshape(offsets, 1, slots)
     far_out_ids = far_send.reshape(far_send.shape[2:]).T
     far_in_ids = far_recv.reshape(far_recv.shape[2:]).T
+    def stored(*dims):
+        return pltpu.HBM(dims, BF16)
+
+    def work(blocks):
+        wide = pltpu.VMEM((channels, blocks * slots), BF16)
+        return wide, wide, pltpu.VMEM((nodes, blocks * slots), BF16)
+
     block = shape(SENT, slots)
     pair = shape(2, SENT, slots)
     padded = pltpu.VMEM((SENT, rows), BF16)
 
     up, down, three, own = call(
-        pack_body, [pair, pair, block, block], (core, x, pack), [padded], name="pack"
+        pack_body,
+        [pair, pair, block, block],
+        (core,),
+        [pltpu.VMEM((rows, 2 * slots), BF16)],
+        name="pack",
+        stored=(x, pack),
     )
     up, down, three, own, w_embed, w_edge, w_proc, w_dec = lax.optimization_barrier(
         (up, down, three, own, w_embed, w_edge, w_proc, w_dec)
@@ -310,9 +345,10 @@
     shard = call(
         weights_body,
         shape(w_edge.shape[1], (WIDE + 3 * channels) // 2),
-        (core, w_embed, w_edge, w_proc, w_dec),
+        (core,),
         [pltpu.VMEM((WIDE, w_edge.shape[1]), BF16)],
         name="weights",
+        stored=(w_embed, w_edge, w_proc, w_dec),
     )
     mine = lax.all_gather(shard, "chan", axis=0, tiled=True)
     mine, up, down, three = lax.optimization_barrier((mine, up, down, three))
@@ -322,21 +358,23 @@
         early_body,
         shape(nodes, channels, kind=F32),
         (core, x, pack, up, down, three, mine, other, recv, mesh_embed),
-        [padded],
+        [*work(4), padded],
         name="early",
     )
     mesh_latent, node_msg, far_sent = call(
         encode_body,
-        [shape(nodes, channels), shape(nodes, channels), shape(8 * 16, channels)],
+        [stored(nodes, channels), stored(nodes, channels), shape(8 * 16, channels)],
         (core, here, early, sib, mine, other, recv, far_out_ids),
+        [*work(3)],
         name="encode",
     )
     arrived = far_exchange(far_sent)
     base = call(
         local_body,
         shape(nodes, channels, kind=F32),
-        (mesh_latent, node_msg, loc_nbr.T),
+        (),
         name="short",
+        stored=(mesh_latent, node_msg, loc_nbr.T),
     )
     dec_msg = call(
         decode_body,
@@ -347,28 +385,32 @@
     up = shifted(dec_msg, 2)
     down = shifted(dec_msg, -2)
     sib = by_core(dec_msg, 1, -1)
-    latent, table = call(
+    dec_msg, x, edges = lax.optimization_barrier((dec_msg, x, dec_edge.T))
+    latent, own_table, near_table, late_table = call(
         prepare_body,
-        [shape(rows, channels), shape(rows, 3 * nodes)],
-        (core, x, mine, other, dec_edge.T),
+        [shape(rows, channels)] + [shape(rows, n * nodes) for n in (2, 2, 3)],
+        (core, mine, other),
         [pltpu.VMEM((WIDE, rows), BF16)],
         name="prepare",
-    )
-    up, down, sib, latent, table = lax.optimization_barrier((up, down, sib, latent, table))
+        stored=(x, edges),
+    )
+
+    def added(name, before, blocks, table, kind=F32):
+        return call(
+            add_body,
+            shape(rows, channels, kind=kind) if kind == F32 else stored(rows, channels),
+            (before, *blocks, table),
+            [pltpu.VMEM((len(blocks) * nodes, channels), BF16)],
+            name=name,
+        )
+
+    total = added("own", latent, (dec_msg, sib), own_table)
+    up, down, total = lax.optimization_barrier((up, down, total))
     three = by_core(jnp.where(core[0] == 0, down, up), -1, 1)
-    relay = by_core(jnp.stack([up, down]), 1, -1)
-    near = call(
-        near_body,
-        shape(rows, channels, kind=F32),
-        (core, latent, dec_edge.T, dec_msg, sib, up, down),
-        name="near",
-    )
-    return call(
-        collect_body,
-        shape(rows, channels),
-        (near, table, relay, three),
-        name="collect",
-    )
+    relay_up = by_core(up, 1, -1)
+    relay_down = by_core(down, 1, -1)
+    total = added("near", total, (up, down), near_table)
+    return added("collect", total, (three, relay_up, relay_down), late_table, BF16)
 
 
 def solution(mesh):

time: 149 us -> 127 us (0.85)
  Pallas kernels: 44.8 us -> 25.1 us
  local copies, waits for them, and re-layouts: 4.25 us -> 0.08 us
  waiting for transfers between devices: 17.1 us -> 20.1 us
    pallas_call x9 -> x10, Pallas kernels: 44.8 us -> 25.1 us  [call(): pl.pallas_call(body, out_shape=out_shape, in_specs=[smem if a.ndim == 1 e...]
    unnamed x24 -> x12, local copies, waits for them, and re-layouts: 4.19 us -> 0.03 us
    ppermute x6 -> x7, starting transfers between devices: 13.3 us -> 15.7 us  [by_core(): return lax.ppermute(value, 'patch', pairs)]
    ppermute x4, waiting for transfers between devices: 10.5 us -> 8.41 us  [shifted(): lax.ppermute(value, 'patch', [(i, (i + steps) % count) for i in range(cou...]
    ppermute x4, waiting for transfers between devices: 1.14 us -> 3.21 us  [far_exchange(): arrived.append(lax.ppermute(mine[:, kind], ('patch', 'chan'), pairs))]
    ppermute x6 -> x7, waiting for transfers between devices: 4.31 us -> 6.31 us  [by_core(): return lax.ppermute(value, 'patch', pairs)]
    all_to_all x1, starting transfers between devices: 8.11 us -> 6.24 us  [far_exchange(): lax.all_to_all(back, 'chan', 0, 0, tiled=True).reshape(count, channels)]
  transfers between devices with their start and end apart: 15 -> 16, of which waited for: 6 -> 6; matrix products, arithmetic and copies ran while one was open for 1% -> 0% of each run, Pallas kernels for 18% -> 12%
where the time goes in v3:
time: 127 us
  starting transfers between devices  57.2 us (45%)
  Pallas kernels  25.1 us (20%)
  blocking collectives  22.9 us (18%)
  waiting for transfers between devices  20.1 us (16%)
    pallas_call x10, Pallas kernels, call(): pl.pallas_call(body, out_shape=out_shape, in_specs=[smem if a.ndim == 1 e...  25.1 us
    ppermute x4, starting transfers between devices, shifted(): lax.ppermute(value, 'patch', [(i, (i + steps) % count) for i in range(cou...  21.5 us
    ppermute x7, starting transfers between devices, by_core(): return lax.ppermute(value, 'patch', pairs)  15.7 us
    all_gather x1, blocking collectives, shards(): mine = lax.all_gather(shard, 'chan', axis=0, tiled=True)  14 us
    ppermute x4, starting transfers between devices, far_exchange(): arrived.append(lax.ppermute(mine[:, kind], ('patch', 'chan'), pairs))  13.7 us
    all_to_all x1, blocking collectives, far_exchange(): lax.all_to_all(rows.reshape(chans, kinds * each, channels), 'chan', 0, 0,...  8.94 us
    ppermute x4, waiting for transfers between devices, shifted(): lax.ppermute(value, 'patch', [(i, (i + steps) % count) for i in range(cou...  8.41 us
    ppermute x7, waiting for transfers between devices, by_core(): return lax.ppermute(value, 'patch', pairs)  6.31 us
  transfers between devices with their start and end apart: 16, of which 6 were waited for; matrix products, arithmetic and copies ran while one was open for 0% of the time, Pallas kernels for 12%

profile of v3, /device:TPU:8, one launch (start us, length us, event | category | flops | bytes accessed | tf_op | source)
XLA Modules:
  0.0 126.5 jit_solution(15507847732454455369)
XLA Ops:
  0.0 0.0 copy-start
  0.0 0.0 copy-start.1
  0.0 0.0 copy-start.2
  0.0 0.0 copy-start.3
  0.0 2.8 %pack.1 = (bf16[2,240,384]{2,1,0:T(8,128)(2,1)S(1)}, bf16[2,240,384]{2,1,0:T(8,128)(2,1)S(1)}, bf16[240,384]{1,0:T(8,128)(2,1)S(1)}, bf16[240,384]{1,0:T(8,128)(2,1)S(1)}) custom-call(s32[1]{0:T(128)} %bitcast.core, bf16[227,1024]{1,0:T(8,128)(2,1)} %bitcast.39, s32[7,1,384]{2,1,0:T(1,128)} %bitcast.47), custom_call_target="tpu_custom_call" | custom-call | tf_op jit(solution)/shard_map/pack/pallas_call | solution.py:258
  2.8 3.8 %collective-permute-start = (bf16[2,240,384]{2,1,0:T(8,128)(2,1)S(1)}, bf16[2,240,384]{2,1,0:T(8,128)(2,1)S(1)}, u32[]{:S(2)}, u32[]{:S(2)}) collective-permute-start(bf16[2,240,384]{2,1,0:T(8,128)(2,1)S(1)} %get-tuple-element.42), channel_id=1, source_target_pairs={{0,8},{4,12},{8,16},{12,20},{16,24},{20,28},{24,32},{28,36},{32,40... | collective-permute-start | bytes 1105928 | tf_op jit(solution)/shard_map/ppermute | solution.py:38
  6.6 11.7 %collective-permute-start.1 = (bf16[2,240,384]{2,1,0:T(8,128)(2,1)S(1)}, bf16[2,240,384]{2,1,0:T(8,128)(2,1)S(1)}, u32[]{:S(2)}, u32[]{:S(2)}) collective-permute-start(bf16[2,240,384]{2,1,0:T(8,128)(2,1)S(1)} %get-tuple-element.43), channel_id=1, source_target_pairs={{0,504},{4,508},{8,0},{12,4},{16,8},{20,12},{24,16},{28,20},{32,24... | collective-permute-start | bytes 1105928 | tf_op jit(solution)/shard_map/ppermute | solution.py:38
  18.3 3.2 %collective-permute-start.2 = (bf16[240,384]{1,0:T(8,128)(2,1)S(1)}, bf16[240,384]{1,0:T(8,128)(2,1)S(1)}, u32[]{:S(2)}, u32[]{:S(2)}) collective-permute-start(bf16[240,384]{1,0:T(8,128)(2,1)S(1)} %get-tuple-element.44), channel_id=1, source_target_pairs={{0,500},{4,16},{8,508},{12,24},{16,4},{20,32},{24,12},{28,40},{32,... | collective-permute-start | bytes 552968 | tf_op jit(solution)/shard_map/ppermute | solution.py:44
  21.6 1.3 %weights.1 = bf16[128,896]{1,0:T(8,128)(2,1)S(1)} custom-call(s32[1]{0:T(128)} %bitcast.core, bf16[227,128]{1,0:T(8,128)(2,1)} %embed.1, bf16[512,128]{1,0:T(8,128)(2,1)} %edge, bf16[512,128]{1,0:T(8,128)(2,1)} %proc, bf16[512,128]{1,0:T(8,128)(2,1)} %dec), custom_call_target="tpu_custom_call" | custom-call | tf_op jit(solution)/shard_map/weights/pallas_call | solution.py:258
  22.9 14.0 %all_gather.3.mine = bf16[512,896]{1,0:T(8,128)(2,1)S(1)} all-gather(bf16[128,896]{1,0:T(8,128)(2,1)S(1)} %weights.1), channel_id=1, replica_groups=mesh['patch'=128,'chan'=4] {'chan'}, dimensions={0}, use_global_device_ids=true | all-gather | bytes 1146880 | tf_op jit(solution)/shard_map/all_gather | solution.py:353
  36.9 0.0 collective-permute-done.2.three
  36.9 0.0 collective-permute-done.up
  36.9 0.0 collective-permute-done.1.down
  36.9 1.9 %collective-permute-start.3 = (bf16[512,896]{1,0:T(8,128)(2,1)S(1)}, bf16[512,896]{1,0:T(8,128)(2,1)S(1)}, u32[]{:S(2)}, u32[]{:S(2)}) collective-permute-start(bf16[512,896]{1,0:T(8,128)(2,1)S(1)} %all_gather.3.mine), channel_id=1, source_target_pairs={{0,4},{4,0},{8,12},{12,8},{16,20},{20,16},{24,28},{28,24},{32,36},... | collective-permute-start | bytes 2752520 | tf_op jit(solution)/shard_map/ppermute | solution.py:44
  38.9 0.1 pad_maximum_fusion
  39.0 2.4 %collective-permute-start.4 = (bf16[3,240,384]{2,1,0:T(8,128)(2,1)S(1)}, bf16[3,240,384]{2,1,0:T(8,128)(2,1)S(1)}, u32[]{:S(2)}, u32[]{:S(2)}) collective-permute-start(bf16[3,240,384]{2,1,0:T(8,128)(2,1)S(1)} %pad_maximum_fusion), channel_id=1, source_target_pairs={{0,4},{4,0},{8,12},{12,8},{16,20},{20,16},{24,28},{28,24},{32,36},... | collective-permute-start | bytes 1658888 | tf_op jit(solution)/shard_map/ppermute | solution.py:44
  41.4 0.0 collective-permute-done.3.other
  41.4 0.0 copy-done
  41.4 0.0 copy-done.1
  41.4 0.0 copy-done.2
  41.5 0.0 copy-done.3
  41.5 0.0 copy-start.4
  41.5 3.3 %early.1 = f32[512,512]{1,0:T(8,128)S(1)} custom-call(s32[1]{0:T(128)} %bitcast.core, bf16[227,1024]{1,0:T(8,128)(2,1)S(1)} %bitcast.41, s32[7,1,384]{2,1,0:T(1,128)S(1)} %bitcast.48, bf16[2,240,384]{2,1,0:T(8,128)(2,1)S(1)} %collective-permute-done.up, bf16[2,240,384]{2,1,0:T(8,128)(2,1)S(1)} %collective-permute-done.1.down, ...), custom_call_target="tpu_custom_call" | custom-call | tf_op jit(solution)/shard_map/early/pallas_call | solution.py:258
  44.7 0.0 collective-permute-done.4.sib
  44.8 0.0 copy-done.4
  44.8 3.4 %encode.1 = (bf16[512,512]{1,0:T(8,128)(2,1)}, bf16[512,512]{1,0:T(8,128)(2,1)}, bf16[128,512]{1,0:T(8,128)(2,1)S(1)}) custom-call(s32[1]{0:T(128)} %bitcast.core, s32[1]{0:T(128)} %bitcast.1.here, f32[512,512]{1,0:T(8,128)S(1)} %early.1, bf16[3,240,384]{2,1,0:T(8,128)(2,1)S(1)} %collective-permute-done.4.sib, bf16[512,896]{1,0:T(8,128)(2,1)S(1)} %all_gather.3.mine, ...), custom_call_target="tpu_custom_call" | custom-call | tf_op jit(solution)/shard_map/encode/pallas_call | solution.py:258
  48.1 0.0 copy-start.5
  48.1 8.9 %all_to_all.10 = bf16[4,32,512]{2,1,0:T(8,128)(2,1)S(1)} all-to-all(bf16[4,32,512]{2,1,0:T(8,128)(2,1)S(1)} %bitcast.44), channel_id=1, replica_groups=mesh['patch'=128,'chan'=4] {'chan'}, dimensions={0} | all-to-all | bytes 262144 | tf_op jit(solution)/shard_map/all_to_all | solution.py:278
  57.1 9.2 %collective-permute-start.5 = (bf16[4,8,512]{2,1,0:T(8,128)(2,1)S(1)}, bf16[4,8,512]{2,1,0:T(8,128)(2,1)S(1)}, u32[]{:S(2)}, u32[]{:S(2)}) collective-permute-start(bf16[4,8,512]{2,1,0:T(8,128)(2,1)S(1)} %get-tuple-element.63), channel_id=1, source_target_pairs={{0,64},{4,68},{8,72},{12,76},{16,80},{20,84},{24,88},{28,92},{32,9... | collective-permute-start | bytes 98312 | tf_op jit(solution)/shard_map/ppermute | solution.py:289
  66.3 1.9 %collective-permute-start.6 = (bf16[4,8,512]{2,1,0:T(8,128)(2,1)S(1)}, bf16[4,8,512]{2,1,0:T(8,128)(2,1)S(1)}, u32[]{:S(2)}, u32[]{:S(2)}) collective-permute-start(bf16[4,8,512]{2,1,0:T(8,128)(2,1)S(1)} %get-tuple-element.65), channel_id=1, source_target_pairs={{0,4},{4,8},{8,12},{12,16},{16,20},{20,24},{24,28},{28,32},{32,36}... | collective-permute-start | bytes 98312 | tf_op jit(solution)/shard_map/ppermute | solution.py:289
  68.2 1.9 %collective-permute-start.7 = (bf16[4,8,512]{2,1,0:T(8,128)(2,1)S(1)}, bf16[4,8,512]{2,1,0:T(8,128)(2,1)S(1)}, u32[]{:S(2)}, u32[]{:S(2)}) collective-permute-start(bf16[4,8,512]{2,1,0:T(8,128)(2,1)S(1)} %get-tuple-element.64), channel_id=1, source_target_pairs={{0,8},{4,12},{8,16},{12,20},{16,24},{20,28},{24,32},{28,36},{32,40... | collective-permute-start | bytes 98312 | tf_op jit(solution)/shard_map/ppermute | solution.py:289
  70.2 0.7 collective-permute-start.8
  70.8 0.8 collective-permute-done.5
  71.6 0.0 collective-permute-done.6
  71.6 2.4 %collective-permute-done.7 = bf16[4,8,512]{2,1,0:T(8,128)(2,1)S(1)} collective-permute-done((bf16[4,8,512]{2,1,0:T(8,128)(2,1)S(1)}, bf16[4,8,512]{2,1,0:T(8,128)(2,1)S(1)}, u32[]{:S(2)}, u32[]{:S(2)}) %collective-permute-start.7) | collective-permute-done | bytes 32800 | tf_op jit(solution)/shard_map/ppermute | solution.py:289
  74.0 0.0 collective-permute-done.8
  74.0 0.7 maximum_bitcast_fusion
  74.7 6.2 %all-to-all-start.1 = ((bf16[4,32,512]{2,1,0:T(8,128)(2,1)}), bf16[4,32,512]{2,1,0:T(8,128)(2,1)S(1)}, u32[]{:S(2)}, u32[]{:S(2)}) async-start(bf16[4,32,512]{2,1,0:T(8,128)(2,1)} %maximum_bitcast_fusion), calls=%async_computation.1 | async-start | bytes 262144 | tf_op jit(solution)/shard_map/all_to_all | solution.py:291
  81.0 2.4 %short.1.base = f32[512,512]{1,0:T(8,128)S(1)} custom-call(bf16[512,512]{1,0:T(8,128)(2,1)} %get-tuple-element.50.latent, bf16[512,512]{1,0:T(8,128)(2,1)} %get-tuple-element.51.message, s32[6,512]{1,0:T(8,128)} %bitcast.56), custom_call_target="tpu_custom_call" | custom-call | tf_op jit(solution)/shard_map/short/pallas_call | solution.py:258
  83.4 2.1 %all-to-all-done.1 = bf16[4,32,512]{2,1,0:T(8,128)(2,1)S(1)} async-done(((bf16[4,32,512]{2,1,0:T(8,128)(2,1)}), bf16[4,32,512]{2,1,0:T(8,128)(2,1)S(1)}, u32[]{:S(2)}, u32[]{:S(2)}) %all-to-all-start.1) | async-done | bytes 131104 | tf_op jit(solution)/shard_map/all_to_all | solution.py:291
  85.5 0.0 copy-done.5
  85.5 0.7 decode.1.rest_0_
  86.2 1.9 %collective-permute-start.11 = (bf16[512,512]{1,0:T(8,128)(2,1)S(1)}, bf16[512,512]{1,0:T(8,128)(2,1)}, u32[]{:S(2)}, u32[]{:S(2)}) collective-permute-start(bf16[512,512]{1,0:T(8,128)(2,1)S(1)} %decode.1.rest_0_), channel_id=1, source_target_pairs={{0,4},{4,0},{8,12},{12,8},{16,20},{20,16},{24,28},{28,24},{32,36},... | collective-permute-start | bytes 1572872 | tf_op jit(solution)/shard_map/ppermute | solution.py:44
  88.2 2.4 %collective-permute-start.10 = (bf16[512,512]{1,0:T(8,128)(2,1)S(1)}, bf16[512,512]{1,0:T(8,128)(2,1)S(1)}, u32[]{:S(2)}, u32[]{:S(2)}) collective-permute-start(bf16[512,512]{1,0:T(8,128)(2,1)S(1)} %decode.1.rest_0_), channel_id=1, source_target_pairs={{0,504},{4,508},{8,0},{12,4},{16,8},{20,12},{24,16},{28,20},{32,24... | collective-permute-start | bytes 1572872 | tf_op jit(solution)/shard_map/ppermute | solution.py:38
  90.6 3.6 %collective-permute-start.9 = (bf16[512,512]{1,0:T(8,128)(2,1)S(1)}, bf16[512,512]{1,0:T(8,128)(2,1)S(1)}, u32[]{:S(2)}, u32[]{:S(2)}) collective-permute-start(bf16[512,512]{1,0:T(8,128)(2,1)S(1)} %decode.1.rest_0_), channel_id=1, source_target_pairs={{0,8},{4,12},{8,16},{12,20},{16,24},{20,28},{24,32},{28,36},{32,40... | collective-permute-start | bytes 1572872 | tf_op jit(solution)/shard_map/ppermute | solution.py:38
  94.2 4.9 %prepare.1 = (bf16[1024,512]{1,0:T(8,128)(2,1)S(1)}, bf16[1024,1024]{1,0:T(8,128)(2,1)S(1)}, bf16[1024,1024]{1,0:T(8,128)(2,1)S(1)}, bf16[1024,1536]{1,0:T(8,128)(2,1)S(1)}) custom-call(s32[1]{0:T(128)} %bitcast.core, bf16[512,896]{1,0:T(8,128)(2,1)S(1)} %all_gather.3.mine, bf16[512,896]{1,0:T(8,128)(2,1)S(1)} %collective-permute-done.3.other, ...), custom_call_target="tpu_custom_call" | custom-call | tf_op jit(solution)/shard_map/prepare/pallas_call | solution.py:258
  99.2 0.0 collective-permute-done.11.rest_1_
  99.2 2.3 %own.1.before = f32[1024,512]{1,0:T(8,128)S(1)} custom-call(bf16[1024,512]{1,0:T(8,128)(2,1)S(1)} %get-tuple-element.55.before, bf16[512,512]{1,0:T(8,128)(2,1)S(1)} %decode.1.rest_0_, bf16[512,512]{1,0:T(8,128)(2,1)} %collective-permute-done.11.rest_1_, bf16[1024,1024]{1,0:T(8,128)(2,1)S(1)} %get-tuple-element.57.rest_2_), custom_call_target="tpu_custom_call" | custom-call | tf_op jit(solution)/shard_map/own/pallas_call | solution.py:258
  101.5 2.9 %collective-permute-done.10.rest_1_ = bf16[512,512]{1,0:T(8,128)(2,1)S(1)} collective-permute-done((bf16[512,512]{1,0:T(8,128)(2,1)S(1)}, bf16[512,512]{1,0:T(8,128)(2,1)S(1)}, u32[]{:S(2)}, u32[]{:S(2)}) %collective-permute-start.10) | collective-permute-done | bytes 524320 | tf_op jit(solution)/shard_map/ppermute | solution.py:38
  104.4 5.5 %collective-permute-done.9.rest_0_ = bf16[512,512]{1,0:T(8,128)(2,1)S(1)} collective-permute-done((bf16[512,512]{1,0:T(8,128)(2,1)S(1)}, bf16[512,512]{1,0:T(8,128)(2,1)S(1)}, u32[]{:S(2)}, u32[]{:S(2)}) %collective-permute-start.9) | collective-permute-done | bytes 524320 | tf_op jit(solution)/shard_map/ppermute | solution.py:38
  109.9 0.1 broadcast_select_fusion
  109.9 1.9 %collective-permute-start.12 = (bf16[512,512]{1,0:T(8,128)(2,1)S(1)}, bf16[512,512]{1,0:T(8,128)(2,1)S(1)}, u32[]{:S(2)}, u32[]{:S(2)}) collective-permute-start(bf16[512,512]{1,0:T(8,128)(2,1)S(1)} %broadcast_select_fusion), channel_id=1, source_target_pairs={{0,508},{4,8},{8,4},{12,16},{16,12},{20,24},{24,20},{28,32},{32,28... | collective-permute-start | bytes 1572872 | tf_op jit(solution)/shard_map/ppermute | solution.py:44
  111.9 1.9 %collective-permute-start.13 = (bf16[512,512]{1,0:T(8,128)(2,1)S(1)}, bf16[512,512]{1,0:T(8,128)(2,1)S(1)}, u32[]{:S(2)}, u32[]{:S(2)}) collective-permute-start(bf16[512,512]{1,0:T(8,128)(2,1)S(1)} %collective-permute-done.9.rest_0_), channel_id=1, source_target_pairs={{0,4},{4,0},{8,12},{12,8},{16,20},{20,16},{24,28},{28,24},{32,36},... | collective-permute-start | bytes 1572872 | tf_op jit(solution)/shard_map/ppermute | solution.py:44
  113.8 2.4 %collective-permute-start.14 = (bf16[512,512]{1,0:T(8,128)(2,1)S(1)}, bf16[512,512]{1,0:T(8,128)(2,1)S(1)}, u32[]{:S(2)}, u32[]{:S(2)}) collective-permute-start(bf16[512,512]{1,0:T(8,128)(2,1)S(1)} %collective-permute-done.10.rest_1_), channel_id=1, source_target_pairs={{0,4},{4,0},{8,12},{12,8},{16,20},{20,16},{24,28},{28,24},{32,36},... | collective-permute-start | bytes 1572872 | tf_op jit(solution)/shard_map/ppermute | solution.py:44
  116.2 1.2 near.1.before
  117.5 6.3 %collective-permute-done.12.rest_0_ = bf16[512,512]{1,0:T(8,128)(2,1)S(1)} collective-permute-done((bf16[512,512]{1,0:T(8,128)(2,1)S(1)}, bf16[512,512]{1,0:T(8,128)(2,1)S(1)}, u32[]{:S(2)}, u32[]{:S(2)}) %collective-permute-start.12) | collective-permute-done | bytes 524320 | tf_op jit(solution)/shard_map/ppermute | solution.py:44
  123.7 0.0 collective-permute-done.13.rest_1_
  123.8 0.0 collective-permute-done.14.rest_2_
  123.8 2.8 %collect.1 = bf16[1024,512]{1,0:T(8,128)(2,1)} custom-call(f32[1024,512]{1,0:T(8,128)S(1)} %near.1.before, bf16[512,512]{1,0:T(8,128)(2,1)S(1)} %collective-permute-done.12.rest_0_, bf16[512,512]{1,0:T(8,128)(2,1)S(1)} %collective-permute-done.13.rest_1_, bf16[512,512]{1,0:T(8,128)(2,1)S(1)} %collective-permute-done.14.rest_2_, ...), custom_call_target="tpu_custom_call" | custom-call | tf_op jit(solution)/shard_map/collect/pallas_call | solution.py:258
  (3 shorter events, 0.1 us)
Async XLA Ops:
  0.0 41.4 %copy-start = (bf16[1024,227]{0,1:T(8,128)(2,1)S(1)}, bf16[1024,227]{0,1:T(8,128)(2,1)}, u32[]{:S(2)}) copy-start(bf16[1024,227]{0,1:T(8,128)(2,1)} %param.12) | copy-start | bytes 1394692
  0.0 41.4 %copy-start.1 = (bf16[512,512]{1,0:T(8,128)(2,1)S(1)}, bf16[512,512]{1,0:T(8,128)(2,1)}, u32[]{:S(2)}) copy-start(bf16[512,512]{1,0:T(8,128)(2,1)} %embed.2) | copy-start | bytes 1572868
  0.0 41.4 %copy-start.2 = (s32[1,1,7,384]{3,1,2,0:T(1,128)S(1)}, s32[1,1,7,384]{3,1,2,0:T(1,128)}, u32[]{:S(2)}) copy-start(s32[1,1,7,384]{3,1,2,0:T(1,128)} %param.19) | copy-start | bytes 32260
  0.0 41.4 %copy-start.3 = (s32[1,1,7,384]{3,1,2,0:T(1,128)S(1)}, s32[1,1,7,384]{3,1,2,0:T(1,128)}, u32[]{:S(2)}) copy-start(s32[1,1,7,384]{3,1,2,0:T(1,128)} %param.18) | copy-start | bytes 32260
  2.8 34.1 %collective-permute-start = (bf16[2,240,384]{2,1,0:T(8,128)(2,1)S(1)}, bf16[2,240,384]{2,1,0:T(8,128)(2,1)S(1)}, u32[]{:S(2)}, u32[]{:S(2)}) collective-permute-start(bf16[2,240,384]{2,1,0:T(8,128)(2,1)S(1)} %get-tuple-element.42), channel_id=1, source_target_pairs={{0,8},{4,12},{8,16},{12,20},{16,24},{20,28},{24,32},{28,36},{32,40... | collective-permute-start | bytes 1105928 | tf_op jit(solution)/shard_map/ppermute | solution.py:38
  6.6 30.3 %collective-permute-start.1 = (bf16[2,240,384]{2,1,0:T(8,128)(2,1)S(1)}, bf16[2,240,384]{2,1,0:T(8,128)(2,1)S(1)}, u32[]{:S(2)}, u32[]{:S(2)}) collective-permute-start(bf16[2,240,384]{2,1,0:T(8,128)(2,1)S(1)} %get-tuple-element.43), channel_id=1, source_target_pairs={{0,504},{4,508},{8,0},{12,4},{16,8},{20,12},{24,16},{28,20},{32,24... | collective-permute-start | bytes 1105928 | tf_op jit(solution)/shard_map/ppermute | solution.py:38
  18.3 18.6 %collective-permute-start.2 = (bf16[240,384]{1,0:T(8,128)(2,1)S(1)}, bf16[240,384]{1,0:T(8,128)(2,1)S(1)}, u32[]{:S(2)}, u32[]{:S(2)}) collective-permute-start(bf16[240,384]{1,0:T(8,128)(2,1)S(1)} %get-tuple-element.44), channel_id=1, source_target_pairs={{0,500},{4,16},{8,508},{12,24},{16,4},{20,32},{24,12},{28,40},{32,... | collective-permute-start | bytes 552968 | tf_op jit(solution)/shard_map/ppermute | solution.py:44
  36.9 4.5 %collective-permute-start.3 = (bf16[512,896]{1,0:T(8,128)(2,1)S(1)}, bf16[512,896]{1,0:T(8,128)(2,1)S(1)}, u32[]{:S(2)}, u32[]{:S(2)}) collective-permute-start(bf16[512,896]{1,0:T(8,128)(2,1)S(1)} %all_gather.3.mine), channel_id=1, source_target_pairs={{0,4},{4,0},{8,12},{12,8},{16,20},{20,16},{24,28},{28,24},{32,36},... | collective-permute-start | bytes 2752520 | tf_op jit(solution)/shard_map/ppermute | solution.py:44
  39.0 5.7 %collective-permute-start.4 = (bf16[3,240,384]{2,1,0:T(8,128)(2,1)S(1)}, bf16[3,240,384]{2,1,0:T(8,128)(2,1)S(1)}, u32[]{:S(2)}, u32[]{:S(2)}) collective-permute-start(bf16[3,240,384]{2,1,0:T(8,128)(2,1)S(1)} %pad_maximum_fusion), channel_id=1, source_target_pairs={{0,4},{4,0},{8,12},{12,8},{16,20},{20,16},{24,28},{28,24},{32,36},... | collective-permute-start | bytes 1658888 | tf_op jit(solution)/shard_map/ppermute | solution.py:44
  41.5 3.3 %copy-start.4 = (s32[1,1,128,8]{2,3,1,0:T(8,128)S(1)}, s32[1,1,128,8]{2,3,1,0:T(8,128)}, u32[]{:S(2)}) copy-start(s32[1,1,128,8]{2,3,1,0:T(8,128)} %param.20) | copy-start | bytes 12292
  48.1 37.3 %copy-start.5 = (s32[1,1,128,8]{2,3,1,0:T(8,128)S(1)}, s32[1,1,128,8]{2,3,1,0:T(8,128)}, u32[]{:S(2)}) copy-start(s32[1,1,128,8]{2,3,1,0:T(8,128)} %param.21) | copy-start | bytes 12292
  57.1 14.5 %collective-permute-start.5 = (bf16[4,8,512]{2,1,0:T(8,128)(2,1)S(1)}, bf16[4,8,512]{2,1,0:T(8,128)(2,1)S(1)}, u32[]{:S(2)}, u32[]{:S(2)}) collective-permute-start(bf16[4,8,512]{2,1,0:T(8,128)(2,1)S(1)} %get-tuple-element.63), channel_id=1, source_target_pairs={{0,64},{4,68},{8,72},{12,76},{16,80},{20,84},{24,88},{28,92},{32,9... | collective-permute-start | bytes 98312 | tf_op jit(solution)/shard_map/ppermute | solution.py:289
  66.3 5.3 %collective-permute-start.6 = (bf16[4,8,512]{2,1,0:T(8,128)(2,1)S(1)}, bf16[4,8,512]{2,1,0:T(8,128)(2,1)S(1)}, u32[]{:S(2)}, u32[]{:S(2)}) collective-permute-start(bf16[4,8,512]{2,1,0:T(8,128)(2,1)S(1)} %get-tuple-element.65), channel_id=1, source_target_pairs={{0,4},{4,8},{8,12},{12,16},{16,20},{20,24},{24,28},{28,32},{32,36}... | collective-permute-start | bytes 98312 | tf_op jit(solution)/shard_map/ppermute | solution.py:289
  68.2 5.8 %collective-permute-start.7 = (bf16[4,8,512]{2,1,0:T(8,128)(2,1)S(1)}, bf16[4,8,512]{2,1,0:T(8,128)(2,1)S(1)}, u32[]{:S(2)}, u32[]{:S(2)}) collective-permute-start(bf16[4,8,512]{2,1,0:T(8,128)(2,1)S(1)} %get-tuple-element.64), channel_id=1, source_target_pairs={{0,8},{4,12},{8,16},{12,20},{16,24},{20,28},{24,32},{28,36},{32,40... | collective-permute-start | bytes 98312 | tf_op jit(solution)/shard_map/ppermute | solution.py:289
  70.2 3.9 %collective-permute-start.8 = (bf16[4,8,512]{2,1,0:T(8,128)(2,1)S(1)}, bf16[4,8,512]{2,1,0:T(8,128)(2,1)S(1)}, u32[]{:S(2)}, u32[]{:S(2)}) collective-permute-start(bf16[4,8,512]{2,1,0:T(8,128)(2,1)S(1)} %get-tuple-element.66), channel_id=1, source_target_pairs={{2,258},{6,262},{10,266},{14,270},{18,274},{22,278},{26,282},{30,2... | collective-permute-start | bytes 98312 | tf_op jit(solution)/shard_map/ppermute | solution.py:289
  74.7 10.8 %all-to-all-start.1 = ((bf16[4,32,512]{2,1,0:T(8,128)(2,1)}), bf16[4,32,512]{2,1,0:T(8,128)(2,1)S(1)}, u32[]{:S(2)}, u32[]{:S(2)}) async-start(bf16[4,32,512]{2,1,0:T(8,128)(2,1)} %maximum_bitcast_fusion), calls=%async_computation.1 | async-start | bytes 262144 | tf_op jit(solution)/shard_map/all_to_all | solution.py:291
  86.2 12.9 %collective-permute-start.11 = (bf16[512,512]{1,0:T(8,128)(2,1)S(1)}, bf16[512,512]{1,0:T(8,128)(2,1)}, u32[]{:S(2)}, u32[]{:S(2)}) collective-permute-start(bf16[512,512]{1,0:T(8,128)(2,1)S(1)} %decode.1.rest_0_), channel_id=1, source_target_pairs={{0,4},{4,0},{8,12},{12,8},{16,20},{20,16},{24,28},{28,24},{32,36},... | collective-permute-start | bytes 1572872 | tf_op jit(solution)/shard_map/ppermute | solution.py:44
  88.2 16.2 %collective-permute-start.10 = (bf16[512,512]{1,0:T(8,128)(2,1)S(1)}, bf16[512,512]{1,0:T(8,128)(2,1)S(1)}, u32[]{:S(2)}, u32[]{:S(2)}) collective-permute-start(bf16[512,512]{1,0:T(8,128)(2,1)S(1)} %decode.1.rest_0_), channel_id=1, source_target_pairs={{0,504},{4,508},{8,0},{12,4},{16,8},{20,12},{24,16},{28,20},{32,24... | collective-permute-start | bytes 1572872 | tf_op jit(solution)/shard_map/ppermute | solution.py:38
  90.6 19.3 %collective-permute-start.9 = (bf16[512,512]{1,0:T(8,128)(2,1)S(1)}, bf16[512,512]{1,0:T(8,128)(2,1)S(1)}, u32[]{:S(2)}, u32[]{:S(2)}) collective-permute-start(bf16[512,512]{1,0:T(8,128)(2,1)S(1)} %decode.1.rest_0_), channel_id=1, source_target_pairs={{0,8},{4,12},{8,16},{12,20},{16,24},{20,28},{24,32},{28,36},{32,40... | collective-permute-start | bytes 1572872 | tf_op jit(solution)/shard_map/ppermute | solution.py:38
  109.9 13.8 %collective-permute-start.12 = (bf16[512,512]{1,0:T(8,128)(2,1)S(1)}, bf16[512,512]{1,0:T(8,128)(2,1)S(1)}, u32[]{:S(2)}, u32[]{:S(2)}) collective-permute-start(bf16[512,512]{1,0:T(8,128)(2,1)S(1)} %broadcast_select_fusion), channel_id=1, source_target_pairs={{0,508},{4,8},{8,4},{12,16},{16,12},{20,24},{24,20},{28,32},{32,28... | collective-permute-start | bytes 1572872 | tf_op jit(solution)/shard_map/ppermute | solution.py:44
  111.9 11.9 %collective-permute-start.13 = (bf16[512,512]{1,0:T(8,128)(2,1)S(1)}, bf16[512,512]{1,0:T(8,128)(2,1)S(1)}, u32[]{:S(2)}, u32[]{:S(2)}) collective-permute-start(bf16[512,512]{1,0:T(8,128)(2,1)S(1)} %collective-permute-done.9.rest_0_), channel_id=1, source_target_pairs={{0,4},{4,0},{8,12},{12,8},{16,20},{20,16},{24,28},{28,24},{32,36},... | collective-permute-start | bytes 1572872 | tf_op jit(solution)/shard_map/ppermute | solution.py:44
  113.8 10.0 %collective-permute-start.14 = (bf16[512,512]{1,0:T(8,128)(2,1)S(1)}, bf16[512,512]{1,0:T(8,128)(2,1)S(1)}, u32[]{:S(2)}, u32[]{:S(2)}) collective-permute-start(bf16[512,512]{1,0:T(8,128)(2,1)S(1)} %collective-permute-done.10.rest_1_), channel_id=1, source_target_pairs={{0,4},{4,0},{8,12},{12,8},{16,20},{20,16},{24,28},{28,24},{32,36},... | collective-permute-start | bytes 1572872 | tf_op jit(solution)/shard_map/ppermute | solution.py:44

commit v4 on v3

--- a/solution.py
+++ b/solution.py
@@ -11,8 +11,7 @@
 F32 = jnp.float32
 SENT = 240
 WIDE = 256
-SPLIT = 128
-FAR = ((16, 1, 2, None), (-16, -1, -2, None), (8, 4, 32, 64), (-8, -4, -32, None))
+FAR = ((None, 2, 1, 16), (None, -2, -1, -16), (64, 32, 4, 8), (None, -32, -4, -8))
 VMEM = pltpu.CompilerParams(vmem_limit_bytes=20 * 1024 * 1024)
 
 
@@ -57,7 +56,7 @@
     return lax.broadcasted_iota(jnp.int32, dims, axis).astype(jnp.int16)
 
 
-def pack_body(core, x, pack, up, down, three, own, hot):
+def pack_body(core, x, pack, three, up, down, own, hot):
     here = core[0]
     channels, rows = x.shape
     slots = pack.shape[-1]
@@ -77,49 +76,32 @@
     chosen((three, own), (jnp.where(here == 0, 0, 6), jnp.where(here == 0, 4, 2)))
 
 
-def weights_body(core, embed, edge, proc, dec, out, padded):
-    width = out.shape[0]
+def weights_body(embed, edge, proc, dec, out, padded):
+    copies, width, columns = out.shape
     eye = one_hot(
         positions((width, width), 0), lax.broadcasted_iota(jnp.int32, (width, width), 1)
     )
-
-    def turn(piece, at):
-        out[:, at : at + piece.shape[0]] = mul_nt(eye, piece).astype(BF16)
-
-    @pl.when(core[0] == 0)
-    def _():
-        padded[...] = jnp.zeros_like(padded)
-        padded[0 : embed.shape[0], :] = embed[...]
-        turn(padded[...], 0)
-        turn(edge[...], WIDE)
-        turn(proc[0:SPLIT, :], WIDE + edge.shape[0])
-
-    @pl.when(core[0] != 0)
-    def _():
-        turn(proc[SPLIT:, :], 0)
-        turn(dec[...], proc.shape[0] - SPLIT)
-
-
-def prepare_body(core, mine, other, x, edges, latent, *rest):
-    *tables, padded = rest
+    padded[...] = jnp.zeros_like(padded)
+    padded[0 : embed.shape[0], :] = embed[...]
+    at = 0
+    for piece in (padded, edge, proc, dec):
+        turned = mul_nt(eye, piece[...]).astype(BF16)
+        for i in range(copies):
+            out[i, :, at : at + piece.shape[0]] = turned
+        at += piece.shape[0]
+
+
+def tables_body(core, edges, *tables):
     is_even = core[0] == 0
-    channels, rows = x.shape
-    padded[...] = jnp.zeros_like(padded)
-    padded[0:channels, :] = x[...]
-    w_embed = jnp.where(is_even, mine[:, 0:WIDE], other[:, 0:WIDE])
-    latent[...] = silu(
-        lax.dot_general(
-            padded[...], w_embed, (((0,), (1,)), ((), ())), preferred_element_type=F32
-        )
-    ).astype(BF16)
+    rows = edges.shape[1]
     order = (
         3,
         jnp.where(is_even, 4, 2),
-        1,
-        5,
+        jnp.where(is_even, 5, 1),
+        jnp.where(is_even, 1, 5),
         jnp.where(is_even, 0, 6),
-        jnp.where(is_even, 2, 0),
-        jnp.where(is_even, 6, 4),
+        jnp.where(is_even, 2, 4),
+        jnp.where(is_even, 6, 0),
     )
     count = edges.shape[0]
     spare = jnp.zeros((8 - count, rows), jnp.int32)
@@ -164,38 +146,38 @@
 
 
 def early_body(
-    core, x, pack, up, down, three, mine, other, recv, embed, out, rows, sent, hot, padded
+    core, x, pack, up, down, three, weights, recv, embed, out, rows, sent, hot, padded, near, arrived
 ):
     is_even = core[0] == 0
     nodes, channels = embed.shape
+    fetch = pltpu.make_async_copy(embed, near, arrived)
+    fetch.start()
     slots = recv.shape[-1]
-    w_embed = jnp.where(is_even, mine[:, 0:SENT], other[:, 0:SENT])
-    w_edge = jnp.where(is_even, mine[:, WIDE : WIDE + channels], other[:, WIDE : WIDE + channels])
+    w_embed = weights[:, 0:SENT]
+    w_edge = weights[:, WIDE : WIDE + channels]
     padded[...] = jnp.zeros_like(padded)
     padded[0 : x.shape[0], :] = x[...]
     local = mul(padded[...], one_hot(positions((x.shape[1], slots), 0), pack[3])).astype(BF16)
     messages((local, up[0], down[0], three[...]), w_embed, w_edge, rows, sent)
     receivers(recv, (3, 5, 1, jnp.where(is_even, 6, 0)), hot)
-    out[...] = embed[...].astype(F32) + mul_nt(hot[...], sent[...])
+    total = mul_nt(hot[...], sent[...])
+    fetch.wait()
+    out[...] = near[...].astype(F32) + total
 
 
 def encode_body(
-    core, here, early, sib, mine, other, recv, far_ids, latent, message, far, rows, sent, hot
+    core, here, early, sib, weights, recv, far_ids, latent, message, far, rows, sent, hot
 ):
     is_even = core[0] == 0
     nodes, channels = early.shape
-    w_embed = jnp.where(is_even, mine[:, 0:SENT], other[:, 0:SENT])
-    w_edge = jnp.where(is_even, mine[:, WIDE : WIDE + channels], other[:, WIDE : WIDE + channels])
-    first = WIDE + channels
-    low = jnp.where(is_even, mine[:, first : first + SPLIT], other[:, first : first + SPLIT])
-    rest = channels - SPLIT
-    high = jnp.where(is_even, other[:, 0:rest], mine[:, 0:rest])
-    w_proc = jnp.concatenate([low, high], axis=1)
+    w_embed = weights[:, 0:SENT]
+    w_edge = weights[:, WIDE : WIDE + channels]
     messages((sib[0], sib[1], sib[2]), w_embed, w_edge, rows, sent)
     offsets = (jnp.where(is_even, 2, 4), jnp.where(is_even, 4, 6), jnp.where(is_even, 0, 2))
     receivers(recv, offsets, hot)
     rounded = (early[...] + mul_nt(hot[...], sent[...])).astype(BF16)
     latent[...] = rounded
+    w_proc = weights[:, WIDE + channels : WIDE + 2 * channels]
     made = silu(mul_nt(rounded, w_proc)).astype(BF16)
     message[...] = made
     far[...] = mul(far_table(far_ids, here[0], 1, nodes), made).astype(BF16)
@@ -216,6 +198,18 @@
     return jnp.concatenate(pieces, axis=0).astype(BF16)
 
 
+def own_body(weights, x, block, table, out, padded):
+    channels = x.shape[0]
+    padded[...] = jnp.zeros_like(padded)
+    padded[0:channels, :] = x[...]
+    grid = silu(
+        lax.dot_general(
+            padded[...], weights[:, 0:WIDE], (((0,), (1,)), ((), ())), preferred_element_type=F32
+        )
+    ).astype(BF16)
+    out[...] = grid.astype(F32) + mul(table[...], block[...])
+
+
 def local_body(latent, message, neighbours, out):
     nodes = latent.shape[0]
     count = neighbours.shape[0]
@@ -228,10 +222,9 @@
     out[...] = latent[...].astype(F32) + mul(table.astype(BF16), message[...])
 
 
-def decode_body(core, here, base, far_ids, arrived, mine, other, out):
+def decode_body(here, base, far_ids, arrived, weights, out):
     nodes, channels = base.shape
-    at = channels - SPLIT
-    w_dec = jnp.where(core[0] == 0, other[:, at : at + channels], mine[:, at : at + channels])
+    w_dec = weights[:, WIDE + 2 * channels :]
     hot = far_table(far_ids, here[0], -1, nodes)
     after = (base[...] + mul_tn(hot, arrived[...])).astype(BF16)
     out[...] = silu(mul_nt(after, w_dec)).astype(BF16)
@@ -245,9 +238,11 @@
     out[...] = (before[...].astype(F32) + mul(table[...], joined[...])).astype(out.dtype)
 
 
-def call(body, out_shape, args, scratch=(), name=None, stored=()):
+def call(body, out_shape, args, scratch=(), name=None, stored=(), far_off=()):
     near = len(args)
-    args = (*args, *stored)
+    last = near + len(stored)
+    args = (*args, *stored, *far_off)
+    hbm = pl.BlockSpec(memory_space=pltpu.HBM)
     smem = pl.BlockSpec(memory_space=pltpu.SMEM)
     vmem = pl.BlockSpec(memory_space=pltpu.VMEM)
     many = isinstance(out_shape, (list, tuple))
@@ -258,7 +253,9 @@
     return pl.pallas_call(
         body,
         out_shape=out_shape,
-        in_specs=[smem if a.ndim == 1 else vmem for a in args],
+        in_specs=[
+            smem if a.ndim == 1 else hbm if i >= last else vmem for i, a in enumerate(args)
+        ],
         out_specs=[vmem for _ in out_shape] if many else vmem,
         scratch_shapes=scratch,
         compiler_params=VMEM,
@@ -328,47 +325,53 @@
     pair = shape(2, SENT, slots)
     padded = pltpu.VMEM((SENT, rows), BF16)
 
-    up, down, three, own = call(
+    width = w_edge.shape[1]
+    chans = lax.axis_size("chan")
+    copies = call(
+        weights_body,
+        stored(chans, width, WIDE + 3 * channels),
+        (),
+        [pltpu.VMEM((WIDE, width), BF16)],
+        name="weights",
+        stored=(w_embed, w_edge, w_proc, w_dec),
+    )
+    copies, x, edges = lax.optimization_barrier((copies, x, dec_edge.T))
+    weights = lax.all_to_all(copies, "chan", 0, 0, tiled=True).reshape(chans * width, -1)
+    three, up, down, own = call(
         pack_body,
-        [pair, pair, block, block],
+        [block, pair, pair, block],
         (core,),
         [pltpu.VMEM((rows, 2 * slots), BF16)],
         name="pack",
         stored=(x, pack),
     )
-    up, down, three, own, w_embed, w_edge, w_proc, w_dec = lax.optimization_barrier(
-        (up, down, three, own, w_embed, w_edge, w_proc, w_dec)
-    )
     three = by_core(three, -3, 3)
     up = shifted(up, 2)
     down = shifted(down, -2)
-    shard = call(
-        weights_body,
-        shape(w_edge.shape[1], (WIDE + 3 * channels) // 2),
+    own_table, near_table, late_table = call(
+        tables_body,
+        [stored(rows, n * nodes) for n in (1, 3, 3)],
         (core,),
-        [pltpu.VMEM((WIDE, w_edge.shape[1]), BF16)],
-        name="weights",
-        stored=(w_embed, w_edge, w_proc, w_dec),
-    )
-    mine = lax.all_gather(shard, "chan", axis=0, tiled=True)
-    mine, up, down, three = lax.optimization_barrier((mine, up, down, three))
+        name="tables",
+        stored=(edges,),
+    )
+    up, down, three, own_table = lax.optimization_barrier((up, down, three, own_table))
     sib = by_core(jnp.stack([own, up[1], down[1]]), 1, -1)
-    other = by_core(mine, 1, -1)
     early = call(
         early_body,
         shape(nodes, channels, kind=F32),
-        (core, x, pack, up, down, three, mine, other, recv, mesh_embed),
-        [*work(4), padded],
+        (core, x, pack, up, down, three, weights, recv),
+        [*work(4), padded, pltpu.VMEM((nodes, channels), BF16), pltpu.SemaphoreType.DMA],
         name="early",
+        far_off=(mesh_embed,),
     )
     mesh_latent, node_msg, far_sent = call(
         encode_body,
         [stored(nodes, channels), stored(nodes, channels), shape(8 * 16, channels)],
-        (core, here, early, sib, mine, other, recv, far_out_ids),
+        (core, here, early, sib, weights, recv, far_out_ids),
         [*work(3)],
         name="encode",
     )
-    arrived = far_exchange(far_sent)
     base = call(
         local_body,
         shape(nodes, channels, kind=F32),
@@ -376,23 +379,12 @@
         name="short",
         stored=(mesh_latent, node_msg, loc_nbr.T),
     )
+    arrived = far_exchange(far_sent)
     dec_msg = call(
         decode_body,
         shape(nodes, channels),
-        (core, here, base, far_in_ids, arrived, mine, other),
+        (here, base, far_in_ids, arrived, weights),
         name="decode",
-    )
-    up = shifted(dec_msg, 2)
-    down = shifted(dec_msg, -2)
-    sib = by_core(dec_msg, 1, -1)
-    dec_msg, x, edges = lax.optimization_barrier((dec_msg, x, dec_edge.T))
-    latent, own_table, near_table, late_table = call(
-        prepare_body,
-        [shape(rows, channels)] + [shape(rows, n * nodes) for n in (2, 2, 3)],
-        (core, mine, other),
-        [pltpu.VMEM((WIDE, rows), BF16)],
-        name="prepare",
-        stored=(x, edges),
     )
 
     def added(name, before, blocks, table, kind=F32):
@@ -404,13 +396,22 @@
             name=name,
         )
 
-    total = added("own", latent, (dec_msg, sib), own_table)
-    up, down, total = lax.optimization_barrier((up, down, total))
-    three = by_core(jnp.where(core[0] == 0, down, up), -1, 1)
-    relay_up = by_core(up, 1, -1)
-    relay_down = by_core(down, 1, -1)
-    total = added("near", total, (up, down), near_table)
-    return added("collect", total, (three, relay_up, relay_down), late_table, BF16)
+    second = by_core(dec_msg, 2, -2)
+    first = by_core(dec_msg, -2, 2)
+    sib = by_core(dec_msg, 1, -1)
+    total = call(
+        own_body,
+        shape(rows, channels, kind=F32),
+        (weights, x, dec_msg, own_table),
+        [pltpu.VMEM((WIDE, rows), BF16)],
+        name="own",
+    )
+    first, total = lax.optimization_barrier((first, total))
+    three = by_core(first, -1, 1)
+    relay_first = by_core(first, 1, -1)
+    relay_second = by_core(second, 1, -1)
+    total = added("near", total, (sib, first, second), near_table)
+    return added("collect", total, (three, relay_first, relay_second), late_table, BF16)
 
 
 def solution(mesh):

time: 127 us -> 120 us (0.945)
  blocking collectives: 22.9 us -> 9.23 us
  starting transfers between devices: 57.2 us -> 61.7 us
  Pallas kernels: 25.1 us -> 29.4 us
  waiting for transfers between devices: 20.1 us -> 17.3 us
    all_gather x1 -> x0, blocking collectives: 14 us -> none  [shards(): mine = lax.all_gather(shard, 'chan', axis=0, tiled=True)]
    ppermute x4 -> x2, starting transfers between devices: 21.5 us -> 11.1 us  [shifted(): lax.ppermute(value, 'patch', [(i, (i + steps) % count) for i in range(cou...]
    all_to_all x0 -> x1, starting transfers between devices: none -> 9.37 us  [shards(): lax.all_to_all(copies, 'chan', 0, 0, tiled=True).reshape(chans * width, -1)]
    ppermute x4 -> x2, waiting for transfers between devices: 8.41 us -> 0.01 us  [shifted(): lax.ppermute(value, 'patch', [(i, (i + steps) % count) for i in range(cou...]
    ppermute x7 -> x8, waiting for transfers between devices: 6.31 us -> 14.3 us  [by_core(): return lax.ppermute(value, 'patch', pairs)]
    pallas_call x10, Pallas kernels: 25.1 us -> 29.4 us  [call(): pl.pallas_call(body, out_shape=out_shape, in_specs=[smem if a.ndim == 1 e...]
    ppermute x7 -> x8, starting transfers between devices: 15.7 us -> 18.9 us  [by_core(): return lax.ppermute(value, 'patch', pairs)]
    ppermute x4, waiting for transfers between devices: 3.21 us -> 0.89 us  [far_exchange(): arrived.append(lax.ppermute(mine[:, kind], ('patch', 'chan'), pairs))]
  transfers between devices with their start and end apart: 16 -> 16, of which waited for: 6 -> 5; matrix products, arithmetic and copies ran while one was open for 0% -> 1% of each run, Pallas kernels for 12% -> 16%
where the time goes in v4:
time: 120 us
  starting transfers between devices  61.7 us (51%)
  Pallas kernels  29.4 us (24%)
  waiting for transfers between devices  17.3 us (14%)
  blocking collectives  9.23 us (8%)
  other arithmetic  1.57 us (1%)
    pallas_call x10, Pallas kernels, call(): pl.pallas_call(body, out_shape=out_shape, in_specs=[smem if a.ndim == 1 e...  29.4 us
    ppermute x8, starting transfers between devices, by_core(): return lax.ppermute(value, 'patch', pairs)  18.9 us
    ppermute x4, starting transfers between devices, far_exchange(): arrived.append(lax.ppermute(mine[:, kind], ('patch', 'chan'), pairs))  15.2 us
    ppermute x8, waiting for transfers between devices, by_core(): return lax.ppermute(value, 'patch', pairs)  14.3 us
    ppermute x2, starting transfers between devices, shifted(): lax.ppermute(value, 'patch', [(i, (i + steps) % count) for i in range(cou...  11.1 us
    all_to_all x1, starting transfers between devices, shards(): lax.all_to_all(copies, 'chan', 0, 0, tiled=True).reshape(chans * width, -1)  9.37 us
    all_to_all x1, blocking collectives, far_exchange(): lax.all_to_all(rows.reshape(chans, kinds * each, channels), 'chan', 0, 0,...  9.23 us
    all_to_all x1, starting transfers between devices, far_exchange(): lax.all_to_all(back, 'chan', 0, 0, tiled=True).reshape(count, channels)  7.09 us
  transfers between devices with their start and end apart: 16, of which 5 were waited for; matrix products, arithmetic and copies ran while one was open for 1% of the time, Pallas kernels for 16%

profile of v4, /device:TPU:8, one launch (start us, length us, event | category | flops | bytes accessed | tf_op | source)
XLA Modules:
  0.0 119.5 jit_solution(2226616997651432707)
XLA Ops:
  0.0 2.6 %weights.1 = bf16[4,128,1792]{2,1,0:T(8,128)(2,1)} custom-call(bf16[227,128]{1,0:T(8,128)(2,1)} %embed.2, bf16[512,128]{1,0:T(8,128)(2,1)} %edge.1, bf16[512,128]{1,0:T(8,128)(2,1)} %proc.1, bf16[512,128]{1,0:T(8,128)(2,1)} %dec.1), custom_call_target="tpu_custom_call" | custom-call | tf_op jit(solution)/shard_map/weights/pallas_call | solution.py:253
  2.6 9.4 %all-to-all-start = ((bf16[4,128,1792]{2,1,0:T(8,128)(2,1)}), bf16[4,128,1792]{2,1,0:T(8,128)(2,1)S(1)}, u32[]{:S(2)}, u32[]{:S(2)}) async-start(bf16[4,128,1792]{2,1,0:T(8,128)(2,1)} %weights.1), calls=%async_computation | async-start | bytes 3670016 | tf_op jit(solution)/shard_map/all_to_all | solution.py:339
  12.0 0.0 copy-start
  12.0 0.0 copy-start.4
  12.0 0.0 copy-start.5
  12.0 2.8 %pack.1 = (bf16[240,384]{1,0:T(8,128)(2,1)S(1)}, bf16[2,240,384]{2,1,0:T(8,128)(2,1)S(1)}, bf16[2,240,384]{2,1,0:T(8,128)(2,1)S(1)}, bf16[240,384]{1,0:T(8,128)(2,1)S(1)}) custom-call(s32[1]{0:T(128)} %bitcast.1.core, bf16[227,1024]{1,0:T(8,128)(2,1)} %bitcast.44, s32[7,1,384]{2,1,0:T(1,128)} %bitcast.52), custom_call_target="tpu_custom_call" | custom-call | tf_op jit(solution)/shard_map/pack/pallas_call | solution.py:253
  14.8 1.9 %collective-permute-start = (bf16[2,240,384]{2,1,0:T(8,128)(2,1)S(1)}, bf16[2,240,384]{2,1,0:T(8,128)(2,1)S(1)}, u32[]{:S(2)}, u32[]{:S(2)}) collective-permute-start(bf16[2,240,384]{2,1,0:T(8,128)(2,1)S(1)} %get-tuple-element.25), channel_id=1, source_target_pairs={{0,8},{4,12},{8,16},{12,20},{16,24},{20,28},{24,32},{28,36},{32,40... | collective-permute-start | bytes 1105928 | tf_op jit(solution)/shard_map/ppermute | solution.py:37
  16.7 9.1 %collective-permute-start.1 = (bf16[2,240,384]{2,1,0:T(8,128)(2,1)S(1)}, bf16[2,240,384]{2,1,0:T(8,128)(2,1)S(1)}, u32[]{:S(2)}, u32[]{:S(2)}) collective-permute-start(bf16[2,240,384]{2,1,0:T(8,128)(2,1)S(1)} %get-tuple-element.26), channel_id=1, source_target_pairs={{0,504},{4,508},{8,0},{12,4},{16,8},{20,12},{24,16},{28,20},{32,24... | collective-permute-start | bytes 1105928 | tf_op jit(solution)/shard_map/ppermute | solution.py:37
  25.8 2.7 %collective-permute-start.2 = (bf16[240,384]{1,0:T(8,128)(2,1)S(1)}, bf16[240,384]{1,0:T(8,128)(2,1)S(1)}, u32[]{:S(2)}, u32[]{:S(2)}) collective-permute-start(bf16[240,384]{1,0:T(8,128)(2,1)S(1)} %get-tuple-element.27), channel_id=1, source_target_pairs={{0,500},{4,16},{8,508},{12,24},{16,4},{20,32},{24,12},{28,40},{32,... | collective-permute-start | bytes 552968 | tf_op jit(solution)/shard_map/ppermute | solution.py:43
  28.5 7.2 %tables.1 = (bf16[1024,512]{1,0:T(8,128)(2,1)}, bf16[1024,1536]{1,0:T(8,128)(2,1)}, bf16[1024,1536]{1,0:T(8,128)(2,1)}) custom-call(s32[1]{0:T(128)} %bitcast.1.core, s32[3,1024]{1,0:T(4,128)} %bitcast.62), custom_call_target="tpu_custom_call" | custom-call | tf_op jit(solution)/shard_map/tables/pallas_call | solution.py:253
  35.7 2.6 %collective-permute-done.2.three = bf16[240,384]{1,0:T(8,128)(2,1)S(1)} collective-permute-done((bf16[240,384]{1,0:T(8,128)(2,1)S(1)}, bf16[240,384]{1,0:T(8,128)(2,1)S(1)}, u32[]{:S(2)}, u32[]{:S(2)}) %collective-permute-start.2) | collective-permute-done | bytes 184352 | tf_op jit(solution)/shard_map/ppermute | solution.py:43
  38.3 0.0 collective-permute-done.up
  38.3 0.0 collective-permute-done.1.down
  38.4 0.9 pad_maximum_fusion
  39.3 1.9 %collective-permute-start.3 = (bf16[3,240,384]{2,1,0:T(8,128)(2,1)}, bf16[3,240,384]{2,1,0:T(8,128)(2,1)}, u32[]{:S(2)}, u32[]{:S(2)}) collective-permute-start(bf16[3,240,384]{2,1,0:T(8,128)(2,1)} %pad_maximum_fusion), channel_id=1, source_target_pairs={{0,4},{4,0},{8,12},{12,8},{16,20},{20,16},{24,28},{28,24},{32,36},... | collective-permute-start | bytes 1658888 | tf_op jit(solution)/shard_map/ppermute | solution.py:43
  41.2 0.0 all-to-all-done
  41.2 0.0 copy-done
  41.2 0.0 copy-done.4
  41.3 0.0 copy-done.5
  41.3 0.0 copy-start.6
  41.3 3.7 %early.1 = f32[512,512]{1,0:T(8,128)S(1)} custom-call(s32[1]{0:T(128)} %bitcast.1.core, bf16[227,1024]{1,0:T(8,128)(2,1)S(1)} %bitcast.45, s32[7,1,384]{2,1,0:T(1,128)S(1)} %bitcast.53, bf16[2,240,384]{2,1,0:T(8,128)(2,1)S(1)} %collective-permute-done.up, bf16[2,240,384]{2,1,0:T(8,128)(2,1)S(1)} %collective-permute-done.1.down, ...), custom_call_target="tpu_custom_call" | custom-call | tf_op jit(solution)/shard_map/early/pallas_call | solution.py:253
  44.9 0.0 collective-permute-done.3.sib
  44.9 0.0 copy-done.6
  45.0 4.3 %encode.1 = (bf16[512,512]{1,0:T(8,128)(2,1)}, bf16[512,512]{1,0:T(8,128)(2,1)}, bf16[128,512]{1,0:T(8,128)(2,1)S(1)}) custom-call(s32[1]{0:T(128)} %bitcast.1.core, s32[1]{0:T(128)} %bitcast.here, f32[512,512]{1,0:T(8,128)S(1)} %early.1, bf16[3,240,384]{2,1,0:T(8,128)(2,1)} %collective-permute-done.3.sib, bf16[512,1792]{1,0:T(8,128)(2,1)S(1)} %bitcast.41, ...), custom_call_target="tpu_custom_call" | custom-call | tf_op jit(solution)/shard_map/encode/pallas_call | solution.py:253
  49.3 0.0 copy-start.7
  49.3 9.2 %all_to_all.15 = bf16[4,32,512]{2,1,0:T(8,128)(2,1)S(1)} all-to-all(bf16[4,32,512]{2,1,0:T(8,128)(2,1)S(1)} %bitcast.49), channel_id=1, replica_groups=mesh['patch'=128,'chan'=4] {'chan'}, dimensions={0} | all-to-all | bytes 262144 | tf_op jit(solution)/shard_map/all_to_all | solution.py:275
  58.5 8.4 %collective-permute-start.7 = (bf16[4,8,512]{2,1,0:T(8,128)(2,1)S(1)}, bf16[4,8,512]{2,1,0:T(8,128)(2,1)S(1)}, u32[]{:S(2)}, u32[]{:S(2)}) collective-permute-start(bf16[4,8,512]{2,1,0:T(8,128)(2,1)S(1)} %get-tuple-element.46), channel_id=1, source_target_pairs={{0,64},{4,68},{8,72},{12,76},{16,80},{20,84},{24,88},{28,92},{32,9... | collective-permute-start | bytes 98312 | tf_op jit(solution)/shard_map/ppermute | solution.py:286
  66.9 1.9 %collective-permute-start.6 = (bf16[4,8,512]{2,1,0:T(8,128)(2,1)S(1)}, bf16[4,8,512]{2,1,0:T(8,128)(2,1)S(1)}, u32[]{:S(2)}, u32[]{:S(2)}) collective-permute-start(bf16[4,8,512]{2,1,0:T(8,128)(2,1)S(1)} %get-tuple-element.44), channel_id=1, source_target_pairs={{0,4},{4,8},{8,12},{12,16},{16,20},{20,24},{24,28},{28,32},{32,36}... | collective-permute-start | bytes 98312 | tf_op jit(solution)/shard_map/ppermute | solution.py:286
  68.9 4.2 %collective-permute-start.5 = (bf16[4,8,512]{2,1,0:T(8,128)(2,1)S(1)}, bf16[4,8,512]{2,1,0:T(8,128)(2,1)S(1)}, u32[]{:S(2)}, u32[]{:S(2)}) collective-permute-start(bf16[4,8,512]{2,1,0:T(8,128)(2,1)S(1)} %get-tuple-element.45), channel_id=1, source_target_pairs={{0,8},{4,12},{8,16},{12,20},{16,24},{20,28},{24,32},{28,36},{32,40... | collective-permute-start | bytes 98312 | tf_op jit(solution)/shard_map/ppermute | solution.py:286
  73.1 0.7 collective-permute-start.4
  73.8 0.0 collective-permute-done.7
  73.8 0.0 collective-permute-done.6
  73.8 0.9 collective-permute-done.5
  74.7 0.0 collective-permute-done.4
  74.7 0.7 maximum_bitcast_fusion
  75.3 7.1 %all-to-all-start.2 = ((bf16[4,32,512]{2,1,0:T(8,128)(2,1)}), bf16[4,32,512]{2,1,0:T(8,128)(2,1)S(1)}, u32[]{:S(2)}, u32[]{:S(2)}) async-start(bf16[4,32,512]{2,1,0:T(8,128)(2,1)} %maximum_bitcast_fusion), calls=%async_computation.2 | async-start | bytes 262144 | tf_op jit(solution)/shard_map/all_to_all | solution.py:288
  82.4 2.4 %short.1.base = f32[512,512]{1,0:T(8,128)S(1)} custom-call(bf16[512,512]{1,0:T(8,128)(2,1)} %get-tuple-element.35.latent, bf16[512,512]{1,0:T(8,128)(2,1)} %get-tuple-element.36.message, s32[6,512]{1,0:T(8,128)} %bitcast.61), custom_call_target="tpu_custom_call" | custom-call | tf_op jit(solution)/shard_map/short/pallas_call | solution.py:253
  84.8 2.1 %all-to-all-done.2 = bf16[4,32,512]{2,1,0:T(8,128)(2,1)S(1)} async-done(((bf16[4,32,512]{2,1,0:T(8,128)(2,1)}), bf16[4,32,512]{2,1,0:T(8,128)(2,1)S(1)}, u32[]{:S(2)}, u32[]{:S(2)}) %all-to-all-start.2) | async-done | bytes 131104 | tf_op jit(solution)/shard_map/all_to_all | solution.py:288
  87.0 0.0 copy-start.3
  87.0 0.0 copy-done.7
  87.0 0.7 decode.1.block
  87.7 0.0 copy-start.1
  87.7 4.0 %collective-permute-start.8 = (bf16[512,512]{1,0:T(8,128)(2,1)S(1)}, bf16[512,512]{1,0:T(8,128)(2,1)S(1)}, u32[]{:S(2)}, u32[]{:S(2)}) collective-permute-start(bf16[512,512]{1,0:T(8,128)(2,1)S(1)} %decode.1.block), channel_id=1, source_target_pairs={{0,504},{4,12},{8,0},{12,20},{16,8},{20,28},{24,16},{28,36},{32,24... | collective-permute-start | bytes 1572872 | tf_op jit(solution)/shard_map/ppermute | solution.py:43
  91.7 2.1 %collective-permute-start.10 = (bf16[512,512]{1,0:T(8,128)(2,1)S(1)}, bf16[512,512]{1,0:T(8,128)(2,1)S(1)}, u32[]{:S(2)}, u32[]{:S(2)}) collective-permute-start(bf16[512,512]{1,0:T(8,128)(2,1)S(1)} %decode.1.block), channel_id=1, source_target_pairs={{0,8},{4,508},{8,16},{12,4},{16,24},{20,12},{24,32},{28,20},{32,40... | collective-permute-start | bytes 1572872 | tf_op jit(solution)/shard_map/ppermute | solution.py:43
  93.8 2.0 %collective-permute-start.9 = (bf16[512,512]{1,0:T(8,128)(2,1)S(1)}, bf16[512,512]{1,0:T(8,128)(2,1)S(1)}, u32[]{:S(2)}, u32[]{:S(2)}) collective-permute-start(bf16[512,512]{1,0:T(8,128)(2,1)S(1)} %decode.1.block), channel_id=1, source_target_pairs={{0,4},{4,0},{8,12},{12,8},{16,20},{20,16},{24,28},{28,24},{32,36},... | collective-permute-start | bytes 1572872 | tf_op jit(solution)/shard_map/ppermute | solution.py:43
  95.8 0.0 copy-done.3
  95.8 1.2 own.1.before
  97.0 5.9 %collective-permute-done.8.rest_1_ = bf16[512,512]{1,0:T(8,128)(2,1)S(1)} collective-permute-done((bf16[512,512]{1,0:T(8,128)(2,1)S(1)}, bf16[512,512]{1,0:T(8,128)(2,1)S(1)}, u32[]{:S(2)}, u32[]{:S(2)}) %collective-permute-start.8) | collective-permute-done | bytes 524320 | tf_op jit(solution)/shard_map/ppermute | solution.py:43
  102.9 1.9 %collective-permute-start.11 = (bf16[512,512]{1,0:T(8,128)(2,1)S(1)}, bf16[512,512]{1,0:T(8,128)(2,1)S(1)}, u32[]{:S(2)}, u32[]{:S(2)}) collective-permute-start(bf16[512,512]{1,0:T(8,128)(2,1)S(1)} %collective-permute-done.8.rest_1_), channel_id=1, source_target_pairs={{0,508},{4,8},{8,4},{12,16},{16,12},{20,24},{24,20},{28,32},{32,28... | collective-permute-start | bytes 1572872 | tf_op jit(solution)/shard_map/ppermute | solution.py:43
  104.9 1.9 %collective-permute-start.12 = (bf16[512,512]{1,0:T(8,128)(2,1)S(1)}, bf16[512,512]{1,0:T(8,128)(2,1)S(1)}, u32[]{:S(2)}, u32[]{:S(2)}) collective-permute-start(bf16[512,512]{1,0:T(8,128)(2,1)S(1)} %collective-permute-done.8.rest_1_), channel_id=1, source_target_pairs={{0,4},{4,0},{8,12},{12,8},{16,20},{20,16},{24,28},{28,24},{32,36},... | collective-permute-start | bytes 1572872 | tf_op jit(solution)/shard_map/ppermute | solution.py:43
  106.8 0.0 collective-permute-done.10.rest_2_
  106.8 2.4 %collective-permute-start.13 = (bf16[512,512]{1,0:T(8,128)(2,1)S(1)}, bf16[512,512]{1,0:T(8,128)(2,1)S(1)}, u32[]{:S(2)}, u32[]{:S(2)}) collective-permute-start(bf16[512,512]{1,0:T(8,128)(2,1)S(1)} %collective-permute-done.10.rest_2_), channel_id=1, source_target_pairs={{0,4},{4,0},{8,12},{12,8},{16,20},{20,16},{24,28},{28,24},{32,36},... | collective-permute-start | bytes 1572872 | tf_op jit(solution)/shard_map/ppermute | solution.py:43
  109.2 0.0 collective-permute-done.9.rest_0_
  109.2 0.0 copy-done.1
  109.2 0.0 copy-start.2
  109.2 1.8 %near.1.before = f32[1024,512]{1,0:T(8,128)S(1)} custom-call(f32[1024,512]{1,0:T(8,128)S(1)} %own.1.before, bf16[512,512]{1,0:T(8,128)(2,1)S(1)} %collective-permute-done.9.rest_0_, bf16[512,512]{1,0:T(8,128)(2,1)S(1)} %collective-permute-done.8.rest_1_, bf16[512,512]{1,0:T(8,128)(2,1)S(1)} %collective-permute-done.10.rest_2_, bf16[1024,1536]{1,0:T(8,128)(2,1)S(1)} %copy-done.1), custom_call_target="tpu_custom_call" | custom-call | tf_op jit(solution)/shard_map/near/pallas_call | solution.py:253
  111.0 5.7 %collective-permute-done.11.rest_0_ = bf16[512,512]{1,0:T(8,128)(2,1)S(1)} collective-permute-done((bf16[512,512]{1,0:T(8,128)(2,1)S(1)}, bf16[512,512]{1,0:T(8,128)(2,1)S(1)}, u32[]{:S(2)}, u32[]{:S(2)}) %collective-permute-start.11) | collective-permute-done | bytes 524320 | tf_op jit(solution)/shard_map/ppermute | solution.py:43
  116.7 0.0 collective-permute-done.12.rest_1_
  116.7 0.0 collective-permute-done.13.rest_2_
  116.7 0.0 copy-done.2
  116.8 2.8 %collect.1 = bf16[1024,512]{1,0:T(8,128)(2,1)} custom-call(f32[1024,512]{1,0:T(8,128)S(1)} %near.1.before, bf16[512,512]{1,0:T(8,128)(2,1)S(1)} %collective-permute-done.11.rest_0_, bf16[512,512]{1,0:T(8,128)(2,1)S(1)} %collective-permute-done.12.rest_1_, bf16[512,512]{1,0:T(8,128)(2,1)S(1)} %collective-permute-done.13.rest_2_, bf16[1024,1536]{1,0:T(8,128)(2,1)S(1)} %copy-done.2), custom_call_target="tpu_custom_call" | custom-call | tf_op jit(solution)/shard_map/collect/pallas_call | solution.py:253
  (3 shorter events, 0.0 us)
Async XLA Ops:
  2.6 38.6 %all-to-all-start = ((bf16[4,128,1792]{2,1,0:T(8,128)(2,1)}), bf16[4,128,1792]{2,1,0:T(8,128)(2,1)S(1)}, u32[]{:S(2)}, u32[]{:S(2)}) async-start(bf16[4,128,1792]{2,1,0:T(8,128)(2,1)} %weights.1), calls=%async_computation | async-start | bytes 3670016 | tf_op jit(solution)/shard_map/all_to_all | solution.py:339
  12.0 29.2 %copy-start = (bf16[1024,227]{0,1:T(8,128)(2,1)S(1)}, bf16[1024,227]{0,1:T(8,128)(2,1)}, u32[]{:S(2)}) copy-start(bf16[1024,227]{0,1:T(8,128)(2,1)} %param.12) | copy-start | bytes 1394692
  12.0 29.3 %copy-start.4 = (s32[1,1,7,384]{3,1,2,0:T(1,128)S(1)}, s32[1,1,7,384]{3,1,2,0:T(1,128)}, u32[]{:S(2)}) copy-start(s32[1,1,7,384]{3,1,2,0:T(1,128)} %param.19) | copy-start | bytes 32260
  12.0 29.3 %copy-start.5 = (s32[1,1,7,384]{3,1,2,0:T(1,128)S(1)}, s32[1,1,7,384]{3,1,2,0:T(1,128)}, u32[]{:S(2)}) copy-start(s32[1,1,7,384]{3,1,2,0:T(1,128)} %param.18) | copy-start | bytes 32260
  14.8 23.6 %collective-permute-start = (bf16[2,240,384]{2,1,0:T(8,128)(2,1)S(1)}, bf16[2,240,384]{2,1,0:T(8,128)(2,1)S(1)}, u32[]{:S(2)}, u32[]{:S(2)}) collective-permute-start(bf16[2,240,384]{2,1,0:T(8,128)(2,1)S(1)} %get-tuple-element.25), channel_id=1, source_target_pairs={{0,8},{4,12},{8,16},{12,20},{16,24},{20,28},{24,32},{28,36},{32,40... | collective-permute-start | bytes 1105928 | tf_op jit(solution)/shard_map/ppermute | solution.py:37
  16.7 21.7 %collective-permute-start.1 = (bf16[2,240,384]{2,1,0:T(8,128)(2,1)S(1)}, bf16[2,240,384]{2,1,0:T(8,128)(2,1)S(1)}, u32[]{:S(2)}, u32[]{:S(2)}) collective-permute-start(bf16[2,240,384]{2,1,0:T(8,128)(2,1)S(1)} %get-tuple-element.26), channel_id=1, source_target_pairs={{0,504},{4,508},{8,0},{12,4},{16,8},{20,12},{24,16},{28,20},{32,24... | collective-permute-start | bytes 1105928 | tf_op jit(solution)/shard_map/ppermute | solution.py:37
  25.8 12.5 %collective-permute-start.2 = (bf16[240,384]{1,0:T(8,128)(2,1)S(1)}, bf16[240,384]{1,0:T(8,128)(2,1)S(1)}, u32[]{:S(2)}, u32[]{:S(2)}) collective-permute-start(bf16[240,384]{1,0:T(8,128)(2,1)S(1)} %get-tuple-element.27), channel_id=1, source_target_pairs={{0,500},{4,16},{8,508},{12,24},{16,4},{20,32},{24,12},{28,40},{32,... | collective-permute-start | bytes 552968 | tf_op jit(solution)/shard_map/ppermute | solution.py:43
  39.3 5.6 %collective-permute-start.3 = (bf16[3,240,384]{2,1,0:T(8,128)(2,1)}, bf16[3,240,384]{2,1,0:T(8,128)(2,1)}, u32[]{:S(2)}, u32[]{:S(2)}) collective-permute-start(bf16[3,240,384]{2,1,0:T(8,128)(2,1)} %pad_maximum_fusion), channel_id=1, source_target_pairs={{0,4},{4,0},{8,12},{12,8},{16,20},{20,16},{24,28},{28,24},{32,36},... | collective-permute-start | bytes 1658888 | tf_op jit(solution)/shard_map/ppermute | solution.py:43
  41.3 3.7 %copy-start.6 = (s32[1,1,128,8]{2,3,1,0:T(8,128)S(1)}, s32[1,1,128,8]{2,3,1,0:T(8,128)}, u32[]{:S(2)}) copy-start(s32[1,1,128,8]{2,3,1,0:T(8,128)} %param.20) | copy-start | bytes 12292
  49.3 37.7 %copy-start.7 = (s32[1,1,128,8]{2,3,1,0:T(8,128)S(1)}, s32[1,1,128,8]{2,3,1,0:T(8,128)}, u32[]{:S(2)}) copy-start(s32[1,1,128,8]{2,3,1,0:T(8,128)} %param.21) | copy-start | bytes 12292
  58.5 15.3 %collective-permute-start.7 = (bf16[4,8,512]{2,1,0:T(8,128)(2,1)S(1)}, bf16[4,8,512]{2,1,0:T(8,128)(2,1)S(1)}, u32[]{:S(2)}, u32[]{:S(2)}) collective-permute-start(bf16[4,8,512]{2,1,0:T(8,128)(2,1)S(1)} %get-tuple-element.46), channel_id=1, source_target_pairs={{0,64},{4,68},{8,72},{12,76},{16,80},{20,84},{24,88},{28,92},{32,9... | collective-permute-start | bytes 98312 | tf_op jit(solution)/shard_map/ppermute | solution.py:286
  66.9 6.9 %collective-permute-start.6 = (bf16[4,8,512]{2,1,0:T(8,128)(2,1)S(1)}, bf16[4,8,512]{2,1,0:T(8,128)(2,1)S(1)}, u32[]{:S(2)}, u32[]{:S(2)}) collective-permute-start(bf16[4,8,512]{2,1,0:T(8,128)(2,1)S(1)} %get-tuple-element.44), channel_id=1, source_target_pairs={{0,4},{4,8},{8,12},{12,16},{16,20},{20,24},{24,28},{28,32},{32,36}... | collective-permute-start | bytes 98312 | tf_op jit(solution)/shard_map/ppermute | solution.py:286
  68.9 5.8 %collective-permute-start.5 = (bf16[4,8,512]{2,1,0:T(8,128)(2,1)S(1)}, bf16[4,8,512]{2,1,0:T(8,128)(2,1)S(1)}, u32[]{:S(2)}, u32[]{:S(2)}) collective-permute-start(bf16[4,8,512]{2,1,0:T(8,128)(2,1)S(1)} %get-tuple-element.45), channel_id=1, source_target_pairs={{0,8},{4,12},{8,16},{12,20},{16,24},{20,28},{24,32},{28,36},{32,40... | collective-permute-start | bytes 98312 | tf_op jit(solution)/shard_map/ppermute | solution.py:286
  73.1 1.6 %collective-permute-start.4 = (bf16[4,8,512]{2,1,0:T(8,128)(2,1)S(1)}, bf16[4,8,512]{2,1,0:T(8,128)(2,1)S(1)}, u32[]{:S(2)}, u32[]{:S(2)}) collective-permute-start(bf16[4,8,512]{2,1,0:T(8,128)(2,1)S(1)} %get-tuple-element.43), channel_id=1, source_target_pairs={{2,258},{6,262},{10,266},{14,270},{18,274},{22,278},{26,282},{30,2... | collective-permute-start | bytes 98312 | tf_op jit(solution)/shard_map/ppermute | solution.py:286
  75.3 11.6 %all-to-all-start.2 = ((bf16[4,32,512]{2,1,0:T(8,128)(2,1)}), bf16[4,32,512]{2,1,0:T(8,128)(2,1)S(1)}, u32[]{:S(2)}, u32[]{:S(2)}) async-start(bf16[4,32,512]{2,1,0:T(8,128)(2,1)} %maximum_bitcast_fusion), calls=%async_computation.2 | async-start | bytes 262144 | tf_op jit(solution)/shard_map/all_to_all | solution.py:288
  87.0 8.9 %copy-start.3 = (bf16[1024,512]{1,0:T(8,128)(2,1)S(1)}, bf16[1024,512]{1,0:T(8,128)(2,1)}, u32[]{:S(2)}) copy-start(bf16[1024,512]{1,0:T(8,128)(2,1)} %get-tuple-element.38.table) | copy-start | bytes 3145732
  87.7 21.5 %copy-start.1 = (bf16[1024,1536]{1,0:T(8,128)(2,1)S(1)}, bf16[1024,1536]{1,0:T(8,128)(2,1)}, u32[]{:S(2)}) copy-start(bf16[1024,1536]{1,0:T(8,128)(2,1)} %get-tuple-element.41.rest_3_) | copy-start | bytes 9437188
  87.7 15.2 %collective-permute-start.8 = (bf16[512,512]{1,0:T(8,128)(2,1)S(1)}, bf16[512,512]{1,0:T(8,128)(2,1)S(1)}, u32[]{:S(2)}, u32[]{:S(2)}) collective-permute-start(bf16[512,512]{1,0:T(8,128)(2,1)S(1)} %decode.1.block), channel_id=1, source_target_pairs={{0,504},{4,12},{8,0},{12,20},{16,8},{20,28},{24,16},{28,36},{32,24... | collective-permute-start | bytes 1572872 | tf_op jit(solution)/shard_map/ppermute | solution.py:43
  91.7 15.0 %collective-permute-start.10 = (bf16[512,512]{1,0:T(8,128)(2,1)S(1)}, bf16[512,512]{1,0:T(8,128)(2,1)S(1)}, u32[]{:S(2)}, u32[]{:S(2)}) collective-permute-start(bf16[512,512]{1,0:T(8,128)(2,1)S(1)} %decode.1.block), channel_id=1, source_target_pairs={{0,8},{4,508},{8,16},{12,4},{16,24},{20,12},{24,32},{28,20},{32,40... | collective-permute-start | bytes 1572872 | tf_op jit(solution)/shard_map/ppermute | solution.py:43
  93.8 15.4 %collective-permute-start.9 = (bf16[512,512]{1,0:T(8,128)(2,1)S(1)}, bf16[512,512]{1,0:T(8,128)(2,1)S(1)}, u32[]{:S(2)}, u32[]{:S(2)}) collective-permute-start(bf16[512,512]{1,0:T(8,128)(2,1)S(1)} %decode.1.block), channel_id=1, source_target_pairs={{0,4},{4,0},{8,12},{12,8},{16,20},{20,16},{24,28},{28,24},{32,36},... | collective-permute-start | bytes 1572872 | tf_op jit(solution)/shard_map/ppermute | solution.py:43
  102.9 13.8 %collective-permute-start.11 = (bf16[512,512]{1,0:T(8,128)(2,1)S(1)}, bf16[512,512]{1,0:T(8,128)(2,1)S(1)}, u32[]{:S(2)}, u32[]{:S(2)}) collective-permute-start(bf16[512,512]{1,0:T(8,128)(2,1)S(1)} %collective-permute-done.8.rest_1_), channel_id=1, source_target_pairs={{0,508},{4,8},{8,4},{12,16},{16,12},{20,24},{24,20},{28,32},{32,28... | collective-permute-start | bytes 1572872 | tf_op jit(solution)/shard_map/ppermute | solution.py:43
  104.9 11.9 %collective-permute-start.12 = (bf16[512,512]{1,0:T(8,128)(2,1)S(1)}, bf16[512,512]{1,0:T(8,128)(2,1)S(1)}, u32[]{:S(2)}, u32[]{:S(2)}) collective-permute-start(bf16[512,512]{1,0:T(8,128)(2,1)S(1)} %collective-permute-done.8.rest_1_), channel_id=1, source_target_pairs={{0,4},{4,0},{8,12},{12,8},{16,20},{20,16},{24,28},{28,24},{32,36},... | collective-permute-start | bytes 1572872 | tf_op jit(solution)/shard_map/ppermute | solution.py:43
  106.8 10.0 %collective-permute-start.13 = (bf16[512,512]{1,0:T(8,128)(2,1)S(1)}, bf16[512,512]{1,0:T(8,128)(2,1)S(1)}, u32[]{:S(2)}, u32[]{:S(2)}) collective-permute-start(bf16[512,512]{1,0:T(8,128)(2,1)S(1)} %collective-permute-done.10.rest_2_), channel_id=1, source_target_pairs={{0,4},{4,0},{8,12},{12,8},{16,20},{20,16},{24,28},{28,24},{32,36},... | collective-permute-start | bytes 1572872 | tf_op jit(solution)/shard_map/ppermute | solution.py:43
  109.2 7.5 %copy-start.2 = (bf16[1024,1536]{1,0:T(8,128)(2,1)S(1)}, bf16[1024,1536]{1,0:T(8,128)(2,1)}, u32[]{:S(2)}) copy-start(bf16[1024,1536]{1,0:T(8,128)(2,1)} %get-tuple-element.42.rest_3_) | copy-start | bytes 9437188

commit v5 on v4

--- a/solution.py
+++ b/solution.py
@@ -61,15 +61,16 @@
     channels, rows = x.shape
     slots = pack.shape[-1]
     row_of = positions((rows, slots), 0)
-    blank = jnp.zeros((SENT - channels, slots), BF16)
+    last = channels // 16 * 16
+    blank = jnp.zeros((SENT - last, slots), BF16)
 
     def chosen(outs, offsets):
         for i, offset in enumerate(offsets):
             hot[:, i * slots : (i + 1) * slots] = one_hot(row_of, pack[offset])
         found = mul(x[...], hot[...]).astype(BF16)
         for i, out in enumerate(outs):
+            out[last:SENT, :] = blank
             out[0:channels, :] = found[:, i * slots : (i + 1) * slots]
-            out[channels:SENT, :] = blank
 
     chosen((up.at[0], up.at[1]), (5, jnp.where(here == 0, 6, 4)))
     chosen((down.at[0], down.at[1]), (1, jnp.where(here == 0, 2, 0)))
@@ -166,19 +167,19 @@
 
 
 def encode_body(
-    core, here, early, sib, weights, recv, far_ids, latent, message, far, rows, sent, hot
+    core, here, early, sib, weights, recv, far_ids, latent, message, far, rows, sent, hot, w_proc
 ):
     is_even = core[0] == 0
     nodes, channels = early.shape
     w_embed = weights[:, 0:SENT]
     w_edge = weights[:, WIDE : WIDE + channels]
+    w_proc[...] = weights[:, WIDE + channels : WIDE + 2 * channels]
     messages((sib[0], sib[1], sib[2]), w_embed, w_edge, rows, sent)
     offsets = (jnp.where(is_even, 2, 4), jnp.where(is_even, 4, 6), jnp.where(is_even, 0, 2))
     receivers(recv, offsets, hot)
     rounded = (early[...] + mul_nt(hot[...], sent[...])).astype(BF16)
     latent[...] = rounded
-    w_proc = weights[:, WIDE + channels : WIDE + 2 * channels]
-    made = silu(mul_nt(rounded, w_proc)).astype(BF16)
+    made = silu(mul_nt(rounded, w_proc[...])).astype(BF16)
     message[...] = made
     far[...] = mul(far_table(far_ids, here[0], 1, nodes), made).astype(BF16)
 
@@ -235,10 +236,26 @@
     nodes = blocks[0].shape[0]
     for i, block in enumerate(blocks):
         joined[i * nodes : (i + 1) * nodes, :] = block[...]
-    out[...] = (before[...].astype(F32) + mul(table[...], joined[...])).astype(out.dtype)
-
-
-def call(body, out_shape, args, scratch=(), name=None, stored=(), far_off=()):
+    out[...] = before[...] + mul(table[...], joined[...])
+
+
+def collect_body(before, *rest):
+    *blocks, table, out, joined, done, left = rest
+    nodes = blocks[0].shape[0]
+    for i, block in enumerate(blocks):
+        joined[i * nodes : (i + 1) * nodes, :] = block[...]
+    step = out.shape[0] // 4
+    stores = []
+    for i in range(4):
+        at = pl.ds(i * step, step)
+        done[at, :] = (before[at, :] + mul(table[at, :], joined[...])).astype(BF16)
+        stores.append(pltpu.make_async_copy(done.at[at, :], out.at[at, :], left.at[i]))
+        stores[-1].start()
+    for store in stores:
+        store.wait()
+
+
+def call(body, out_shape, args, scratch=(), name=None, stored=(), far_off=(), keeps=0):
     near = len(args)
     last = near + len(stored)
     args = (*args, *stored, *far_off)
@@ -256,7 +273,7 @@
         in_specs=[
             smem if a.ndim == 1 else hbm if i >= last else vmem for i, a in enumerate(args)
         ],
-        out_specs=[vmem for _ in out_shape] if many else vmem,
+        out_specs=[vmem for _ in out_shape] if many else hbm if keeps else vmem,
         scratch_shapes=scratch,
         compiler_params=VMEM,
         name=name,
@@ -355,7 +372,8 @@
         name="tables",
         stored=(edges,),
     )
-    up, down, three, own_table = lax.optimization_barrier((up, down, three, own_table))
+    three, up, own_table = lax.optimization_barrier((three, up, own_table))
+    up, down = lax.optimization_barrier((up, down))
     sib = by_core(jnp.stack([own, up[1], down[1]]), 1, -1)
     early = call(
         early_body,
@@ -369,7 +387,7 @@
         encode_body,
         [stored(nodes, channels), stored(nodes, channels), shape(8 * 16, channels)],
         (core, here, early, sib, weights, recv, far_out_ids),
-        [*work(3)],
+        [*work(3), pltpu.VMEM((channels, channels), BF16)],
         name="encode",
     )
     base = call(
@@ -387,10 +405,10 @@
         name="decode",
     )
 
-    def added(name, before, blocks, table, kind=F32):
+    def added(name, before, blocks, table):
         return call(
             add_body,
-            shape(rows, channels, kind=kind) if kind == F32 else stored(rows, channels),
+            shape(rows, channels, kind=F32),
             (before, *blocks, table),
             [pltpu.VMEM((len(blocks) * nodes, channels), BF16)],
             name=name,
@@ -411,7 +429,18 @@
     relay_first = by_core(first, 1, -1)
     relay_second = by_core(second, 1, -1)
     total = added("near", total, (sib, first, second), near_table)
-    return added("collect", total, (three, relay_first, relay_second), late_table, BF16)
+    return call(
+        collect_body,
+        stored(rows, channels),
+        (total, three, relay_first, relay_second, late_table),
+        [
+            pltpu.VMEM((3 * nodes, channels), BF16),
+            pltpu.VMEM((rows, channels), BF16),
+            pltpu.SemaphoreType.DMA((4,)),
+        ],
+        name="collect",
+        keeps=1,
+    )
 
 
 def solution(mesh):

time: 120 us -> 120 us (level)
  no operation moved by 1% of the time
where the time goes in v5:
time: 120 us; the launch traced here: 119 us
  starting transfers between devices  61.6 us (51%)
  Pallas kernels  29.1 us (24%)
  waiting for transfers between devices  17.3 us (14%)
  blocking collectives  9.24 us (8%)
  other arithmetic  1.57 us (1%)
    pallas_call x10, Pallas kernels, call(): pl.pallas_call(body, out_shape=out_shape, in_specs=[smem if a.ndim == 1 e...  29.1 us
    ppermute x8, starting transfers between devices, by_core(): return lax.ppermute(value, 'patch', pairs)  18.9 us
    ppermute x4, starting transfers between devices, far_exchange(): arrived.append(lax.ppermute(mine[:, kind], ('patch', 'chan'), pairs))  15.2 us
    ppermute x8, waiting for transfers between devices, by_core(): return lax.ppermute(value, 'patch', pairs)  14.3 us
    ppermute x2, starting transfers between devices, shifted(): lax.ppermute(value, 'patch', [(i, (i + steps) % count) for i in range(cou...  11.1 us
    all_to_all x1, starting transfers between devices, shards(): lax.all_to_all(copies, 'chan', 0, 0, tiled=True).reshape(chans * width, -1)  9.37 us
    all_to_all x1, blocking collectives, far_exchange(): lax.all_to_all(rows.reshape(chans, kinds * each, channels), 'chan', 0, 0,...  9.24 us
    all_to_all x1, starting transfers between devices, far_exchange(): lax.all_to_all(back, 'chan', 0, 0, tiled=True).reshape(count, channels)  7.1 us
  transfers between devices with their start and end apart: 16, of which 5 were waited for; matrix products, arithmetic and copies ran while one was open for 1% of the time, Pallas kernels for 16%

profile of v5, /device:TPU:8, one launch (start us, length us, event | category | flops | bytes accessed | tf_op | source)
XLA Modules:
  0.0 119.5 jit_solution(301977976036220156)
XLA Ops:
  0.0 2.6 %weights.1 = bf16[4,128,1792]{2,1,0:T(8,128)(2,1)} custom-call(bf16[227,128]{1,0:T(8,128)(2,1)} %embed.2, bf16[512,128]{1,0:T(8,128)(2,1)} %edge.1, bf16[512,128]{1,0:T(8,128)(2,1)} %proc.1, bf16[512,128]{1,0:T(8,128)(2,1)} %dec.1), custom_call_target="tpu_custom_call" | custom-call | tf_op jit(solution)/shard_map/weights/pallas_call | solution.py:270
  2.6 9.4 %all-to-all-start = ((bf16[4,128,1792]{2,1,0:T(8,128)(2,1)}), bf16[4,128,1792]{2,1,0:T(8,128)(2,1)S(1)}, u32[]{:S(2)}, u32[]{:S(2)}) async-start(bf16[4,128,1792]{2,1,0:T(8,128)(2,1)} %weights.1), calls=%async_computation | async-start | bytes 3670016 | tf_op jit(solution)/shard_map/all_to_all | solution.py:356
  12.0 0.0 copy-start
  12.0 0.0 copy-start.4
  12.0 0.0 copy-start.5
  12.0 2.8 %pack.1 = (bf16[240,384]{1,0:T(8,128)(2,1)S(1)}, bf16[2,240,384]{2,1,0:T(8,128)(2,1)S(1)}, bf16[2,240,384]{2,1,0:T(8,128)(2,1)S(1)}, bf16[240,384]{1,0:T(8,128)(2,1)S(1)}) custom-call(s32[1]{0:T(128)} %bitcast.1.core, bf16[227,1024]{1,0:T(8,128)(2,1)} %bitcast.44, s32[7,1,384]{2,1,0:T(1,128)} %bitcast.52), custom_call_target="tpu_custom_call" | custom-call | tf_op jit(solution)/shard_map/pack/pallas_call | solution.py:270
  14.8 1.9 %collective-permute-start.1 = (bf16[2,240,384]{2,1,0:T(8,128)(2,1)S(1)}, bf16[2,240,384]{2,1,0:T(8,128)(2,1)S(1)}, u32[]{:S(2)}, u32[]{:S(2)}) collective-permute-start(bf16[2,240,384]{2,1,0:T(8,128)(2,1)S(1)} %get-tuple-element.27), channel_id=1, source_target_pairs={{0,8},{4,12},{8,16},{12,20},{16,24},{20,28},{24,32},{28,36},{32,40... | collective-permute-start | bytes 1105928 | tf_op jit(solution)/shard_map/ppermute | solution.py:37
  16.7 9.1 %collective-permute-start.2 = (bf16[2,240,384]{2,1,0:T(8,128)(2,1)S(1)}, bf16[2,240,384]{2,1,0:T(8,128)(2,1)S(1)}, u32[]{:S(2)}, u32[]{:S(2)}) collective-permute-start(bf16[2,240,384]{2,1,0:T(8,128)(2,1)S(1)} %get-tuple-element.31), channel_id=1, source_target_pairs={{0,504},{4,508},{8,0},{12,4},{16,8},{20,12},{24,16},{28,20},{32,24... | collective-permute-start | bytes 1105928 | tf_op jit(solution)/shard_map/ppermute | solution.py:37
  25.8 2.7 %collective-permute-start = (bf16[240,384]{1,0:T(8,128)(2,1)S(1)}, bf16[240,384]{1,0:T(8,128)(2,1)S(1)}, u32[]{:S(2)}, u32[]{:S(2)}) collective-permute-start(bf16[240,384]{1,0:T(8,128)(2,1)S(1)} %get-tuple-element.26), channel_id=1, source_target_pairs={{0,500},{4,16},{8,508},{12,24},{16,4},{20,32},{24,12},{28,40},{32,... | collective-permute-start | bytes 552968 | tf_op jit(solution)/shard_map/ppermute | solution.py:43
  28.5 7.2 %tables.1 = (bf16[1024,512]{1,0:T(8,128)(2,1)}, bf16[1024,1536]{1,0:T(8,128)(2,1)}, bf16[1024,1536]{1,0:T(8,128)(2,1)}) custom-call(s32[1]{0:T(128)} %bitcast.1.core, s32[3,1024]{1,0:T(4,128)} %bitcast.62), custom_call_target="tpu_custom_call" | custom-call | tf_op jit(solution)/shard_map/tables/pallas_call | solution.py:270
  35.7 2.6 %collective-permute-done.three = bf16[240,384]{1,0:T(8,128)(2,1)S(1)} collective-permute-done((bf16[240,384]{1,0:T(8,128)(2,1)S(1)}, bf16[240,384]{1,0:T(8,128)(2,1)S(1)}, u32[]{:S(2)}, u32[]{:S(2)}) %collective-permute-start) | collective-permute-done | bytes 184352 | tf_op jit(solution)/shard_map/ppermute | solution.py:43
  38.3 0.0 collective-permute-done.1.up
  38.3 0.0 collective-permute-done.2.down
  38.4 0.9 pad_maximum_fusion
  39.3 1.9 %collective-permute-start.3 = (bf16[3,240,384]{2,1,0:T(8,128)(2,1)}, bf16[3,240,384]{2,1,0:T(8,128)(2,1)}, u32[]{:S(2)}, u32[]{:S(2)}) collective-permute-start(bf16[3,240,384]{2,1,0:T(8,128)(2,1)} %pad_maximum_fusion), channel_id=1, source_target_pairs={{0,4},{4,0},{8,12},{12,8},{16,20},{20,16},{24,28},{28,24},{32,36},... | collective-permute-start | bytes 1658888 | tf_op jit(solution)/shard_map/ppermute | solution.py:43
  41.2 0.0 all-to-all-done
  41.2 0.0 copy-done
  41.2 0.0 copy-done.4
  41.3 0.0 copy-done.5
  41.3 0.0 copy-start.6
  41.3 3.7 %early.1 = f32[512,512]{1,0:T(8,128)S(1)} custom-call(s32[1]{0:T(128)} %bitcast.1.core, bf16[227,1024]{1,0:T(8,128)(2,1)S(1)} %bitcast.45, s32[7,1,384]{2,1,0:T(1,128)S(1)} %bitcast.53, bf16[2,240,384]{2,1,0:T(8,128)(2,1)S(1)} %collective-permute-done.1.up, bf16[2,240,384]{2,1,0:T(8,128)(2,1)S(1)} %collective-permute-done.2.down, ...), custom_call_target="tpu_custom_call" | custom-call | tf_op jit(solution)/shard_map/early/pallas_call | solution.py:270
  44.9 0.0 collective-permute-done.3.sib
  45.0 0.0 copy-done.6
  45.0 4.3 %encode.1 = (bf16[512,512]{1,0:T(8,128)(2,1)}, bf16[512,512]{1,0:T(8,128)(2,1)}, bf16[128,512]{1,0:T(8,128)(2,1)S(1)}) custom-call(s32[1]{0:T(128)} %bitcast.1.core, s32[1]{0:T(128)} %bitcast.here, f32[512,512]{1,0:T(8,128)S(1)} %early.1, bf16[3,240,384]{2,1,0:T(8,128)(2,1)} %collective-permute-done.3.sib, bf16[512,1792]{1,0:T(8,128)(2,1)S(1)} %bitcast.41, ...), custom_call_target="tpu_custom_call" | custom-call | tf_op jit(solution)/shard_map/encode/pallas_call | solution.py:270
  49.3 0.0 copy-start.7
  49.3 9.2 %all_to_all.15 = bf16[4,32,512]{2,1,0:T(8,128)(2,1)S(1)} all-to-all(bf16[4,32,512]{2,1,0:T(8,128)(2,1)S(1)} %bitcast.49), channel_id=1, replica_groups=mesh['patch'=128,'chan'=4] {'chan'}, dimensions={0} | all-to-all | bytes 262144 | tf_op jit(solution)/shard_map/all_to_all | solution.py:292
  58.5 8.4 %collective-permute-start.7 = (bf16[4,8,512]{2,1,0:T(8,128)(2,1)S(1)}, bf16[4,8,512]{2,1,0:T(8,128)(2,1)S(1)}, u32[]{:S(2)}, u32[]{:S(2)}) collective-permute-start(bf16[4,8,512]{2,1,0:T(8,128)(2,1)S(1)} %get-tuple-element.48), channel_id=1, source_target_pairs={{0,64},{4,68},{8,72},{12,76},{16,80},{20,84},{24,88},{28,92},{32,9... | collective-permute-start | bytes 98312 | tf_op jit(solution)/shard_map/ppermute | solution.py:303
  66.9 1.9 %collective-permute-start.6 = (bf16[4,8,512]{2,1,0:T(8,128)(2,1)S(1)}, bf16[4,8,512]{2,1,0:T(8,128)(2,1)S(1)}, u32[]{:S(2)}, u32[]{:S(2)}) collective-permute-start(bf16[4,8,512]{2,1,0:T(8,128)(2,1)S(1)} %get-tuple-element.46), channel_id=1, source_target_pairs={{0,4},{4,8},{8,12},{12,16},{16,20},{20,24},{24,28},{28,32},{32,36}... | collective-permute-start | bytes 98312 | tf_op jit(solution)/shard_map/ppermute | solution.py:303
  68.9 4.2 %collective-permute-start.5 = (bf16[4,8,512]{2,1,0:T(8,128)(2,1)S(1)}, bf16[4,8,512]{2,1,0:T(8,128)(2,1)S(1)}, u32[]{:S(2)}, u32[]{:S(2)}) collective-permute-start(bf16[4,8,512]{2,1,0:T(8,128)(2,1)S(1)} %get-tuple-element.47), channel_id=1, source_target_pairs={{0,8},{4,12},{8,16},{12,20},{16,24},{20,28},{24,32},{28,36},{32,40... | collective-permute-start | bytes 98312 | tf_op jit(solution)/shard_map/ppermute | solution.py:303
  73.1 0.7 collective-permute-start.4
  73.8 0.0 collective-permute-done.7
  73.8 0.0 collective-permute-done.6
  73.8 0.9 collective-permute-done.5
  74.7 0.0 collective-permute-done.4
  74.7 0.7 maximum_bitcast_fusion
  75.3 7.1 %all-to-all-start.2 = ((bf16[4,32,512]{2,1,0:T(8,128)(2,1)}), bf16[4,32,512]{2,1,0:T(8,128)(2,1)S(1)}, u32[]{:S(2)}, u32[]{:S(2)}) async-start(bf16[4,32,512]{2,1,0:T(8,128)(2,1)} %maximum_bitcast_fusion), calls=%async_computation.2 | async-start | bytes 262144 | tf_op jit(solution)/shard_map/all_to_all | solution.py:305
  82.4 2.4 %short.1.base = f32[512,512]{1,0:T(8,128)S(1)} custom-call(bf16[512,512]{1,0:T(8,128)(2,1)} %get-tuple-element.37.latent, bf16[512,512]{1,0:T(8,128)(2,1)} %get-tuple-element.38.message, s32[6,512]{1,0:T(8,128)} %bitcast.61), custom_call_target="tpu_custom_call" | custom-call | tf_op jit(solution)/shard_map/short/pallas_call | solution.py:270
  84.9 2.1 %all-to-all-done.2 = bf16[4,32,512]{2,1,0:T(8,128)(2,1)S(1)} async-done(((bf16[4,32,512]{2,1,0:T(8,128)(2,1)}), bf16[4,32,512]{2,1,0:T(8,128)(2,1)S(1)}, u32[]{:S(2)}, u32[]{:S(2)}) %all-to-all-start.2) | async-done | bytes 131104 | tf_op jit(solution)/shard_map/all_to_all | solution.py:305
  87.0 0.0 copy-start.3
  87.0 0.0 copy-done.7
  87.0 0.7 decode.1.block
  87.7 0.0 copy-start.1
  87.7 4.0 %collective-permute-start.8 = (bf16[512,512]{1,0:T(8,128)(2,1)S(1)}, bf16[512,512]{1,0:T(8,128)(2,1)S(1)}, u32[]{:S(2)}, u32[]{:S(2)}) collective-permute-start(bf16[512,512]{1,0:T(8,128)(2,1)S(1)} %decode.1.block), channel_id=1, source_target_pairs={{0,504},{4,12},{8,0},{12,20},{16,8},{20,28},{24,16},{28,36},{32,24... | collective-permute-start | bytes 1572872 | tf_op jit(solution)/shard_map/ppermute | solution.py:43
  91.7 2.1 %collective-permute-start.10 = (bf16[512,512]{1,0:T(8,128)(2,1)S(1)}, bf16[512,512]{1,0:T(8,128)(2,1)S(1)}, u32[]{:S(2)}, u32[]{:S(2)}) collective-permute-start(bf16[512,512]{1,0:T(8,128)(2,1)S(1)} %decode.1.block), channel_id=1, source_target_pairs={{0,8},{4,508},{8,16},{12,4},{16,24},{20,12},{24,32},{28,20},{32,40... | collective-permute-start | bytes 1572872 | tf_op jit(solution)/shard_map/ppermute | solution.py:43
  93.9 2.0 %collective-permute-start.9 = (bf16[512,512]{1,0:T(8,128)(2,1)S(1)}, bf16[512,512]{1,0:T(8,128)(2,1)S(1)}, u32[]{:S(2)}, u32[]{:S(2)}) collective-permute-start(bf16[512,512]{1,0:T(8,128)(2,1)S(1)} %decode.1.block), channel_id=1, source_target_pairs={{0,4},{4,0},{8,12},{12,8},{16,20},{20,16},{24,28},{28,24},{32,36},... | collective-permute-start | bytes 1572872 | tf_op jit(solution)/shard_map/ppermute | solution.py:43
  95.8 0.0 copy-done.3
  95.8 1.2 own.1.before
  97.0 5.9 %collective-permute-done.8.rest_1_ = bf16[512,512]{1,0:T(8,128)(2,1)S(1)} collective-permute-done((bf16[512,512]{1,0:T(8,128)(2,1)S(1)}, bf16[512,512]{1,0:T(8,128)(2,1)S(1)}, u32[]{:S(2)}, u32[]{:S(2)}) %collective-permute-start.8) | collective-permute-done | bytes 524320 | tf_op jit(solution)/shard_map/ppermute | solution.py:43
  102.9 1.9 %collective-permute-start.11 = (bf16[512,512]{1,0:T(8,128)(2,1)S(1)}, bf16[512,512]{1,0:T(8,128)(2,1)S(1)}, u32[]{:S(2)}, u32[]{:S(2)}) collective-permute-start(bf16[512,512]{1,0:T(8,128)(2,1)S(1)} %collective-permute-done.8.rest_1_), channel_id=1, source_target_pairs={{0,508},{4,8},{8,4},{12,16},{16,12},{20,24},{24,20},{28,32},{32,28... | collective-permute-start | bytes 1572872 | tf_op jit(solution)/shard_map/ppermute | solution.py:43
  104.9 1.9 %collective-permute-start.12 = (bf16[512,512]{1,0:T(8,128)(2,1)S(1)}, bf16[512,512]{1,0:T(8,128)(2,1)S(1)}, u32[]{:S(2)}, u32[]{:S(2)}) collective-permute-start(bf16[512,512]{1,0:T(8,128)(2,1)S(1)} %collective-permute-done.8.rest_1_), channel_id=1, source_target_pairs={{0,4},{4,0},{8,12},{12,8},{16,20},{20,16},{24,28},{28,24},{32,36},... | collective-permute-start | bytes 1572872 | tf_op jit(solution)/shard_map/ppermute | solution.py:43
  106.8 0.0 collective-permute-done.10.rest_2_
  106.8 2.4 %collective-permute-start.13 = (bf16[512,512]{1,0:T(8,128)(2,1)S(1)}, bf16[512,512]{1,0:T(8,128)(2,1)S(1)}, u32[]{:S(2)}, u32[]{:S(2)}) collective-permute-start(bf16[512,512]{1,0:T(8,128)(2,1)S(1)} %collective-permute-done.10.rest_2_), channel_id=1, source_target_pairs={{0,4},{4,0},{8,12},{12,8},{16,20},{20,16},{24,28},{28,24},{32,36},... | collective-permute-start | bytes 1572872 | tf_op jit(solution)/shard_map/ppermute | solution.py:43
  109.2 0.0 collective-permute-done.9.rest_0_
  109.2 0.0 copy-done.1
  109.2 0.0 copy-start.2
  109.2 1.8 %near.1.before = f32[1024,512]{1,0:T(8,128)S(1)} custom-call(f32[1024,512]{1,0:T(8,128)S(1)} %own.1.before, bf16[512,512]{1,0:T(8,128)(2,1)S(1)} %collective-permute-done.9.rest_0_, bf16[512,512]{1,0:T(8,128)(2,1)S(1)} %collective-permute-done.8.rest_1_, bf16[512,512]{1,0:T(8,128)(2,1)S(1)} %collective-permute-done.10.rest_2_, bf16[1024,1536]{1,0:T(8,128)(2,1)S(1)} %copy-done.1), custom_call_target="tpu_custom_call" | custom-call | tf_op jit(solution)/shard_map/near/pallas_call | solution.py:270
  111.0 5.7 %collective-permute-done.11.rest_0_ = bf16[512,512]{1,0:T(8,128)(2,1)S(1)} collective-permute-done((bf16[512,512]{1,0:T(8,128)(2,1)S(1)}, bf16[512,512]{1,0:T(8,128)(2,1)S(1)}, u32[]{:S(2)}, u32[]{:S(2)}) %collective-permute-start.11) | collective-permute-done | bytes 524320 | tf_op jit(solution)/shard_map/ppermute | solution.py:43
  116.8 0.0 collective-permute-done.12.rest_1_
  116.8 0.0 collective-permute-done.13.rest_2_
  116.8 0.0 copy-done.2
  116.8 2.5 %collect.1 = bf16[1024,512]{1,0:T(8,128)(2,1)} custom-call(f32[1024,512]{1,0:T(8,128)S(1)} %near.1.before, bf16[512,512]{1,0:T(8,128)(2,1)S(1)} %collective-permute-done.11.rest_0_, bf16[512,512]{1,0:T(8,128)(2,1)S(1)} %collective-permute-done.12.rest_1_, bf16[512,512]{1,0:T(8,128)(2,1)S(1)} %collective-permute-done.13.rest_2_, bf16[1024,1536]{1,0:T(8,128)(2,1)S(1)} %copy-done.2), custom_call_target="tpu_custom_call" | custom-call | tf_op jit(solution)/shard_map/collect/pallas_call | solution.py:270
  (3 shorter events, 0.0 us)
Async XLA Ops:
  2.6 38.6 %all-to-all-start = ((bf16[4,128,1792]{2,1,0:T(8,128)(2,1)}), bf16[4,128,1792]{2,1,0:T(8,128)(2,1)S(1)}, u32[]{:S(2)}, u32[]{:S(2)}) async-start(bf16[4,128,1792]{2,1,0:T(8,128)(2,1)} %weights.1), calls=%async_computation | async-start | bytes 3670016 | tf_op jit(solution)/shard_map/all_to_all | solution.py:356
  12.0 29.2 %copy-start = (bf16[1024,227]{0,1:T(8,128)(2,1)S(1)}, bf16[1024,227]{0,1:T(8,128)(2,1)}, u32[]{:S(2)}) copy-start(bf16[1024,227]{0,1:T(8,128)(2,1)} %param.12) | copy-start | bytes 1394692
  12.0 29.3 %copy-start.4 = (s32[1,1,7,384]{3,1,2,0:T(1,128)S(1)}, s32[1,1,7,384]{3,1,2,0:T(1,128)}, u32[]{:S(2)}) copy-start(s32[1,1,7,384]{3,1,2,0:T(1,128)} %param.19) | copy-start | bytes 32260
  12.0 29.3 %copy-start.5 = (s32[1,1,7,384]{3,1,2,0:T(1,128)S(1)}, s32[1,1,7,384]{3,1,2,0:T(1,128)}, u32[]{:S(2)}) copy-start(s32[1,1,7,384]{3,1,2,0:T(1,128)} %param.18) | copy-start | bytes 32260
  14.8 23.6 %collective-permute-start.1 = (bf16[2,240,384]{2,1,0:T(8,128)(2,1)S(1)}, bf16[2,240,384]{2,1,0:T(8,128)(2,1)S(1)}, u32[]{:S(2)}, u32[]{:S(2)}) collective-permute-start(bf16[2,240,384]{2,1,0:T(8,128)(2,1)S(1)} %get-tuple-element.27), channel_id=1, source_target_pairs={{0,8},{4,12},{8,16},{12,20},{16,24},{20,28},{24,32},{28,36},{32,40... | collective-permute-start | bytes 1105928 | tf_op jit(solution)/shard_map/ppermute | solution.py:37
  16.7 21.7 %collective-permute-start.2 = (bf16[2,240,384]{2,1,0:T(8,128)(2,1)S(1)}, bf16[2,240,384]{2,1,0:T(8,128)(2,1)S(1)}, u32[]{:S(2)}, u32[]{:S(2)}) collective-permute-start(bf16[2,240,384]{2,1,0:T(8,128)(2,1)S(1)} %get-tuple-element.31), channel_id=1, source_target_pairs={{0,504},{4,508},{8,0},{12,4},{16,8},{20,12},{24,16},{28,20},{32,24... | collective-permute-start | bytes 1105928 | tf_op jit(solution)/shard_map/ppermute | solution.py:37
  25.8 12.5 %collective-permute-start = (bf16[240,384]{1,0:T(8,128)(2,1)S(1)}, bf16[240,384]{1,0:T(8,128)(2,1)S(1)}, u32[]{:S(2)}, u32[]{:S(2)}) collective-permute-start(bf16[240,384]{1,0:T(8,128)(2,1)S(1)} %get-tuple-element.26), channel_id=1, source_target_pairs={{0,500},{4,16},{8,508},{12,24},{16,4},{20,32},{24,12},{28,40},{32,... | collective-permute-start | bytes 552968 | tf_op jit(solution)/shard_map/ppermute | solution.py:43
  39.3 5.6 %collective-permute-start.3 = (bf16[3,240,384]{2,1,0:T(8,128)(2,1)}, bf16[3,240,384]{2,1,0:T(8,128)(2,1)}, u32[]{:S(2)}, u32[]{:S(2)}) collective-permute-start(bf16[3,240,384]{2,1,0:T(8,128)(2,1)} %pad_maximum_fusion), channel_id=1, source_target_pairs={{0,4},{4,0},{8,12},{12,8},{16,20},{20,16},{24,28},{28,24},{32,36},... | collective-permute-start | bytes 1658888 | tf_op jit(solution)/shard_map/ppermute | solution.py:43
  41.3 3.7 %copy-start.6 = (s32[1,1,128,8]{2,3,1,0:T(8,128)S(1)}, s32[1,1,128,8]{2,3,1,0:T(8,128)}, u32[]{:S(2)}) copy-start(s32[1,1,128,8]{2,3,1,0:T(8,128)} %param.20) | copy-start | bytes 12292
  49.3 37.7 %copy-start.7 = (s32[1,1,128,8]{2,3,1,0:T(8,128)S(1)}, s32[1,1,128,8]{2,3,1,0:T(8,128)}, u32[]{:S(2)}) copy-start(s32[1,1,128,8]{2,3,1,0:T(8,128)} %param.21) | copy-start | bytes 12292
  58.5 15.3 %collective-permute-start.7 = (bf16[4,8,512]{2,1,0:T(8,128)(2,1)S(1)}, bf16[4,8,512]{2,1,0:T(8,128)(2,1)S(1)}, u32[]{:S(2)}, u32[]{:S(2)}) collective-permute-start(bf16[4,8,512]{2,1,0:T(8,128)(2,1)S(1)} %get-tuple-element.48), channel_id=1, source_target_pairs={{0,64},{4,68},{8,72},{12,76},{16,80},{20,84},{24,88},{28,92},{32,9... | collective-permute-start | bytes 98312 | tf_op jit(solution)/shard_map/ppermute | solution.py:303
  66.9 6.9 %collective-permute-start.6 = (bf16[4,8,512]{2,1,0:T(8,128)(2,1)S(1)}, bf16[4,8,512]{2,1,0:T(8,128)(2,1)S(1)}, u32[]{:S(2)}, u32[]{:S(2)}) collective-permute-start(bf16[4,8,512]{2,1,0:T(8,128)(2,1)S(1)} %get-tuple-element.46), channel_id=1, source_target_pairs={{0,4},{4,8},{8,12},{12,16},{16,20},{20,24},{24,28},{28,32},{32,36}... | collective-permute-start | bytes 98312 | tf_op jit(solution)/shard_map/ppermute | solution.py:303
  68.9 5.8 %collective-permute-start.5 = (bf16[4,8,512]{2,1,0:T(8,128)(2,1)S(1)}, bf16[4,8,512]{2,1,0:T(8,128)(2,1)S(1)}, u32[]{:S(2)}, u32[]{:S(2)}) collective-permute-start(bf16[4,8,512]{2,1,0:T(8,128)(2,1)S(1)} %get-tuple-element.47), channel_id=1, source_target_pairs={{0,8},{4,12},{8,16},{12,20},{16,24},{20,28},{24,32},{28,36},{32,40... | collective-permute-start | bytes 98312 | tf_op jit(solution)/shard_map/ppermute | solution.py:303
  73.1 1.6 %collective-permute-start.4 = (bf16[4,8,512]{2,1,0:T(8,128)(2,1)S(1)}, bf16[4,8,512]{2,1,0:T(8,128)(2,1)S(1)}, u32[]{:S(2)}, u32[]{:S(2)}) collective-permute-start(bf16[4,8,512]{2,1,0:T(8,128)(2,1)S(1)} %get-tuple-element.45), channel_id=1, source_target_pairs={{2,258},{6,262},{10,266},{14,270},{18,274},{22,278},{26,282},{30,2... | collective-permute-start | bytes 98312 | tf_op jit(solution)/shard_map/ppermute | solution.py:303
  75.3 11.6 %all-to-all-start.2 = ((bf16[4,32,512]{2,1,0:T(8,128)(2,1)}), bf16[4,32,512]{2,1,0:T(8,128)(2,1)S(1)}, u32[]{:S(2)}, u32[]{:S(2)}) async-start(bf16[4,32,512]{2,1,0:T(8,128)(2,1)} %maximum_bitcast_fusion), calls=%async_computation.2 | async-start | bytes 262144 | tf_op jit(solution)/shard_map/all_to_all | solution.py:305
  87.0 8.9 %copy-start.3 = (bf16[1024,512]{1,0:T(8,128)(2,1)S(1)}, bf16[1024,512]{1,0:T(8,128)(2,1)}, u32[]{:S(2)}) copy-start(bf16[1024,512]{1,0:T(8,128)(2,1)} %get-tuple-element.40.table) | copy-start | bytes 3145732
  87.7 21.5 %copy-start.1 = (bf16[1024,1536]{1,0:T(8,128)(2,1)S(1)}, bf16[1024,1536]{1,0:T(8,128)(2,1)}, u32[]{:S(2)}) copy-start(bf16[1024,1536]{1,0:T(8,128)(2,1)} %get-tuple-element.43.rest_3_) | copy-start | bytes 9437188
  87.7 15.2 %collective-permute-start.8 = (bf16[512,512]{1,0:T(8,128)(2,1)S(1)}, bf16[512,512]{1,0:T(8,128)(2,1)S(1)}, u32[]{:S(2)}, u32[]{:S(2)}) collective-permute-start(bf16[512,512]{1,0:T(8,128)(2,1)S(1)} %decode.1.block), channel_id=1, source_target_pairs={{0,504},{4,12},{8,0},{12,20},{16,8},{20,28},{24,16},{28,36},{32,24... | collective-permute-start | bytes 1572872 | tf_op jit(solution)/shard_map/ppermute | solution.py:43
  91.7 15.1 %collective-permute-start.10 = (bf16[512,512]{1,0:T(8,128)(2,1)S(1)}, bf16[512,512]{1,0:T(8,128)(2,1)S(1)}, u32[]{:S(2)}, u32[]{:S(2)}) collective-permute-start(bf16[512,512]{1,0:T(8,128)(2,1)S(1)} %decode.1.block), channel_id=1, source_target_pairs={{0,8},{4,508},{8,16},{12,4},{16,24},{20,12},{24,32},{28,20},{32,40... | collective-permute-start | bytes 1572872 | tf_op jit(solution)/shard_map/ppermute | solution.py:43
  93.9 15.4 %collective-permute-start.9 = (bf16[512,512]{1,0:T(8,128)(2,1)S(1)}, bf16[512,512]{1,0:T(8,128)(2,1)S(1)}, u32[]{:S(2)}, u32[]{:S(2)}) collective-permute-start(bf16[512,512]{1,0:T(8,128)(2,1)S(1)} %decode.1.block), channel_id=1, source_target_pairs={{0,4},{4,0},{8,12},{12,8},{16,20},{20,16},{24,28},{28,24},{32,36},... | collective-permute-start | bytes 1572872 | tf_op jit(solution)/shard_map/ppermute | solution.py:43
  102.9 13.8 %collective-permute-start.11 = (bf16[512,512]{1,0:T(8,128)(2,1)S(1)}, bf16[512,512]{1,0:T(8,128)(2,1)S(1)}, u32[]{:S(2)}, u32[]{:S(2)}) collective-permute-start(bf16[512,512]{1,0:T(8,128)(2,1)S(1)} %collective-permute-done.8.rest_1_), channel_id=1, source_target_pairs={{0,508},{4,8},{8,4},{12,16},{16,12},{20,24},{24,20},{28,32},{32,28... | collective-permute-start | bytes 1572872 | tf_op jit(solution)/shard_map/ppermute | solution.py:43
  104.9 11.9 %collective-permute-start.12 = (bf16[512,512]{1,0:T(8,128)(2,1)S(1)}, bf16[512,512]{1,0:T(8,128)(2,1)S(1)}, u32[]{:S(2)}, u32[]{:S(2)}) collective-permute-start(bf16[512,512]{1,0:T(8,128)(2,1)S(1)} %collective-permute-done.8.rest_1_), channel_id=1, source_target_pairs={{0,4},{4,0},{8,12},{12,8},{16,20},{20,16},{24,28},{28,24},{32,36},... | collective-permute-start | bytes 1572872 | tf_op jit(solution)/shard_map/ppermute | solution.py:43
  106.8 10.0 %collective-permute-start.13 = (bf16[512,512]{1,0:T(8,128)(2,1)S(1)}, bf16[512,512]{1,0:T(8,128)(2,1)S(1)}, u32[]{:S(2)}, u32[]{:S(2)}) collective-permute-start(bf16[512,512]{1,0:T(8,128)(2,1)S(1)} %collective-permute-done.10.rest_2_), channel_id=1, source_target_pairs={{0,4},{4,0},{8,12},{12,8},{16,20},{20,16},{24,28},{28,24},{32,36},... | collective-permute-start | bytes 1572872 | tf_op jit(solution)/shard_map/ppermute | solution.py:43
  109.2 7.5 %copy-start.2 = (bf16[1024,1536]{1,0:T(8,128)(2,1)S(1)}, bf16[1024,1536]{1,0:T(8,128)(2,1)}, u32[]{:S(2)}) copy-start(bf16[1024,1536]{1,0:T(8,128)(2,1)} %get-tuple-element.44.rest_3_) | copy-start | bytes 9437188

commit v6 on v5

--- a/solution.py
+++ b/solution.py
@@ -357,10 +357,9 @@
     three, up, down, own = call(
         pack_body,
         [block, pair, pair, block],
-        (core,),
+        (core, x, pack),
         [pltpu.VMEM((rows, 2 * slots), BF16)],
         name="pack",
-        stored=(x, pack),
     )
     three = by_core(three, -3, 3)
     up = shifted(up, 2)

time: 120 us -> 119 us (level)
  transfers between devices with their start and end apart: 16 -> 16, of which waited for: 5 -> 5; matrix products, arithmetic and copies ran while one was open for 1% -> 1% of each run, Pallas kernels for 16% -> 15%
where the time goes in v6:
time: 119 us
  starting transfers between devices  61.7 us (52%)
  Pallas kernels  28 us (24%)
  waiting for transfers between devices  17.5 us (15%)
  blocking collectives  9.24 us (8%)
  other arithmetic  1.57 us (1%)
    pallas_call x10, Pallas kernels, call(): pl.pallas_call(body, out_shape=out_shape, in_specs=[smem if a.ndim == 1 e...  28 us
    ppermute x8, starting transfers between devices, by_core(): return lax.ppermute(value, 'patch', pairs)  19 us
    ppermute x4, starting transfers between devices, far_exchange(): arrived.append(lax.ppermute(mine[:, kind], ('patch', 'chan'), pairs))  15.2 us
    ppermute x8, waiting for transfers between devices, by_core(): return lax.ppermute(value, 'patch', pairs)  14.3 us
    ppermute x2, starting transfers between devices, shifted(): lax.ppermute(value, 'patch', [(i, (i + steps) % count) for i in range(cou...  11.1 us
    all_to_all x1, starting transfers between devices, shards(): lax.all_to_all(copies, 'chan', 0, 0, tiled=True).reshape(chans * width, -1)  9.5 us
    all_to_all x1, blocking collectives, far_exchange(): lax.all_to_all(rows.reshape(chans, kinds * each, channels), 'chan', 0, 0,...  9.24 us
    all_to_all x1, starting transfers between devices, far_exchange(): lax.all_to_all(back, 'chan', 0, 0, tiled=True).reshape(count, channels)  6.87 us
  transfers between devices with their start and end apart: 16, of which 5 were waited for; matrix products, arithmetic and copies ran while one was open for 1% of the time, Pallas kernels for 15%

profile of v6, /device:TPU:8, one launch (start us, length us, event | category | flops | bytes accessed | tf_op | source)
XLA Modules:
  0.0 118.6 jit_solution(14775157886057926830)
XLA Ops:
  0.0 2.6 %weights.1 = bf16[4,128,1792]{2,1,0:T(8,128)(2,1)} custom-call(bf16[227,128]{1,0:T(8,128)(2,1)} %embed.2, bf16[512,128]{1,0:T(8,128)(2,1)} %edge.1, bf16[512,128]{1,0:T(8,128)(2,1)} %proc.1, bf16[512,128]{1,0:T(8,128)(2,1)} %dec.1), custom_call_target="tpu_custom_call" | custom-call | tf_op jit(solution)/shard_map/weights/pallas_call | solution.py:270
  2.6 0.0 copy-start
  2.6 0.0 copy-start.5
  2.6 9.5 %all-to-all-start = ((bf16[4,128,1792]{2,1,0:T(8,128)(2,1)}), bf16[4,128,1792]{2,1,0:T(8,128)(2,1)S(1)}, u32[]{:S(2)}, u32[]{:S(2)}) async-start(bf16[4,128,1792]{2,1,0:T(8,128)(2,1)} %weights.1), calls=%async_computation | async-start | bytes 3670016 | tf_op jit(solution)/shard_map/all_to_all | solution.py:356
  12.1 0.0 copy-start.4
  12.1 0.0 copy-done
  12.1 0.0 copy-done.5
  12.1 1.6 %pack.1 = (bf16[240,384]{1,0:T(8,128)(2,1)S(1)}, bf16[2,240,384]{2,1,0:T(8,128)(2,1)S(1)}, bf16[2,240,384]{2,1,0:T(8,128)(2,1)S(1)}, bf16[240,384]{1,0:T(8,128)(2,1)S(1)}) custom-call(s32[1]{0:T(128)} %bitcast.1.core, bf16[227,1024]{1,0:T(8,128)(2,1)S(1)} %bitcast.44, s32[7,1,384]{2,1,0:T(1,128)S(1)} %bitcast.52), custom_call_target="tpu_custom_call" | custom-call | tf_op jit(solution)/shard_map/pack/pallas_call | solution.py:270
  13.8 1.9 %collective-permute-start.1 = (bf16[2,240,384]{2,1,0:T(8,128)(2,1)S(1)}, bf16[2,240,384]{2,1,0:T(8,128)(2,1)S(1)}, u32[]{:S(2)}, u32[]{:S(2)}) collective-permute-start(bf16[2,240,384]{2,1,0:T(8,128)(2,1)S(1)} %get-tuple-element.27), channel_id=1, source_target_pairs={{0,8},{4,12},{8,16},{12,20},{16,24},{20,28},{24,32},{28,36},{32,40... | collective-permute-start | bytes 1105928 | tf_op jit(solution)/shard_map/ppermute | solution.py:37
  15.7 9.1 %collective-permute-start.2 = (bf16[2,240,384]{2,1,0:T(8,128)(2,1)S(1)}, bf16[2,240,384]{2,1,0:T(8,128)(2,1)S(1)}, u32[]{:S(2)}, u32[]{:S(2)}) collective-permute-start(bf16[2,240,384]{2,1,0:T(8,128)(2,1)S(1)} %get-tuple-element.31), channel_id=1, source_target_pairs={{0,504},{4,508},{8,0},{12,4},{16,8},{20,12},{24,16},{28,20},{32,24... | collective-permute-start | bytes 1105928 | tf_op jit(solution)/shard_map/ppermute | solution.py:37
  24.9 2.7 %collective-permute-start = (bf16[240,384]{1,0:T(8,128)(2,1)S(1)}, bf16[240,384]{1,0:T(8,128)(2,1)S(1)}, u32[]{:S(2)}, u32[]{:S(2)}) collective-permute-start(bf16[240,384]{1,0:T(8,128)(2,1)S(1)} %get-tuple-element.26), channel_id=1, source_target_pairs={{0,500},{4,16},{8,508},{12,24},{16,4},{20,32},{24,12},{28,40},{32,... | collective-permute-start | bytes 552968 | tf_op jit(solution)/shard_map/ppermute | solution.py:43
  27.5 7.2 %tables.1 = (bf16[1024,512]{1,0:T(8,128)(2,1)}, bf16[1024,1536]{1,0:T(8,128)(2,1)}, bf16[1024,1536]{1,0:T(8,128)(2,1)}) custom-call(s32[1]{0:T(128)} %bitcast.1.core, s32[3,1024]{1,0:T(4,128)} %bitcast.62), custom_call_target="tpu_custom_call" | custom-call | tf_op jit(solution)/shard_map/tables/pallas_call | solution.py:270
  34.7 2.6 %collective-permute-done.three = bf16[240,384]{1,0:T(8,128)(2,1)S(1)} collective-permute-done((bf16[240,384]{1,0:T(8,128)(2,1)S(1)}, bf16[240,384]{1,0:T(8,128)(2,1)S(1)}, u32[]{:S(2)}, u32[]{:S(2)}) %collective-permute-start) | collective-permute-done | bytes 184352 | tf_op jit(solution)/shard_map/ppermute | solution.py:43
  37.4 0.0 collective-permute-done.1.up
  37.4 0.0 collective-permute-done.2.down
  37.4 0.9 pad_maximum_fusion
  38.3 1.9 %collective-permute-start.3 = (bf16[3,240,384]{2,1,0:T(8,128)(2,1)}, bf16[3,240,384]{2,1,0:T(8,128)(2,1)}, u32[]{:S(2)}, u32[]{:S(2)}) collective-permute-start(bf16[3,240,384]{2,1,0:T(8,128)(2,1)} %pad_maximum_fusion), channel_id=1, source_target_pairs={{0,4},{4,0},{8,12},{12,8},{16,20},{20,16},{24,28},{28,24},{32,36},... | collective-permute-start | bytes 1658888 | tf_op jit(solution)/shard_map/ppermute | solution.py:43
  40.2 0.0 all-to-all-done
  40.3 0.0 copy-done.4
  40.3 0.0 copy-start.6
  40.3 3.7 %early.1 = f32[512,512]{1,0:T(8,128)S(1)} custom-call(s32[1]{0:T(128)} %bitcast.1.core, bf16[227,1024]{1,0:T(8,128)(2,1)S(1)} %bitcast.45, s32[7,1,384]{2,1,0:T(1,128)S(1)} %bitcast.53, bf16[2,240,384]{2,1,0:T(8,128)(2,1)S(1)} %collective-permute-done.1.up, bf16[2,240,384]{2,1,0:T(8,128)(2,1)S(1)} %collective-permute-done.2.down, ...), custom_call_target="tpu_custom_call" | custom-call | tf_op jit(solution)/shard_map/early/pallas_call | solution.py:270
  43.9 0.0 collective-permute-done.3.sib
  44.0 0.0 copy-done.6
  44.0 4.3 %encode.1 = (bf16[512,512]{1,0:T(8,128)(2,1)}, bf16[512,512]{1,0:T(8,128)(2,1)}, bf16[128,512]{1,0:T(8,128)(2,1)S(1)}) custom-call(s32[1]{0:T(128)} %bitcast.1.core, s32[1]{0:T(128)} %bitcast.here, f32[512,512]{1,0:T(8,128)S(1)} %early.1, bf16[3,240,384]{2,1,0:T(8,128)(2,1)} %collective-permute-done.3.sib, bf16[512,1792]{1,0:T(8,128)(2,1)S(1)} %bitcast.41, ...), custom_call_target="tpu_custom_call" | custom-call | tf_op jit(solution)/shard_map/encode/pallas_call | solution.py:270
  48.3 0.0 copy-start.7
  48.3 9.2 %all_to_all.15 = bf16[4,32,512]{2,1,0:T(8,128)(2,1)S(1)} all-to-all(bf16[4,32,512]{2,1,0:T(8,128)(2,1)S(1)} %bitcast.49), channel_id=1, replica_groups=mesh['patch'=128,'chan'=4] {'chan'}, dimensions={0} | all-to-all | bytes 262144 | tf_op jit(solution)/shard_map/all_to_all | solution.py:292
  57.5 8.6 %collective-permute-start.7 = (bf16[4,8,512]{2,1,0:T(8,128)(2,1)S(1)}, bf16[4,8,512]{2,1,0:T(8,128)(2,1)S(1)}, u32[]{:S(2)}, u32[]{:S(2)}) collective-permute-start(bf16[4,8,512]{2,1,0:T(8,128)(2,1)S(1)} %get-tuple-element.48), channel_id=1, source_target_pairs={{0,64},{4,68},{8,72},{12,76},{16,80},{20,84},{24,88},{28,92},{32,9... | collective-permute-start | bytes 98312 | tf_op jit(solution)/shard_map/ppermute | solution.py:303
  66.2 1.9 %collective-permute-start.6 = (bf16[4,8,512]{2,1,0:T(8,128)(2,1)S(1)}, bf16[4,8,512]{2,1,0:T(8,128)(2,1)S(1)}, u32[]{:S(2)}, u32[]{:S(2)}) collective-permute-start(bf16[4,8,512]{2,1,0:T(8,128)(2,1)S(1)} %get-tuple-element.46), channel_id=1, source_target_pairs={{0,4},{4,8},{8,12},{12,16},{16,20},{20,24},{24,28},{28,32},{32,36}... | collective-permute-start | bytes 98312 | tf_op jit(solution)/shard_map/ppermute | solution.py:303
  68.1 4.0 %collective-permute-start.5 = (bf16[4,8,512]{2,1,0:T(8,128)(2,1)S(1)}, bf16[4,8,512]{2,1,0:T(8,128)(2,1)S(1)}, u32[]{:S(2)}, u32[]{:S(2)}) collective-permute-start(bf16[4,8,512]{2,1,0:T(8,128)(2,1)S(1)} %get-tuple-element.47), channel_id=1, source_target_pairs={{0,8},{4,12},{8,16},{12,20},{16,24},{20,28},{24,32},{28,36},{32,40... | collective-permute-start | bytes 98312 | tf_op jit(solution)/shard_map/ppermute | solution.py:303
  72.1 0.7 collective-permute-start.4
  72.8 0.0 collective-permute-done.7
  72.8 0.0 collective-permute-done.6
  72.8 1.1 collective-permute-done.5
  73.9 0.0 collective-permute-done.4
  73.9 0.7 maximum_bitcast_fusion
  74.6 6.9 %all-to-all-start.2 = ((bf16[4,32,512]{2,1,0:T(8,128)(2,1)}), bf16[4,32,512]{2,1,0:T(8,128)(2,1)S(1)}, u32[]{:S(2)}, u32[]{:S(2)}) async-start(bf16[4,32,512]{2,1,0:T(8,128)(2,1)} %maximum_bitcast_fusion), calls=%async_computation.2 | async-start | bytes 262144 | tf_op jit(solution)/shard_map/all_to_all | solution.py:305
  81.4 2.4 %short.1.base = f32[512,512]{1,0:T(8,128)S(1)} custom-call(bf16[512,512]{1,0:T(8,128)(2,1)} %get-tuple-element.37.latent, bf16[512,512]{1,0:T(8,128)(2,1)} %get-tuple-element.38.message, s32[6,512]{1,0:T(8,128)} %bitcast.61), custom_call_target="tpu_custom_call" | custom-call | tf_op jit(solution)/shard_map/short/pallas_call | solution.py:270
  83.8 2.1 %all-to-all-done.2 = bf16[4,32,512]{2,1,0:T(8,128)(2,1)S(1)} async-done(((bf16[4,32,512]{2,1,0:T(8,128)(2,1)}), bf16[4,32,512]{2,1,0:T(8,128)(2,1)S(1)}, u32[]{:S(2)}, u32[]{:S(2)}) %all-to-all-start.2) | async-done | bytes 131104 | tf_op jit(solution)/shard_map/all_to_all | solution.py:305
  86.0 0.0 copy-start.3
  86.0 0.0 copy-done.7
  86.0 0.7 decode.1.block
  86.7 0.0 copy-start.1
  86.7 4.0 %collective-permute-start.8 = (bf16[512,512]{1,0:T(8,128)(2,1)S(1)}, bf16[512,512]{1,0:T(8,128)(2,1)S(1)}, u32[]{:S(2)}, u32[]{:S(2)}) collective-permute-start(bf16[512,512]{1,0:T(8,128)(2,1)S(1)} %decode.1.block), channel_id=1, source_target_pairs={{0,504},{4,12},{8,0},{12,20},{16,8},{20,28},{24,16},{28,36},{32,24... | collective-permute-start | bytes 1572872 | tf_op jit(solution)/shard_map/ppermute | solution.py:43
  90.7 2.1 %collective-permute-start.10 = (bf16[512,512]{1,0:T(8,128)(2,1)S(1)}, bf16[512,512]{1,0:T(8,128)(2,1)S(1)}, u32[]{:S(2)}, u32[]{:S(2)}) collective-permute-start(bf16[512,512]{1,0:T(8,128)(2,1)S(1)} %decode.1.block), channel_id=1, source_target_pairs={{0,8},{4,508},{8,16},{12,4},{16,24},{20,12},{24,32},{28,20},{32,40... | collective-permute-start | bytes 1572872 | tf_op jit(solution)/shard_map/ppermute | solution.py:43
  92.8 2.1 %collective-permute-start.9 = (bf16[512,512]{1,0:T(8,128)(2,1)S(1)}, bf16[512,512]{1,0:T(8,128)(2,1)S(1)}, u32[]{:S(2)}, u32[]{:S(2)}) collective-permute-start(bf16[512,512]{1,0:T(8,128)(2,1)S(1)} %decode.1.block), channel_id=1, source_target_pairs={{0,4},{4,0},{8,12},{12,8},{16,20},{20,16},{24,28},{28,24},{32,36},... | collective-permute-start | bytes 1572872 | tf_op jit(solution)/shard_map/ppermute | solution.py:43
  94.9 0.0 copy-done.3
  95.0 1.2 own.1.before
  96.1 5.9 %collective-permute-done.8.rest_1_ = bf16[512,512]{1,0:T(8,128)(2,1)S(1)} collective-permute-done((bf16[512,512]{1,0:T(8,128)(2,1)S(1)}, bf16[512,512]{1,0:T(8,128)(2,1)S(1)}, u32[]{:S(2)}, u32[]{:S(2)}) %collective-permute-start.8) | collective-permute-done | bytes 524320 | tf_op jit(solution)/shard_map/ppermute | solution.py:43
  102.1 1.9 %collective-permute-start.11 = (bf16[512,512]{1,0:T(8,128)(2,1)S(1)}, bf16[512,512]{1,0:T(8,128)(2,1)S(1)}, u32[]{:S(2)}, u32[]{:S(2)}) collective-permute-start(bf16[512,512]{1,0:T(8,128)(2,1)S(1)} %collective-permute-done.8.rest_1_), channel_id=1, source_target_pairs={{0,508},{4,8},{8,4},{12,16},{16,12},{20,24},{24,20},{28,32},{32,28... | collective-permute-start | bytes 1572872 | tf_op jit(solution)/shard_map/ppermute | solution.py:43
  104.0 1.9 %collective-permute-start.12 = (bf16[512,512]{1,0:T(8,128)(2,1)S(1)}, bf16[512,512]{1,0:T(8,128)(2,1)S(1)}, u32[]{:S(2)}, u32[]{:S(2)}) collective-permute-start(bf16[512,512]{1,0:T(8,128)(2,1)S(1)} %collective-permute-done.8.rest_1_), channel_id=1, source_target_pairs={{0,4},{4,0},{8,12},{12,8},{16,20},{20,16},{24,28},{28,24},{32,36},... | collective-permute-start | bytes 1572872 | tf_op jit(solution)/shard_map/ppermute | solution.py:43
  105.9 0.0 collective-permute-done.10.rest_2_
  105.9 2.4 %collective-permute-start.13 = (bf16[512,512]{1,0:T(8,128)(2,1)S(1)}, bf16[512,512]{1,0:T(8,128)(2,1)S(1)}, u32[]{:S(2)}, u32[]{:S(2)}) collective-permute-start(bf16[512,512]{1,0:T(8,128)(2,1)S(1)} %collective-permute-done.10.rest_2_), channel_id=1, source_target_pairs={{0,4},{4,0},{8,12},{12,8},{16,20},{20,16},{24,28},{28,24},{32,36},... | collective-permute-start | bytes 1572872 | tf_op jit(solution)/shard_map/ppermute | solution.py:43
  108.3 0.0 collective-permute-done.9.rest_0_
  108.3 0.0 copy-done.1
  108.3 0.0 copy-start.2
  108.4 1.8 %near.1.before = f32[1024,512]{1,0:T(8,128)S(1)} custom-call(f32[1024,512]{1,0:T(8,128)S(1)} %own.1.before, bf16[512,512]{1,0:T(8,128)(2,1)S(1)} %collective-permute-done.9.rest_0_, bf16[512,512]{1,0:T(8,128)(2,1)S(1)} %collective-permute-done.8.rest_1_, bf16[512,512]{1,0:T(8,128)(2,1)S(1)} %collective-permute-done.10.rest_2_, bf16[1024,1536]{1,0:T(8,128)(2,1)S(1)} %copy-done.1), custom_call_target="tpu_custom_call" | custom-call | tf_op jit(solution)/shard_map/near/pallas_call | solution.py:270
  110.2 5.7 %collective-permute-done.11.rest_0_ = bf16[512,512]{1,0:T(8,128)(2,1)S(1)} collective-permute-done((bf16[512,512]{1,0:T(8,128)(2,1)S(1)}, bf16[512,512]{1,0:T(8,128)(2,1)S(1)}, u32[]{:S(2)}, u32[]{:S(2)}) %collective-permute-start.11) | collective-permute-done | bytes 524320 | tf_op jit(solution)/shard_map/ppermute | solution.py:43
  115.9 0.0 collective-permute-done.12.rest_1_
  115.9 0.0 collective-permute-done.13.rest_2_
  115.9 0.0 copy-done.2
  115.9 2.5 %collect.1 = bf16[1024,512]{1,0:T(8,128)(2,1)} custom-call(f32[1024,512]{1,0:T(8,128)S(1)} %near.1.before, bf16[512,512]{1,0:T(8,128)(2,1)S(1)} %collective-permute-done.11.rest_0_, bf16[512,512]{1,0:T(8,128)(2,1)S(1)} %collective-permute-done.12.rest_1_, bf16[512,512]{1,0:T(8,128)(2,1)S(1)} %collective-permute-done.13.rest_2_, bf16[1024,1536]{1,0:T(8,128)(2,1)S(1)} %copy-done.2), custom_call_target="tpu_custom_call" | custom-call | tf_op jit(solution)/shard_map/collect/pallas_call | solution.py:270
  (3 shorter events, 0.0 us)
Async XLA Ops:
  2.6 9.5 %copy-start = (bf16[1024,227]{0,1:T(8,128)(2,1)S(1)}, bf16[1024,227]{0,1:T(8,128)(2,1)}, u32[]{:S(2)}) copy-start(bf16[1024,227]{0,1:T(8,128)(2,1)} %param.12) | copy-start | bytes 1394692
  2.6 9.5 %copy-start.5 = (s32[1,1,7,384]{3,1,2,0:T(1,128)S(1)}, s32[1,1,7,384]{3,1,2,0:T(1,128)}, u32[]{:S(2)}) copy-start(s32[1,1,7,384]{3,1,2,0:T(1,128)} %param.18) | copy-start | bytes 32260
  2.6 37.6 %all-to-all-start = ((bf16[4,128,1792]{2,1,0:T(8,128)(2,1)}), bf16[4,128,1792]{2,1,0:T(8,128)(2,1)S(1)}, u32[]{:S(2)}, u32[]{:S(2)}) async-start(bf16[4,128,1792]{2,1,0:T(8,128)(2,1)} %weights.1), calls=%async_computation | async-start | bytes 3670016 | tf_op jit(solution)/shard_map/all_to_all | solution.py:356
  12.1 28.1 %copy-start.4 = (s32[1,1,7,384]{3,1,2,0:T(1,128)S(1)}, s32[1,1,7,384]{3,1,2,0:T(1,128)}, u32[]{:S(2)}) copy-start(s32[1,1,7,384]{3,1,2,0:T(1,128)} %param.19) | copy-start | bytes 32260
  13.8 23.6 %collective-permute-start.1 = (bf16[2,240,384]{2,1,0:T(8,128)(2,1)S(1)}, bf16[2,240,384]{2,1,0:T(8,128)(2,1)S(1)}, u32[]{:S(2)}, u32[]{:S(2)}) collective-permute-start(bf16[2,240,384]{2,1,0:T(8,128)(2,1)S(1)} %get-tuple-element.27), channel_id=1, source_target_pairs={{0,8},{4,12},{8,16},{12,20},{16,24},{20,28},{24,32},{28,36},{32,40... | collective-permute-start | bytes 1105928 | tf_op jit(solution)/shard_map/ppermute | solution.py:37
  15.7 21.7 %collective-permute-start.2 = (bf16[2,240,384]{2,1,0:T(8,128)(2,1)S(1)}, bf16[2,240,384]{2,1,0:T(8,128)(2,1)S(1)}, u32[]{:S(2)}, u32[]{:S(2)}) collective-permute-start(bf16[2,240,384]{2,1,0:T(8,128)(2,1)S(1)} %get-tuple-element.31), channel_id=1, source_target_pairs={{0,504},{4,508},{8,0},{12,4},{16,8},{20,12},{24,16},{28,20},{32,24... | collective-permute-start | bytes 1105928 | tf_op jit(solution)/shard_map/ppermute | solution.py:37
  24.9 12.5 %collective-permute-start = (bf16[240,384]{1,0:T(8,128)(2,1)S(1)}, bf16[240,384]{1,0:T(8,128)(2,1)S(1)}, u32[]{:S(2)}, u32[]{:S(2)}) collective-permute-start(bf16[240,384]{1,0:T(8,128)(2,1)S(1)} %get-tuple-element.26), channel_id=1, source_target_pairs={{0,500},{4,16},{8,508},{12,24},{16,4},{20,32},{24,12},{28,40},{32,... | collective-permute-start | bytes 552968 | tf_op jit(solution)/shard_map/ppermute | solution.py:43
  38.3 5.6 %collective-permute-start.3 = (bf16[3,240,384]{2,1,0:T(8,128)(2,1)}, bf16[3,240,384]{2,1,0:T(8,128)(2,1)}, u32[]{:S(2)}, u32[]{:S(2)}) collective-permute-start(bf16[3,240,384]{2,1,0:T(8,128)(2,1)} %pad_maximum_fusion), channel_id=1, source_target_pairs={{0,4},{4,0},{8,12},{12,8},{16,20},{20,16},{24,28},{28,24},{32,36},... | collective-permute-start | bytes 1658888 | tf_op jit(solution)/shard_map/ppermute | solution.py:43
  40.3 3.7 %copy-start.6 = (s32[1,1,128,8]{2,3,1,0:T(8,128)S(1)}, s32[1,1,128,8]{2,3,1,0:T(8,128)}, u32[]{:S(2)}) copy-start(s32[1,1,128,8]{2,3,1,0:T(8,128)} %param.20) | copy-start | bytes 12292
  48.3 37.7 %copy-start.7 = (s32[1,1,128,8]{2,3,1,0:T(8,128)S(1)}, s32[1,1,128,8]{2,3,1,0:T(8,128)}, u32[]{:S(2)}) copy-start(s32[1,1,128,8]{2,3,1,0:T(8,128)} %param.21) | copy-start | bytes 12292
  57.5 15.3 %collective-permute-start.7 = (bf16[4,8,512]{2,1,0:T(8,128)(2,1)S(1)}, bf16[4,8,512]{2,1,0:T(8,128)(2,1)S(1)}, u32[]{:S(2)}, u32[]{:S(2)}) collective-permute-start(bf16[4,8,512]{2,1,0:T(8,128)(2,1)S(1)} %get-tuple-element.48), channel_id=1, source_target_pairs={{0,64},{4,68},{8,72},{12,76},{16,80},{20,84},{24,88},{28,92},{32,9... | collective-permute-start | bytes 98312 | tf_op jit(solution)/shard_map/ppermute | solution.py:303
  66.2 6.6 %collective-permute-start.6 = (bf16[4,8,512]{2,1,0:T(8,128)(2,1)S(1)}, bf16[4,8,512]{2,1,0:T(8,128)(2,1)S(1)}, u32[]{:S(2)}, u32[]{:S(2)}) collective-permute-start(bf16[4,8,512]{2,1,0:T(8,128)(2,1)S(1)} %get-tuple-element.46), channel_id=1, source_target_pairs={{0,4},{4,8},{8,12},{12,16},{16,20},{20,24},{24,28},{28,32},{32,36}... | collective-permute-start | bytes 98312 | tf_op jit(solution)/shard_map/ppermute | solution.py:303
  68.1 5.8 %collective-permute-start.5 = (bf16[4,8,512]{2,1,0:T(8,128)(2,1)S(1)}, bf16[4,8,512]{2,1,0:T(8,128)(2,1)S(1)}, u32[]{:S(2)}, u32[]{:S(2)}) collective-permute-start(bf16[4,8,512]{2,1,0:T(8,128)(2,1)S(1)} %get-tuple-element.47), channel_id=1, source_target_pairs={{0,8},{4,12},{8,16},{12,20},{16,24},{20,28},{24,32},{28,36},{32,40... | collective-permute-start | bytes 98312 | tf_op jit(solution)/shard_map/ppermute | solution.py:303
  72.1 1.8 %collective-permute-start.4 = (bf16[4,8,512]{2,1,0:T(8,128)(2,1)S(1)}, bf16[4,8,512]{2,1,0:T(8,128)(2,1)S(1)}, u32[]{:S(2)}, u32[]{:S(2)}) collective-permute-start(bf16[4,8,512]{2,1,0:T(8,128)(2,1)S(1)} %get-tuple-element.45), channel_id=1, source_target_pairs={{2,258},{6,262},{10,266},{14,270},{18,274},{22,278},{26,282},{30,2... | collective-permute-start | bytes 98312 | tf_op jit(solution)/shard_map/ppermute | solution.py:303
  74.6 11.4 %all-to-all-start.2 = ((bf16[4,32,512]{2,1,0:T(8,128)(2,1)}), bf16[4,32,512]{2,1,0:T(8,128)(2,1)S(1)}, u32[]{:S(2)}, u32[]{:S(2)}) async-start(bf16[4,32,512]{2,1,0:T(8,128)(2,1)} %maximum_bitcast_fusion), calls=%async_computation.2 | async-start | bytes 262144 | tf_op jit(solution)/shard_map/all_to_all | solution.py:305
  86.0 9.0 %copy-start.3 = (bf16[1024,512]{1,0:T(8,128)(2,1)S(1)}, bf16[1024,512]{1,0:T(8,128)(2,1)}, u32[]{:S(2)}) copy-start(bf16[1024,512]{1,0:T(8,128)(2,1)} %get-tuple-element.40.table) | copy-start | bytes 3145732
  86.7 21.6 %copy-start.1 = (bf16[1024,1536]{1,0:T(8,128)(2,1)S(1)}, bf16[1024,1536]{1,0:T(8,128)(2,1)}, u32[]{:S(2)}) copy-start(bf16[1024,1536]{1,0:T(8,128)(2,1)} %get-tuple-element.43.rest_3_) | copy-start | bytes 9437188
  86.7 15.3 %collective-permute-start.8 = (bf16[512,512]{1,0:T(8,128)(2,1)S(1)}, bf16[512,512]{1,0:T(8,128)(2,1)S(1)}, u32[]{:S(2)}, u32[]{:S(2)}) collective-permute-start(bf16[512,512]{1,0:T(8,128)(2,1)S(1)} %decode.1.block), channel_id=1, source_target_pairs={{0,504},{4,12},{8,0},{12,20},{16,8},{20,28},{24,16},{28,36},{32,24... | collective-permute-start | bytes 1572872 | tf_op jit(solution)/shard_map/ppermute | solution.py:43
  90.7 15.2 %collective-permute-start.10 = (bf16[512,512]{1,0:T(8,128)(2,1)S(1)}, bf16[512,512]{1,0:T(8,128)(2,1)S(1)}, u32[]{:S(2)}, u32[]{:S(2)}) collective-permute-start(bf16[512,512]{1,0:T(8,128)(2,1)S(1)} %decode.1.block), channel_id=1, source_target_pairs={{0,8},{4,508},{8,16},{12,4},{16,24},{20,12},{24,32},{28,20},{32,40... | collective-permute-start | bytes 1572872 | tf_op jit(solution)/shard_map/ppermute | solution.py:43
  92.8 15.5 %collective-permute-start.9 = (bf16[512,512]{1,0:T(8,128)(2,1)S(1)}, bf16[512,512]{1,0:T(8,128)(2,1)S(1)}, u32[]{:S(2)}, u32[]{:S(2)}) collective-permute-start(bf16[512,512]{1,0:T(8,128)(2,1)S(1)} %decode.1.block), channel_id=1, source_target_pairs={{0,4},{4,0},{8,12},{12,8},{16,20},{20,16},{24,28},{28,24},{32,36},... | collective-permute-start | bytes 1572872 | tf_op jit(solution)/shard_map/ppermute | solution.py:43
  102.1 13.8 %collective-permute-start.11 = (bf16[512,512]{1,0:T(8,128)(2,1)S(1)}, bf16[512,512]{1,0:T(8,128)(2,1)S(1)}, u32[]{:S(2)}, u32[]{:S(2)}) collective-permute-start(bf16[512,512]{1,0:T(8,128)(2,1)S(1)} %collective-permute-done.8.rest_1_), channel_id=1, source_target_pairs={{0,508},{4,8},{8,4},{12,16},{16,12},{20,24},{24,20},{28,32},{32,28... | collective-permute-start | bytes 1572872 | tf_op jit(solution)/shard_map/ppermute | solution.py:43
  104.0 11.9 %collective-permute-start.12 = (bf16[512,512]{1,0:T(8,128)(2,1)S(1)}, bf16[512,512]{1,0:T(8,128)(2,1)S(1)}, u32[]{:S(2)}, u32[]{:S(2)}) collective-permute-start(bf16[512,512]{1,0:T(8,128)(2,1)S(1)} %collective-permute-done.8.rest_1_), channel_id=1, source_target_pairs={{0,4},{4,0},{8,12},{12,8},{16,20},{20,16},{24,28},{28,24},{32,36},... | collective-permute-start | bytes 1572872 | tf_op jit(solution)/shard_map/ppermute | solution.py:43
  105.9 10.0 %collective-permute-start.13 = (bf16[512,512]{1,0:T(8,128)(2,1)S(1)}, bf16[512,512]{1,0:T(8,128)(2,1)S(1)}, u32[]{:S(2)}, u32[]{:S(2)}) collective-permute-start(bf16[512,512]{1,0:T(8,128)(2,1)S(1)} %collective-permute-done.10.rest_2_), channel_id=1, source_target_pairs={{0,4},{4,0},{8,12},{12,8},{16,20},{20,16},{24,28},{28,24},{32,36},... | collective-permute-start | bytes 1572872 | tf_op jit(solution)/shard_map/ppermute | solution.py:43
  108.3 7.5 %copy-start.2 = (bf16[1024,1536]{1,0:T(8,128)(2,1)S(1)}, bf16[1024,1536]{1,0:T(8,128)(2,1)}, u32[]{:S(2)}) copy-start(bf16[1024,1536]{1,0:T(8,128)(2,1)} %get-tuple-element.44.rest_3_) | copy-start | bytes 9437188

commit v7 on v6

--- a/solution.py
+++ b/solution.py
@@ -284,7 +284,7 @@
     return pltpu.VMEM(dims, kind)
 
 
-def far_exchange(rows):
+def far_exchange(rows, beside):
     patches, chans = lax.axis_size("patch"), lax.axis_size("chan")
     kinds = len(FAR[0])
     count, channels = rows.shape
@@ -292,6 +292,7 @@
     mine = lax.all_to_all(
         rows.reshape(chans, kinds * each, channels), "chan", 0, 0, tiled=True
     ).reshape(chans, kinds, each, channels)
+    mine, beside = lax.optimization_barrier((mine, beside))
     arrived = []
     for kind in range(kinds):
         pairs = []
@@ -302,7 +303,7 @@
                 pairs.append((p * chans + c, (p + FAR[c][kind]) % patches * chans + c))
         arrived.append(lax.ppermute(mine[:, kind], ("patch", "chan"), pairs))
     back = jnp.stack(arrived, axis=1).reshape(chans, kinds * each, channels)
-    return lax.all_to_all(back, "chan", 0, 0, tiled=True).reshape(count, channels)
+    return lax.all_to_all(back, "chan", 0, 0, tiled=True).reshape(count, channels), beside
 
 
 def shards(
@@ -396,7 +397,7 @@
         name="short",
         stored=(mesh_latent, node_msg, loc_nbr.T),
     )
-    arrived = far_exchange(far_sent)
+    arrived, base = far_exchange(far_sent, base)
     dec_msg = call(
         decode_body,
         shape(nodes, channels),

time: 119 us -> 119 us (level)
  blocking collectives: 9.24 us -> 11.2 us
  starting transfers between devices: 61.7 us -> 59.9 us
    all_to_all x1, blocking collectives: 9.24 us -> 11.2 us  [far_exchange(): lax.all_to_all(back, 'chan', 0, 0, tiled=True).reshape(count, channels)]
    all_to_all x1, starting transfers between devices: 6.87 us -> 4.93 us  [far_exchange(): lax.all_to_all(rows.reshape(chans, kinds * each, channels), 'chan', 0, 0,...]
where the time goes in v7:
time: 119 us; the launch traced here: 118 us
  starting transfers between devices  59.9 us (50%)
  Pallas kernels  28 us (24%)
  waiting for transfers between devices  17.8 us (15%)
  blocking collectives  11.2 us (9%)
    pallas_call x10, Pallas kernels, call(): pl.pallas_call(body, out_shape=out_shape, in_specs=[smem if a.ndim == 1 e...  28 us
    ppermute x8, starting transfers between devices, by_core(): return lax.ppermute(value, 'patch', pairs)  18.9 us
    ppermute x4, starting transfers between devices, far_exchange(): arrived.append(lax.ppermute(mine[:, kind], ('patch', 'chan'), pairs))  15.5 us
    ppermute x8, waiting for transfers between devices, by_core(): return lax.ppermute(value, 'patch', pairs)  14.6 us
    all_to_all x1, blocking collectives, far_exchange(): lax.all_to_all(back, 'chan', 0, 0, tiled=True).reshape(count, channels)  11.2 us
    ppermute x2, starting transfers between devices, shifted(): lax.ppermute(value, 'patch', [(i, (i + steps) % count) for i in range(cou...  11.1 us
    all_to_all x1, starting transfers between devices, shards(): lax.all_to_all(copies, 'chan', 0, 0, tiled=True).reshape(chans * width, -1)  9.5 us
    all_to_all x1, starting transfers between devices, far_exchange(): lax.all_to_all(rows.reshape(chans, kinds * each, channels), 'chan', 0, 0,...  4.93 us
  transfers between devices with their start and end apart: 16, of which 5 were waited for; matrix products, arithmetic and copies ran while one was open for 1% of the time, Pallas kernels for 15%

profile of v7, /device:TPU:8, one launch (start us, length us, event | category | flops | bytes accessed | tf_op | source)
XLA Modules:
  0.0 118.4 jit_solution(13837046142987490558)
XLA Ops:
  0.0 2.6 %weights.1 = bf16[4,128,1792]{2,1,0:T(8,128)(2,1)} custom-call(bf16[227,128]{1,0:T(8,128)(2,1)} %embed.2, bf16[512,128]{1,0:T(8,128)(2,1)} %edge.1, bf16[512,128]{1,0:T(8,128)(2,1)} %proc.1, bf16[512,128]{1,0:T(8,128)(2,1)} %dec.1), custom_call_target="tpu_custom_call" | custom-call | tf_op jit(solution)/shard_map/weights/pallas_call | solution.py:270
  2.6 0.0 copy-start
  2.6 0.0 copy-start.5
  2.6 9.5 %all-to-all-start = ((bf16[4,128,1792]{2,1,0:T(8,128)(2,1)}), bf16[4,128,1792]{2,1,0:T(8,128)(2,1)S(1)}, u32[]{:S(2)}, u32[]{:S(2)}) async-start(bf16[4,128,1792]{2,1,0:T(8,128)(2,1)} %weights.1), calls=%async_computation | async-start | bytes 3670016 | tf_op jit(solution)/shard_map/all_to_all | solution.py:357
  12.1 0.0 copy-start.4
  12.1 0.0 copy-done
  12.1 0.0 copy-done.5
  12.1 1.6 %pack.1 = (bf16[240,384]{1,0:T(8,128)(2,1)S(1)}, bf16[2,240,384]{2,1,0:T(8,128)(2,1)S(1)}, bf16[2,240,384]{2,1,0:T(8,128)(2,1)S(1)}, bf16[240,384]{1,0:T(8,128)(2,1)S(1)}) custom-call(s32[1]{0:T(128)} %bitcast.1.core, bf16[227,1024]{1,0:T(8,128)(2,1)S(1)} %bitcast.36, s32[7,1,384]{2,1,0:T(1,128)S(1)} %bitcast.43), custom_call_target="tpu_custom_call" | custom-call | tf_op jit(solution)/shard_map/pack/pallas_call | solution.py:270
  13.8 1.9 %collective-permute-start.1 = (bf16[2,240,384]{2,1,0:T(8,128)(2,1)S(1)}, bf16[2,240,384]{2,1,0:T(8,128)(2,1)S(1)}, u32[]{:S(2)}, u32[]{:S(2)}) collective-permute-start(bf16[2,240,384]{2,1,0:T(8,128)(2,1)S(1)} %get-tuple-element.29), channel_id=1, source_target_pairs={{0,8},{4,12},{8,16},{12,20},{16,24},{20,28},{24,32},{28,36},{32,40... | collective-permute-start | bytes 1105928 | tf_op jit(solution)/shard_map/ppermute | solution.py:37
  15.7 9.1 %collective-permute-start.2 = (bf16[2,240,384]{2,1,0:T(8,128)(2,1)S(1)}, bf16[2,240,384]{2,1,0:T(8,128)(2,1)S(1)}, u32[]{:S(2)}, u32[]{:S(2)}) collective-permute-start(bf16[2,240,384]{2,1,0:T(8,128)(2,1)S(1)} %get-tuple-element.33), channel_id=1, source_target_pairs={{0,504},{4,508},{8,0},{12,4},{16,8},{20,12},{24,16},{28,20},{32,24... | collective-permute-start | bytes 1105928 | tf_op jit(solution)/shard_map/ppermute | solution.py:37
  24.9 2.7 %collective-permute-start = (bf16[240,384]{1,0:T(8,128)(2,1)S(1)}, bf16[240,384]{1,0:T(8,128)(2,1)S(1)}, u32[]{:S(2)}, u32[]{:S(2)}) collective-permute-start(bf16[240,384]{1,0:T(8,128)(2,1)S(1)} %get-tuple-element.28), channel_id=1, source_target_pairs={{0,500},{4,16},{8,508},{12,24},{16,4},{20,32},{24,12},{28,40},{32,... | collective-permute-start | bytes 552968 | tf_op jit(solution)/shard_map/ppermute | solution.py:43
  27.5 7.2 %tables.1 = (bf16[1024,512]{1,0:T(8,128)(2,1)}, bf16[1024,1536]{1,0:T(8,128)(2,1)}, bf16[1024,1536]{1,0:T(8,128)(2,1)}) custom-call(s32[1]{0:T(128)} %bitcast.1.core, s32[3,1024]{1,0:T(4,128)} %bitcast.53), custom_call_target="tpu_custom_call" | custom-call | tf_op jit(solution)/shard_map/tables/pallas_call | solution.py:270
  34.7 2.6 %collective-permute-done.three = bf16[240,384]{1,0:T(8,128)(2,1)S(1)} collective-permute-done((bf16[240,384]{1,0:T(8,128)(2,1)S(1)}, bf16[240,384]{1,0:T(8,128)(2,1)S(1)}, u32[]{:S(2)}, u32[]{:S(2)}) %collective-permute-start) | collective-permute-done | bytes 184352 | tf_op jit(solution)/shard_map/ppermute | solution.py:43
  37.4 0.0 collective-permute-done.1.up
  37.4 0.0 collective-permute-done.2.down
  37.4 0.9 pad_maximum_fusion
  38.3 1.9 %collective-permute-start.3 = (bf16[3,240,384]{2,1,0:T(8,128)(2,1)}, bf16[3,240,384]{2,1,0:T(8,128)(2,1)}, u32[]{:S(2)}, u32[]{:S(2)}) collective-permute-start(bf16[3,240,384]{2,1,0:T(8,128)(2,1)} %pad_maximum_fusion), channel_id=1, source_target_pairs={{0,4},{4,0},{8,12},{12,8},{16,20},{20,16},{24,28},{28,24},{32,36},... | collective-permute-start | bytes 1658888 | tf_op jit(solution)/shard_map/ppermute | solution.py:43
  40.2 0.0 all-to-all-done
  40.3 0.0 copy-done.4
  40.3 0.0 copy-start.6
  40.3 3.7 %early.1 = f32[512,512]{1,0:T(8,128)S(1)} custom-call(s32[1]{0:T(128)} %bitcast.1.core, bf16[227,1024]{1,0:T(8,128)(2,1)S(1)} %bitcast.37, s32[7,1,384]{2,1,0:T(1,128)S(1)} %bitcast.44, bf16[2,240,384]{2,1,0:T(8,128)(2,1)S(1)} %collective-permute-done.1.up, bf16[2,240,384]{2,1,0:T(8,128)(2,1)S(1)} %collective-permute-done.2.down, ...), custom_call_target="tpu_custom_call" | custom-call | tf_op jit(solution)/shard_map/early/pallas_call | solution.py:270
  43.9 0.0 collective-permute-done.3.sib
  44.0 0.0 copy-done.6
  44.0 4.3 %encode.1 = (bf16[512,512]{1,0:T(8,128)(2,1)}, bf16[512,512]{1,0:T(8,128)(2,1)}, bf16[128,512]{1,0:T(8,128)(2,1)}) custom-call(s32[1]{0:T(128)} %bitcast.1.core, s32[1]{0:T(128)} %bitcast.here, f32[512,512]{1,0:T(8,128)S(1)} %early.1, bf16[3,240,384]{2,1,0:T(8,128)(2,1)} %collective-permute-done.3.sib, bf16[512,1792]{1,0:T(8,128)(2,1)S(1)} %bitcast.33, ...), custom_call_target="tpu_custom_call" | custom-call | tf_op jit(solution)/shard_map/encode/pallas_call | solution.py:270
  48.3 0.0 copy-start.7
  48.3 4.9 %all-to-all-start.1 = ((bf16[4,32,512]{2,1,0:T(8,128)(2,1)}), bf16[4,32,512]{2,1,0:T(8,128)(2,1)S(1)}, u32[]{:S(2)}, u32[]{:S(2)}) async-start(bf16[4,32,512]{2,1,0:T(8,128)(2,1)} %bitcast.10), calls=%async_computation.1 | async-start | bytes 262144 | tf_op jit(solution)/shard_map/all_to_all | solution.py:292
  53.2 2.4 %short.1.base = f32[512,512]{1,0:T(8,128)S(1)} custom-call(bf16[512,512]{1,0:T(8,128)(2,1)} %get-tuple-element.40.latent, bf16[512,512]{1,0:T(8,128)(2,1)} %get-tuple-element.41.message, s32[6,512]{1,0:T(8,128)} %bitcast.52), custom_call_target="tpu_custom_call" | custom-call | tf_op jit(solution)/shard_map/short/pallas_call | solution.py:270
  55.6 2.1 %all-to-all-done.1 = bf16[4,32,512]{2,1,0:T(8,128)(2,1)S(1)} async-done(((bf16[4,32,512]{2,1,0:T(8,128)(2,1)}), bf16[4,32,512]{2,1,0:T(8,128)(2,1)S(1)}, u32[]{:S(2)}, u32[]{:S(2)}) %all-to-all-start.1) | async-done | bytes 131104 | tf_op jit(solution)/shard_map/all_to_all | solution.py:292
  57.8 0.0 copy-start.3
  57.8 8.8 %collective-permute-start.7 = (bf16[4,8,512]{2,1,0:T(8,128)(2,1)S(1)}, bf16[4,8,512]{2,1,0:T(8,128)(2,1)S(1)}, u32[]{:S(2)}, u32[]{:S(2)}) collective-permute-start(bf16[4,8,512]{2,1,0:T(8,128)(2,1)S(1)} %get-tuple-element.50), channel_id=1, source_target_pairs={{0,64},{4,68},{8,72},{12,76},{16,80},{20,84},{24,88},{28,92},{32,9... | collective-permute-start | bytes 98312 | tf_op jit(solution)/shard_map/ppermute | solution.py:304
  66.5 2.1 %collective-permute-start.6 = (bf16[4,8,512]{2,1,0:T(8,128)(2,1)S(1)}, bf16[4,8,512]{2,1,0:T(8,128)(2,1)S(1)}, u32[]{:S(2)}, u32[]{:S(2)}) collective-permute-start(bf16[4,8,512]{2,1,0:T(8,128)(2,1)S(1)} %get-tuple-element.51), channel_id=1, source_target_pairs={{0,4},{4,8},{8,12},{12,16},{16,20},{20,24},{24,28},{28,32},{32,36}... | collective-permute-start | bytes 98312 | tf_op jit(solution)/shard_map/ppermute | solution.py:304
  68.6 4.0 %collective-permute-start.5 = (bf16[4,8,512]{2,1,0:T(8,128)(2,1)S(1)}, bf16[4,8,512]{2,1,0:T(8,128)(2,1)S(1)}, u32[]{:S(2)}, u32[]{:S(2)}) collective-permute-start(bf16[4,8,512]{2,1,0:T(8,128)(2,1)S(1)} %get-tuple-element.52), channel_id=1, source_target_pairs={{0,8},{4,12},{8,16},{12,20},{16,24},{20,28},{24,32},{28,36},{32,40... | collective-permute-start | bytes 98312 | tf_op jit(solution)/shard_map/ppermute | solution.py:304
  72.7 0.7 collective-permute-start.4
  73.3 0.0 collective-permute-done.7
  73.3 0.0 collective-permute-done.6
  73.3 1.1 collective-permute-done.5
  74.5 0.0 collective-permute-done.4
  74.5 11.2 %all_to_all.15 = bf16[4,32,512]{2,1,0:T(8,128)(2,1)S(1)} all-to-all(bf16[4,32,512]{2,1,0:T(8,128)(2,1)S(1)} %maximum_bitcast_fusion), channel_id=1, replica_groups=mesh['patch'=128,'chan'=4] {'chan'}, dimensions={0} | all-to-all | bytes 262144 | tf_op jit(solution)/shard_map/all_to_all | solution.py:306
  85.7 0.0 copy-done.7
  85.7 0.7 decode.1.block
  86.4 0.0 copy-start.1
  86.4 4.0 %collective-permute-start.8 = (bf16[512,512]{1,0:T(8,128)(2,1)S(1)}, bf16[512,512]{1,0:T(8,128)(2,1)S(1)}, u32[]{:S(2)}, u32[]{:S(2)}) collective-permute-start(bf16[512,512]{1,0:T(8,128)(2,1)S(1)} %decode.1.block), channel_id=1, source_target_pairs={{0,504},{4,12},{8,0},{12,20},{16,8},{20,28},{24,16},{28,36},{32,24... | collective-permute-start | bytes 1572872 | tf_op jit(solution)/shard_map/ppermute | solution.py:43
  90.4 2.1 %collective-permute-start.10 = (bf16[512,512]{1,0:T(8,128)(2,1)S(1)}, bf16[512,512]{1,0:T(8,128)(2,1)S(1)}, u32[]{:S(2)}, u32[]{:S(2)}) collective-permute-start(bf16[512,512]{1,0:T(8,128)(2,1)S(1)} %decode.1.block), channel_id=1, source_target_pairs={{0,8},{4,508},{8,16},{12,4},{16,24},{20,12},{24,32},{28,20},{32,40... | collective-permute-start | bytes 1572872 | tf_op jit(solution)/shard_map/ppermute | solution.py:43
  92.5 1.9 %collective-permute-start.9 = (bf16[512,512]{1,0:T(8,128)(2,1)S(1)}, bf16[512,512]{1,0:T(8,128)(2,1)S(1)}, u32[]{:S(2)}, u32[]{:S(2)}) collective-permute-start(bf16[512,512]{1,0:T(8,128)(2,1)S(1)} %decode.1.block), channel_id=1, source_target_pairs={{0,4},{4,0},{8,12},{12,8},{16,20},{20,16},{24,28},{28,24},{32,36},... | collective-permute-start | bytes 1572872 | tf_op jit(solution)/shard_map/ppermute | solution.py:43
  94.5 0.0 copy-done.3
  94.5 1.2 own.1.before
  95.6 6.3 %collective-permute-done.8.rest_1_ = bf16[512,512]{1,0:T(8,128)(2,1)S(1)} collective-permute-done((bf16[512,512]{1,0:T(8,128)(2,1)S(1)}, bf16[512,512]{1,0:T(8,128)(2,1)S(1)}, u32[]{:S(2)}, u32[]{:S(2)}) %collective-permute-start.8) | collective-permute-done | bytes 524320 | tf_op jit(solution)/shard_map/ppermute | solution.py:43
  101.9 1.9 %collective-permute-start.11 = (bf16[512,512]{1,0:T(8,128)(2,1)S(1)}, bf16[512,512]{1,0:T(8,128)(2,1)S(1)}, u32[]{:S(2)}, u32[]{:S(2)}) collective-permute-start(bf16[512,512]{1,0:T(8,128)(2,1)S(1)} %collective-permute-done.8.rest_1_), channel_id=1, source_target_pairs={{0,508},{4,8},{8,4},{12,16},{16,12},{20,24},{24,20},{28,32},{32,28... | collective-permute-start | bytes 1572872 | tf_op jit(solution)/shard_map/ppermute | solution.py:43
  103.8 1.9 %collective-permute-start.12 = (bf16[512,512]{1,0:T(8,128)(2,1)S(1)}, bf16[512,512]{1,0:T(8,128)(2,1)S(1)}, u32[]{:S(2)}, u32[]{:S(2)}) collective-permute-start(bf16[512,512]{1,0:T(8,128)(2,1)S(1)} %collective-permute-done.8.rest_1_), channel_id=1, source_target_pairs={{0,4},{4,0},{8,12},{12,8},{16,20},{20,16},{24,28},{28,24},{32,36},... | collective-permute-start | bytes 1572872 | tf_op jit(solution)/shard_map/ppermute | solution.py:43
  105.7 0.0 collective-permute-done.10.rest_2_
  105.7 2.4 %collective-permute-start.13 = (bf16[512,512]{1,0:T(8,128)(2,1)S(1)}, bf16[512,512]{1,0:T(8,128)(2,1)S(1)}, u32[]{:S(2)}, u32[]{:S(2)}) collective-permute-start(bf16[512,512]{1,0:T(8,128)(2,1)S(1)} %collective-permute-done.10.rest_2_), channel_id=1, source_target_pairs={{0,4},{4,0},{8,12},{12,8},{16,20},{20,16},{24,28},{28,24},{32,36},... | collective-permute-start | bytes 1572872 | tf_op jit(solution)/shard_map/ppermute | solution.py:43
  108.2 0.0 collective-permute-done.9.rest_0_
  108.2 0.0 copy-done.1
  108.2 0.0 copy-start.2
  108.2 1.8 %near.1.before = f32[1024,512]{1,0:T(8,128)S(1)} custom-call(f32[1024,512]{1,0:T(8,128)S(1)} %own.1.before, bf16[512,512]{1,0:T(8,128)(2,1)S(1)} %collective-permute-done.9.rest_0_, bf16[512,512]{1,0:T(8,128)(2,1)S(1)} %collective-permute-done.8.rest_1_, bf16[512,512]{1,0:T(8,128)(2,1)S(1)} %collective-permute-done.10.rest_2_, bf16[1024,1536]{1,0:T(8,128)(2,1)S(1)} %copy-done.1), custom_call_target="tpu_custom_call" | custom-call | tf_op jit(solution)/shard_map/near/pallas_call | solution.py:270
  110.0 5.7 %collective-permute-done.11.rest_0_ = bf16[512,512]{1,0:T(8,128)(2,1)S(1)} collective-permute-done((bf16[512,512]{1,0:T(8,128)(2,1)S(1)}, bf16[512,512]{1,0:T(8,128)(2,1)S(1)}, u32[]{:S(2)}, u32[]{:S(2)}) %collective-permute-start.11) | collective-permute-done | bytes 524320 | tf_op jit(solution)/shard_map/ppermute | solution.py:43
  115.7 0.0 collective-permute-done.12.rest_1_
  115.7 0.0 collective-permute-done.13.rest_2_
  115.7 0.0 copy-done.2
  115.7 2.5 %collect.1 = bf16[1024,512]{1,0:T(8,128)(2,1)} custom-call(f32[1024,512]{1,0:T(8,128)S(1)} %near.1.before, bf16[512,512]{1,0:T(8,128)(2,1)S(1)} %collective-permute-done.11.rest_0_, bf16[512,512]{1,0:T(8,128)(2,1)S(1)} %collective-permute-done.12.rest_1_, bf16[512,512]{1,0:T(8,128)(2,1)S(1)} %collective-permute-done.13.rest_2_, bf16[1024,1536]{1,0:T(8,128)(2,1)S(1)} %copy-done.2), custom_call_target="tpu_custom_call" | custom-call | tf_op jit(solution)/shard_map/collect/pallas_call | solution.py:270
  (4 shorter events, 0.1 us)
Async XLA Ops:
  2.6 9.5 %copy-start = (bf16[1024,227]{0,1:T(8,128)(2,1)S(1)}, bf16[1024,227]{0,1:T(8,128)(2,1)}, u32[]{:S(2)}) copy-start(bf16[1024,227]{0,1:T(8,128)(2,1)} %param.12) | copy-start | bytes 1394692
  2.6 9.5 %copy-start.5 = (s32[1,1,7,384]{3,1,2,0:T(1,128)S(1)}, s32[1,1,7,384]{3,1,2,0:T(1,128)}, u32[]{:S(2)}) copy-start(s32[1,1,7,384]{3,1,2,0:T(1,128)} %param.18) | copy-start | bytes 32260
  2.6 37.6 %all-to-all-start = ((bf16[4,128,1792]{2,1,0:T(8,128)(2,1)}), bf16[4,128,1792]{2,1,0:T(8,128)(2,1)S(1)}, u32[]{:S(2)}, u32[]{:S(2)}) async-start(bf16[4,128,1792]{2,1,0:T(8,128)(2,1)} %weights.1), calls=%async_computation | async-start | bytes 3670016 | tf_op jit(solution)/shard_map/all_to_all | solution.py:357
  12.1 28.1 %copy-start.4 = (s32[1,1,7,384]{3,1,2,0:T(1,128)S(1)}, s32[1,1,7,384]{3,1,2,0:T(1,128)}, u32[]{:S(2)}) copy-start(s32[1,1,7,384]{3,1,2,0:T(1,128)} %param.19) | copy-start | bytes 32260
  13.8 23.6 %collective-permute-start.1 = (bf16[2,240,384]{2,1,0:T(8,128)(2,1)S(1)}, bf16[2,240,384]{2,1,0:T(8,128)(2,1)S(1)}, u32[]{:S(2)}, u32[]{:S(2)}) collective-permute-start(bf16[2,240,384]{2,1,0:T(8,128)(2,1)S(1)} %get-tuple-element.29), channel_id=1, source_target_pairs={{0,8},{4,12},{8,16},{12,20},{16,24},{20,28},{24,32},{28,36},{32,40... | collective-permute-start | bytes 1105928 | tf_op jit(solution)/shard_map/ppermute | solution.py:37
  15.7 21.7 %collective-permute-start.2 = (bf16[2,240,384]{2,1,0:T(8,128)(2,1)S(1)}, bf16[2,240,384]{2,1,0:T(8,128)(2,1)S(1)}, u32[]{:S(2)}, u32[]{:S(2)}) collective-permute-start(bf16[2,240,384]{2,1,0:T(8,128)(2,1)S(1)} %get-tuple-element.33), channel_id=1, source_target_pairs={{0,504},{4,508},{8,0},{12,4},{16,8},{20,12},{24,16},{28,20},{32,24... | collective-permute-start | bytes 1105928 | tf_op jit(solution)/shard_map/ppermute | solution.py:37
  24.9 12.5 %collective-permute-start = (bf16[240,384]{1,0:T(8,128)(2,1)S(1)}, bf16[240,384]{1,0:T(8,128)(2,1)S(1)}, u32[]{:S(2)}, u32[]{:S(2)}) collective-permute-start(bf16[240,384]{1,0:T(8,128)(2,1)S(1)} %get-tuple-element.28), channel_id=1, source_target_pairs={{0,500},{4,16},{8,508},{12,24},{16,4},{20,32},{24,12},{28,40},{32,... | collective-permute-start | bytes 552968 | tf_op jit(solution)/shard_map/ppermute | solution.py:43
  38.3 5.6 %collective-permute-start.3 = (bf16[3,240,384]{2,1,0:T(8,128)(2,1)}, bf16[3,240,384]{2,1,0:T(8,128)(2,1)}, u32[]{:S(2)}, u32[]{:S(2)}) collective-permute-start(bf16[3,240,384]{2,1,0:T(8,128)(2,1)} %pad_maximum_fusion), channel_id=1, source_target_pairs={{0,4},{4,0},{8,12},{12,8},{16,20},{20,16},{24,28},{28,24},{32,36},... | collective-permute-start | bytes 1658888 | tf_op jit(solution)/shard_map/ppermute | solution.py:43
  40.3 3.7 %copy-start.6 = (s32[1,1,128,8]{2,3,1,0:T(8,128)S(1)}, s32[1,1,128,8]{2,3,1,0:T(8,128)}, u32[]{:S(2)}) copy-start(s32[1,1,128,8]{2,3,1,0:T(8,128)} %param.20) | copy-start | bytes 12292
  48.3 37.4 %copy-start.7 = (s32[1,1,128,8]{2,3,1,0:T(8,128)S(1)}, s32[1,1,128,8]{2,3,1,0:T(8,128)}, u32[]{:S(2)}) copy-start(s32[1,1,128,8]{2,3,1,0:T(8,128)} %param.21) | copy-start | bytes 12292
  48.3 9.5 %all-to-all-start.1 = ((bf16[4,32,512]{2,1,0:T(8,128)(2,1)}), bf16[4,32,512]{2,1,0:T(8,128)(2,1)S(1)}, u32[]{:S(2)}, u32[]{:S(2)}) async-start(bf16[4,32,512]{2,1,0:T(8,128)(2,1)} %bitcast.10), calls=%async_computation.1 | async-start | bytes 262144 | tf_op jit(solution)/shard_map/all_to_all | solution.py:292
  57.8 36.7 %copy-start.3 = (bf16[1024,512]{1,0:T(8,128)(2,1)S(1)}, bf16[1024,512]{1,0:T(8,128)(2,1)}, u32[]{:S(2)}) copy-start(bf16[1024,512]{1,0:T(8,128)(2,1)} %get-tuple-element.44.table) | copy-start | bytes 3145732
  57.8 15.6 %collective-permute-start.7 = (bf16[4,8,512]{2,1,0:T(8,128)(2,1)S(1)}, bf16[4,8,512]{2,1,0:T(8,128)(2,1)S(1)}, u32[]{:S(2)}, u32[]{:S(2)}) collective-permute-start(bf16[4,8,512]{2,1,0:T(8,128)(2,1)S(1)} %get-tuple-element.50), channel_id=1, source_target_pairs={{0,64},{4,68},{8,72},{12,76},{16,80},{20,84},{24,88},{28,92},{32,9... | collective-permute-start | bytes 98312 | tf_op jit(solution)/shard_map/ppermute | solution.py:304
  66.5 6.8 %collective-permute-start.6 = (bf16[4,8,512]{2,1,0:T(8,128)(2,1)S(1)}, bf16[4,8,512]{2,1,0:T(8,128)(2,1)S(1)}, u32[]{:S(2)}, u32[]{:S(2)}) collective-permute-start(bf16[4,8,512]{2,1,0:T(8,128)(2,1)S(1)} %get-tuple-element.51), channel_id=1, source_target_pairs={{0,4},{4,8},{8,12},{12,16},{16,20},{20,24},{24,28},{28,32},{32,36}... | collective-permute-start | bytes 98312 | tf_op jit(solution)/shard_map/ppermute | solution.py:304
  68.6 5.8 %collective-permute-start.5 = (bf16[4,8,512]{2,1,0:T(8,128)(2,1)S(1)}, bf16[4,8,512]{2,1,0:T(8,128)(2,1)S(1)}, u32[]{:S(2)}, u32[]{:S(2)}) collective-permute-start(bf16[4,8,512]{2,1,0:T(8,128)(2,1)S(1)} %get-tuple-element.52), channel_id=1, source_target_pairs={{0,8},{4,12},{8,16},{12,20},{16,24},{20,28},{24,32},{28,36},{32,40... | collective-permute-start | bytes 98312 | tf_op jit(solution)/shard_map/ppermute | solution.py:304
  72.7 1.8 %collective-permute-start.4 = (bf16[4,8,512]{2,1,0:T(8,128)(2,1)S(1)}, bf16[4,8,512]{2,1,0:T(8,128)(2,1)S(1)}, u32[]{:S(2)}, u32[]{:S(2)}) collective-permute-start(bf16[4,8,512]{2,1,0:T(8,128)(2,1)S(1)} %get-tuple-element.49), channel_id=1, source_target_pairs={{2,258},{6,262},{10,266},{14,270},{18,274},{22,278},{26,282},{30,2... | collective-permute-start | bytes 98312 | tf_op jit(solution)/shard_map/ppermute | solution.py:304
  86.4 21.8 %copy-start.1 = (bf16[1024,1536]{1,0:T(8,128)(2,1)S(1)}, bf16[1024,1536]{1,0:T(8,128)(2,1)}, u32[]{:S(2)}) copy-start(bf16[1024,1536]{1,0:T(8,128)(2,1)} %get-tuple-element.47.rest_3_) | copy-start | bytes 9437188
  86.4 15.5 %collective-permute-start.8 = (bf16[512,512]{1,0:T(8,128)(2,1)S(1)}, bf16[512,512]{1,0:T(8,128)(2,1)S(1)}, u32[]{:S(2)}, u32[]{:S(2)}) collective-permute-start(bf16[512,512]{1,0:T(8,128)(2,1)S(1)} %decode.1.block), channel_id=1, source_target_pairs={{0,504},{4,12},{8,0},{12,20},{16,8},{20,28},{24,16},{28,36},{32,24... | collective-permute-start | bytes 1572872 | tf_op jit(solution)/shard_map/ppermute | solution.py:43
  90.4 15.3 %collective-permute-start.10 = (bf16[512,512]{1,0:T(8,128)(2,1)S(1)}, bf16[512,512]{1,0:T(8,128)(2,1)S(1)}, u32[]{:S(2)}, u32[]{:S(2)}) collective-permute-start(bf16[512,512]{1,0:T(8,128)(2,1)S(1)} %decode.1.block), channel_id=1, source_target_pairs={{0,8},{4,508},{8,16},{12,4},{16,24},{20,12},{24,32},{28,20},{32,40... | collective-permute-start | bytes 1572872 | tf_op jit(solution)/shard_map/ppermute | solution.py:43
  92.5 15.6 %collective-permute-start.9 = (bf16[512,512]{1,0:T(8,128)(2,1)S(1)}, bf16[512,512]{1,0:T(8,128)(2,1)S(1)}, u32[]{:S(2)}, u32[]{:S(2)}) collective-permute-start(bf16[512,512]{1,0:T(8,128)(2,1)S(1)} %decode.1.block), channel_id=1, source_target_pairs={{0,4},{4,0},{8,12},{12,8},{16,20},{20,16},{24,28},{28,24},{32,36},... | collective-permute-start | bytes 1572872 | tf_op jit(solution)/shard_map/ppermute | solution.py:43
  101.9 13.8 %collective-permute-start.11 = (bf16[512,512]{1,0:T(8,128)(2,1)S(1)}, bf16[512,512]{1,0:T(8,128)(2,1)S(1)}, u32[]{:S(2)}, u32[]{:S(2)}) collective-permute-start(bf16[512,512]{1,0:T(8,128)(2,1)S(1)} %collective-permute-done.8.rest_1_), channel_id=1, source_target_pairs={{0,508},{4,8},{8,4},{12,16},{16,12},{20,24},{24,20},{28,32},{32,28... | collective-permute-start | bytes 1572872 | tf_op jit(solution)/shard_map/ppermute | solution.py:43
  103.8 11.9 %collective-permute-start.12 = (bf16[512,512]{1,0:T(8,128)(2,1)S(1)}, bf16[512,512]{1,0:T(8,128)(2,1)S(1)}, u32[]{:S(2)}, u32[]{:S(2)}) collective-permute-start(bf16[512,512]{1,0:T(8,128)(2,1)S(1)} %collective-permute-done.8.rest_1_), channel_id=1, source_target_pairs={{0,4},{4,0},{8,12},{12,8},{16,20},{20,16},{24,28},{28,24},{32,36},... | collective-permute-start | bytes 1572872 | tf_op jit(solution)/shard_map/ppermute | solution.py:43
  105.7 10.0 %collective-permute-start.13 = (bf16[512,512]{1,0:T(8,128)(2,1)S(1)}, bf16[512,512]{1,0:T(8,128)(2,1)S(1)}, u32[]{:S(2)}, u32[]{:S(2)}) collective-permute-start(bf16[512,512]{1,0:T(8,128)(2,1)S(1)} %collective-permute-done.10.rest_2_), channel_id=1, source_target_pairs={{0,4},{4,0},{8,12},{12,8},{16,20},{20,16},{24,28},{28,24},{32,36},... | collective-permute-start | bytes 1572872 | tf_op jit(solution)/shard_map/ppermute | solution.py:43
  108.2 7.5 %copy-start.2 = (bf16[1024,1536]{1,0:T(8,128)(2,1)S(1)}, bf16[1024,1536]{1,0:T(8,128)(2,1)}, u32[]{:S(2)}) copy-start(bf16[1024,1536]{1,0:T(8,128)(2,1)} %get-tuple-element.48.rest_3_) | copy-start | bytes 9437188
